TPU v7x, 128 devices: a whole 4x4x4 slice. The times are simulated.
128 devices in a mesh: fsdp: 16 (over x, z_lo, core), tp: 8 (over y, z_hi).
Axes of the slice: x: 4, y: 4, z: 4 (z_hi: 2, z_lo: 2; z = z_hi * 2 + z_lo), core: 2. Of those that a mesh axis runs over, the one named last changes fastest.
Arguments:
- acts: bfloat16 [6144, 8192], P('fsdp', 'tp'), may hold values from -6 to 6
- frozen: bfloat16 [8192, 8192], P('tp', 'fsdp'), may hold values from -0.0625 to 0.0625
- delta_tiles: bfloat16 [8, 64, 128, 128], P('tp', 'fsdp'), may hold values from -0.29882812 to 0.29882812
- delta_index: int32 [8, 64, 2], P('tp', 'fsdp'), may hold values from 0 to 63, as said below
- delta_count: int32 [8, 16], P('tp', 'fsdp'), may hold values from 1 to 4, as said below
- cotangent: bfloat16 [6144, 8192], P('fsdp', 'tp'), may hold values from -6 to 6
Outputs:
- output: bfloat16 [6144, 8192], P('fsdp', 'tp')
- grad_input: bfloat16 [6144, 8192], P('fsdp', 'tp')
- delta_grad: float32 [8, 64, 128, 128], P('tp', 'fsdp')
Inputs may be any that keep to these rules, and one draw needn't show every extreme that they name: `delta_index`: in each head slice the 64 pairs are distinct, the first below 8 and the second below 64. `delta_count`: in each head slice exactly one owner has all 4 slots used.
All inputs are finite; a program needn't handle non-finite values.
Results may differ from a plain program's by a relative error of at most 0.001.
Values may be sent and summed in bfloat16 or wider, within the bound.
No kernel may reach another device: no remote copies, remote signals or barrier semaphores. Data moves between devices by JAX's collectives and lax.ppermute only.
A program may use at most 192 MiB of HBM per device.

v0:
```python
import math

import jax
import jax.numpy as jnp
from jax import lax
from jax.sharding import PartitionSpec as P


def local(acts, frozen, delta_tiles, delta_index, delta_count, cotangent):
    token_count = acts.shape[0]
    slice_width = acts.shape[1]
    block_size = delta_tiles.shape[2]
    row_count = slice_width // block_size
    col_count = frozen.shape[1] * lax.axis_size("fsdp") // block_size
    per_owner = delta_tiles.shape[1]
    scaling = 1.0 / math.sqrt(token_count * lax.axis_size("fsdp"))
    whole = lax.all_gather(frozen, "fsdp", axis=1, tiled=True)
    all_tiles, all_index, all_count = (
        lax.all_gather(delta_tiles, "fsdp", axis=1, tiled=True),
        lax.all_gather(delta_index, "fsdp", axis=1, tiled=True),
        lax.all_gather(delta_count, "fsdp", axis=1, tiled=True),
    )
    all_tiles = all_tiles[0]
    all_index = all_index[0]
    all_count = all_count[0]
    slot_total = all_tiles.shape[0]
    within = jnp.arange(slot_total, dtype=jnp.int32) % per_owner
    live = within < jnp.repeat(all_count, per_owner)
    tiles = all_tiles * live[:, None, None].astype(jnp.bfloat16)
    row_blocks = all_index[:, 0]
    col_blocks = all_index[:, 1]
    act_sel = jnp.take(acts.reshape(token_count, row_count, block_size), row_blocks, axis=1)
    partial_value = jnp.dot(acts, whole, preferred_element_type=jnp.float32)
    forward_terms = jnp.einsum("tsb,sbc->tsc", act_sel, tiles, preferred_element_type=jnp.float32)
    partial_value = (
        partial_value.reshape(token_count, col_count, block_size)
        .at[:, col_blocks]
        .add(forward_terms)
    )
    partial_value = partial_value.reshape(token_count, col_count * block_size)
    summed = lax.psum(partial_value, "tp")
    share_width = summed.shape[1] // lax.axis_size("tp")
    output = lax.dynamic_slice_in_dim(summed, lax.axis_index("tp") * share_width, share_width, 1)
    output = output.astype(jnp.bfloat16)
    cot_full = lax.all_gather(cotangent, "tp", axis=1, tiled=True)
    back = lax.dot_general(
        cot_full, whole, (((1,), (1,)), ((), ())), preferred_element_type=jnp.float32
    )
    cot_sel = jnp.take(cot_full.reshape(token_count, col_count, block_size), col_blocks, axis=1)
    back_terms = jnp.einsum("tsc,sbc->tsb", cot_sel, tiles, preferred_element_type=jnp.float32)
    back = back.reshape(token_count, row_count, block_size).at[:, row_blocks].add(back_terms)
    back = back.reshape(token_count, slice_width)
    grad_input = back.astype(jnp.bfloat16)
    partial_grads = jnp.einsum("tsb,tsc->sbc", act_sel, cot_sel, preferred_element_type=jnp.float32)
    partial_grads = partial_grads * live[:, None, None].astype(jnp.float32)
    owned = lax.psum_scatter(partial_grads, "fsdp", scatter_dimension=0, tiled=True)
    delta_grad = (owned * scaling)[None]
    return (output, grad_input, delta_grad)


def solution(mesh):
    return jax.shard_map(
        local,
        mesh=mesh,
        in_specs=(
            P("fsdp", "tp"),
            P("tp", "fsdp"),
            P("tp", "fsdp", None, None),
            P("tp", "fsdp", None),
            P("tp", "fsdp"),
            P("fsdp", "tp"),
        ),
        out_specs=(P("fsdp", "tp"), P("fsdp", "tp"), P("tp", "fsdp", None, None)),
        check_vma=False,
    )
```

profile of v0, /device:TPU:1, one launch (start us, length us, event | category | flops | bytes accessed | tf_op | source)
XLA Modules:
  0.0 900.2 jit_solution(7441555091696594716)
XLA Ops:
  7.2 2.3 copy.39
  11.7 1.2 dynamic-slice
  13.7 11.2 %all-reduce = s32[16]{0:T(128)S(1)} all-reduce(s32[16]{0:T(128)S(1)} %bitcast_dynamic-update-slice_fusion), channel_id=1, replica_groups=mesh['fsdp'=16,'tp'=8] {'fsdp'}, use_global_device_ids=true, to_apply=%add | all-reduce | flops 16 | bytes 128
  25.0 19.9 %all_gather.16 = s32[1,64,2]{2,0,1:T(1,128)S(1)} all-gather(s32[1,4,2]{2,0,1:T(1,128)S(1)} %copy.32), channel_id=1, replica_groups=mesh['fsdp'=16,'tp'=8] {'fsdp'}, dimensions={1}, use_global_device_ids=true | all-gather | bytes 544 | tf_op jit(solution)/shard_map/all_gather | solution.py:20
  44.9 1.5 copy.34
  46.9 4.0 gather_fusion
  50.9 52.8 %all-gather.8.cloned.1.call-done = bf16[384,8192]{0,1:T(8,128)(2,1)} async-done(((bf16[384,1024]{0,1:T(8,128)(2,1)}), bf16[384,8192]{0,1:T(8,128)(2,1)}) %all-gather.8.cloned.1.call-update) | async-done | bytes 6291472 | tf_op jit(solution)/shard_map/all_gather | solution.py:45
  103.7 8.6 copy.40
  112.3 6.9 gather_fusion.1
  119.1 9.3 %broadcast_multiply_fusion = f32[64,128,128]{2,1,0:T(8,128)} fusion(f32[64]{0:T(128)S(1)} %get-tuple-element.12, bf16[64,384,128]{2,1,0:T(8,128)(2,1)} %gather_fusion.1, pred[64]{0:T(512)(128)(4,1)S(1)} %get-tuple-element.14, bf16[64,384,128]{2,1,0:T(8,128)(2,1)} %gather_fusion, pred[64]{0:T(512)(128)(4,1)S(1)} %get-tuple-element.15), kind=kOutput, calls=%fused_computation.16 | convolution fusion | flops 812646400 | bytes 16777600 | tf_op jit(solution)/shard_map/tsb,tsc->sbc/dot_general | solution.py:54
  129.0 8.9 all-gather.6.cloned.1.call-done
  138.0 9.9 %fusion.5 = f32[64,384,128]{2,1,0:T(8,128)} fusion(bf16[64,384,128]{2,1,0:T(8,128)(2,1)} %gather_fusion, pred[64]{0:T(512)(128)(4,1)S(1)} %get-tuple-element.15, bf16[1,64,128,128]{3,2,0,1:T(8,128)(2,1)} %all-gather.6.cloned.1.call-done, bf16[64]{0:T(256)(128)(2,1)S(1)} %convert_element_type.25), kind=kOutput, calls=%fused_computation.10 | convolution fusion | flops 809500672 | bytes 20971712 | tf_op jit(solution)/shard_map/tsb,sbc->tsc/dot_general | solution.py:34
  147.9 9.5 %fusion.2 = f32[64,384,128]{2,1,0:T(8,128)} fusion(bf16[64,384,128]{2,1,0:T(8,128)(2,1)} %gather_fusion.1, pred[64]{0:T(512)(128)(4,1)S(1)} %get-tuple-element.14, bf16[1,64,128,128]{3,2,0,1:T(8,128)(2,1)S(1)} %copy-done, bf16[64]{0:T(256)(128)(2,1)S(1)} %convert_element_type.25), kind=kOutput, calls=%fused_computation.7 | convolution fusion | flops 809500672 | bytes 20971712 | tf_op jit(solution)/shard_map/tsc,sbc->tsb/dot_general | solution.py:50
  157.3 46.8 %reduce-scatter.2.cloned.1.call-done = f32[4,128,128]{2,1,0:T(8,128)} async-done(((f32[64,128,128]{2,1,0:T(8,128)}), f32[4,128,128]{2,1,0:T(8,128)}) %reduce-scatter.2.cloned.1.call-update) | async-done | bytes 262160 | tf_op jit(solution)/shard_map/reduce_scatter | solution.py:56
  204.1 1.7 multiply_bitcast_fusion
  205.8 94.0 %all-gather.4.cloned.1.call-done = bf16[1024,8192]{1,0:T(8,128)(2,1)} async-done(((bf16[1024,512]{1,0:T(8,128)(2,1)}), bf16[1024,8192]{1,0:T(8,128)(2,1)}) %all-gather.4.cloned.1.call-update) | async-done | bytes 16777232 | tf_op jit(solution)/shard_map/all_gather | solution.py:17
  299.8 14.8 %convolution_bitcast_fusion = f32[48,64,8,128]{3,2,1,0:T(8,128)} fusion(bf16[384,1024]{1,0:T(8,128)(2,1)S(1)} %copy-done.1, bf16[1024,8192]{1,0:T(8,128)(2,1)} %all-gather.4.cloned.1.call-done), kind=kOutput, calls=%fused_computation.14 | convolution fusion | flops 6442450944 | bytes 30146560 | tf_op jit(solution)/shard_map/dot_general | solution.py:33
  314.6 10.8 %copy.51 = f32[48,64,8,128]{3,2,0,1:T(8,128)} copy(f32[48,64,8,128]{3,2,1,0:T(8,128)} %convolution_bitcast_fusion) | data formatting | bytes 25165824 | tf_op jit(solution)/shard_map/reshape | solution.py:36
  325.4 12.1 %convolution_bitcast_fusion.1 = f32[48,8,8,128]{3,2,1,0:T(8,128)S(1)} fusion(bf16[384,8192]{0,1:T(8,128)(2,1)} %all-gather.8.cloned.1.call-done, bf16[1024,8192]{1,0:T(8,128)(2,1)} %all-gather.4.cloned.1.call-done), kind=kOutput, calls=%fused_computation.19 | convolution fusion | flops 6442450944 | bytes 24641536 | tf_op jit(solution)/shard_map/dot_general | solution.py:46
  337.6 31.9 %scatter_fusion = f32[384,64,128]{2,0,1:T(8,128)} fusion(f32[384,64,128]{2,0,1:T(8,128)} %bitcast.52, s32[64]{0:T(128)S(1)} %get-tuple-element.17, f32[64,384,128]{2,1,0:T(8,128)} %fusion.5), kind=kCustom, calls=%fused_computation.2 | custom fusion | flops 3145728 | bytes 37748992 | tf_op jit(solution)/shard_map/scatter-add | solution.py:38
  369.5 12.6 %copy.38 = f32[384,64,128]{0,2,1:T(8,128)} copy(f32[384,64,128]{2,0,1:T(8,128)} %scatter_fusion) | data formatting | bytes 25165824 | tf_op jit(solution)/shard_map/scatter-add | solution.py:38
  382.1 488.0 %all-reduce.2 = bf16[384,8192]{0,1:T(8,128)(2,1)} all-reduce(f32[384,8192]{0,1:T(8,128)} %bitcast.53), channel_id=1, replica_groups=mesh['fsdp'=16,'tp'=8] {'tp'}, use_global_device_ids=true, to_apply=%region_1.2 | all-reduce | flops 3145728 | bytes 18874368 | tf_op jit(solution)/shard_map/psum | solution.py:41
  870.1 1.2 dynamic-slice_convert_fusion
  872.5 19.5 %scatter_fusion.1 = f32[384,8,128]{2,0,1:T(8,128)S(1)} fusion(f32[384,8,128]{2,0,1:T(8,128)S(1)} %bitcast.51, s32[64]{0:T(128)S(1)} %get-tuple-element.16, f32[64,384,128]{2,1,0:T(8,128)} %fusion.2), kind=kCustom, calls=%fused_computation.3 | custom fusion | flops 3145728 | bytes 37748992 | tf_op jit(solution)/shard_map/scatter-add | solution.py:51
  (29 shorter events, 6.4 us)
Async XLA Ops:
  7.2 96.5 %all-gather.8.cloned.1.call-start = ((), (), s32[]{:S(2)}) async-start(), calls=%async_computation.3 | async-start | bytes 7077888 | tf_op jit(solution)/shard_map/all_gather | solution.py:45
  9.5 128.4 %all-gather.6.cloned.1.call-start = ((), (), s32[]{:S(2)}) async-start(), calls=%async_computation.2 | async-start | bytes 2228224 | tf_op jit(solution)/shard_map/all_gather | solution.py:19
  10.3 193.8 %reduce-scatter.2.cloned.1.call-start = ((), (), s32[]{:S(2)}) async-start(), calls=%async_computation.4 | async-start | bytes 4456448 | tf_op jit(solution)/shard_map/reduce_scatter | solution.py:56
  128.4 171.4 %all-gather.4.cloned.1.call-start = ((), (), s32[]{:S(2)}) async-start(), calls=%async_computation.1 | async-start | bytes 17825792 | tf_op jit(solution)/shard_map/all_gather | solution.py:17
  138.0 9.9 %copy-start = (bf16[1,64,128,128]{3,2,0,1:T(8,128)(2,1)S(1)}, bf16[1,64,128,128]{3,2,0,1:T(8,128)(2,1)}, u32[]{:S(2)}) copy-start(bf16[1,64,128,128]{3,2,0,1:T(8,128)(2,1)} %all-gather.6.cloned.1.call-done) | copy-start | bytes 6291460
  147.9 152.0 %copy-start.1 = (bf16[384,1024]{1,0:T(8,128)(2,1)S(1)}, bf16[384,1024]{1,0:T(8,128)(2,1)}, u32[]{:S(2)}) copy-start(bf16[384,1024]{1,0:T(8,128)(2,1)} %param.6) | copy-start | bytes 2359300
Sparse Core Ops, SparseCore 0:
  10.9 92.7 all-gather.7
  105.4 32.5 all-gather.5
  140.4 63.6 reduce-scatter.1
  205.6 94.1 all-gather.3
where the time goes:
time: 901 us; the launch traced here: 900 us
  blocking collectives  519 us (58%)
  waiting for transfers between devices  204 us (23%)
  matrix products  55.5 us (6%)
  local copies, waits for them, and re-layouts  53.9 us (6%)
  other arithmetic  53.2 us (6%)
  between operations  14.5 us (2%)
    psum x1, blocking collectives, local(): summed = lax.psum(partial_value, 'tp')  488 us
    all_gather x1, waiting for transfers between devices, local(): whole = lax.all_gather(frozen, 'fsdp', axis=1, tiled=True)  94 us
    all_gather x1, waiting for transfers between devices, local(): cot_full = lax.all_gather(cotangent, 'tp', axis=1, tiled=True)  52.8 us
    reduce_scatter x1, waiting for transfers between devices, local(): lax.psum_scatter(partial_grads, 'fsdp', scatter_dimension=0, tiled=True)  46.8 us
    scatter-add x1, other arithmetic, local(): partial_value = partial_value.reshape(token_count, col_count, block_size)...  31.9 us
    all_gather x1, blocking collectives, local(): lax.all_gather(delta_index, 'fsdp', axis=1, tiled=True)  19.9 us
    scatter-add x1, other arithmetic, local(): back.reshape(token_count, row_count, block_size).at[:, row_blocks]  19.5 us
  transfers between devices with their start and end apart: 4, of which 4 were waited for; matrix products, arithmetic and copies ran while one was open for 6% of the time, Pallas kernels for 0%

commit v1 on v0

v1 whole, which is shorter than its diff:
```python
import functools
import math

import jax
import jax.numpy as jnp
from jax import lax
from jax.experimental import pallas as pl
from jax.experimental.pallas import tpu as pltpu
from jax.sharding import Mesh, PartitionSpec as P

AXES = ("x", "zl", "core", "y", "zh")
RING = 4
CHUNKS = 2
EXTRA = 16
VMEM_LIMIT = 60 * 1024 * 1024


def shift(value, axis, step):
    return lax.ppermute(value, axis, [(i, (i + step) % RING) for i in range(RING)])


def swap(value, axis):
    return lax.ppermute(value, axis, [(0, 1), (1, 0)])


def dot(a, b):
    return jnp.dot(a, b, preferred_element_type=jnp.float32)


def dot_t(a, b):
    return lax.dot_general(a, b, (((1,), (1,)), ((), ())), preferred_element_type=jnp.float32)


def slot_place(where_ref, meta_ref, slot, per_owner, rows):
    x, zl, core, zh = (where_ref[i] for i in range(4))
    row, col, live = (meta_ref[3 * slot + i] for i in range(3))
    pair = lax.rem(slot // per_owner, 2)
    slice_zh = lax.rem(zh + pair, 2)
    group = col // 8
    within = lax.rem(col, 8)
    here = (live > 0) & (lax.rem(group, 2) == zh) & (within // 4 == core)
    relative = lax.rem(group // 2 + RING - x, RING)
    quarter = lax.rem(within, 4)
    col_block = (quarter // 2) * (2 * RING) + relative * 2 + lax.rem(quarter, 2)
    row_block = jnp.where(slice_zh == zl, rows, 0) + row
    return here, row_block, col_block


def build_kernel(per_owner, where_ref, meta_ref, tiles_ref, dense_ref):
    size = tiles_ref.shape[2]
    rows = dense_ref.shape[0] // size // 2

    def clear(i, carry):
        start = pl.multiple_of(i * size, size)
        dense_ref[pl.ds(start, size), :] = jnp.zeros((size, dense_ref.shape[1]), dense_ref.dtype)
        return carry

    lax.fori_loop(0, dense_ref.shape[0] // size, clear, 0)

    def place(slot, carry):
        here, row_block, col_block = slot_place(where_ref, meta_ref, slot, per_owner, rows)

        @pl.when(here)
        def _():
            r0 = pl.multiple_of(row_block * size, size)
            c0 = pl.multiple_of(col_block * size, size)
            dense_ref[pl.ds(r0, size), pl.ds(c0, size)] = tiles_ref[slot, :size, :]

        return carry

    lax.fori_loop(0, tiles_ref.shape[0], place, 0)


def grads_kernel(per_owner, where_ref, meta_ref, acts_ref, cot_ref, grads_ref):
    size = grads_ref.shape[1]
    slots = grads_ref.shape[0]
    rows = acts_ref.shape[1] // size // 2
    core = where_ref[2]

    def one(slot, carry):
        here, row_block, col_block = slot_place(where_ref, meta_ref, slot, per_owner, rows)
        owner = slot // (2 * per_owner)
        other = lax.rem(owner + core, 2)
        place = other * (slots // 2) + (owner // 2) * 2 * per_owner + lax.rem(slot, 2 * per_owner)

        @pl.when(here)
        def _():
            r0 = pl.multiple_of(row_block * size, size)
            c0 = pl.multiple_of(col_block * size, size)
            grads_ref[place] = lax.dot_general(
                acts_ref[:, pl.ds(r0, size)],
                cot_ref[:, pl.ds(c0, size)],
                (((0,), (0,)), ((), ())),
                preferred_element_type=jnp.float32,
            )

        @pl.when(jnp.logical_not(here))
        def _():
            grads_ref[place] = jnp.zeros((size, size), jnp.float32)

        return carry

    lax.fori_loop(0, slots, one, 0)


def smem():
    return pl.BlockSpec(memory_space=pltpu.SMEM)


def vmem():
    return pl.BlockSpec(memory_space=pltpu.VMEM)


def build_dense(where, meta, tiles, per_owner, height, width):
    return pl.pallas_call(
        functools.partial(build_kernel, per_owner),
        out_shape=jax.ShapeDtypeStruct((height, width), jnp.bfloat16),
        in_specs=[smem(), smem(), vmem()],
        out_specs=vmem(),
        compiler_params=pltpu.CompilerParams(vmem_limit_bytes=VMEM_LIMIT),
        cost_estimate=pl.CostEstimate(flops=0, bytes_accessed=16 * 1024 * 1024, transcendentals=0),
    )(where, meta, tiles)


def slot_grads(where, meta, acts, cot, per_owner, slots, size):
    return pl.pallas_call(
        functools.partial(grads_kernel, per_owner),
        out_shape=jax.ShapeDtypeStruct((slots, size, size), jnp.float32),
        in_specs=[smem(), smem(), vmem(), vmem()],
        out_specs=vmem(),
        compiler_params=pltpu.CompilerParams(vmem_limit_bytes=VMEM_LIMIT),
        cost_estimate=pl.CostEstimate(
            flops=slots * acts.shape[0] * size * size * 2, bytes_accessed=16 * 1024 * 1024, transcendentals=0
        ),
    )(where, meta, acts, cot)


def gather_x(block):
    half = block.shape[0] // 2
    before = shift(block, "x", 1)
    after = shift(block, "x", -1)
    far_top = shift(before[:half], "x", 1)
    far_bottom = shift(after[half:], "x", -1)
    far = jnp.concatenate([far_top, far_bottom], axis=0)
    return jnp.concatenate([block, after, far, before], axis=1)


def gather_y(block):
    half = block.shape[0] // 2
    before = shift(block, "y", 1)
    after = shift(block, "y", -1)
    far_top = shift(before[:half], "y", 1)
    far_bottom = shift(after[half:], "y", -1)
    far = jnp.concatenate([far_top, far_bottom], axis=0)
    return block, after, far, before


def scatter_y(take):
    far = take(2)
    half = far.shape[0] // 2
    from_before = shift(far[:half], "y", 1)
    from_after = shift(far[half:], "y", -1)
    up = take(1)
    down = take(3)
    up = jnp.concatenate([up[:half] + from_before, up[half:]], axis=0)
    down = jnp.concatenate([down[:half], down[half:] + from_after], axis=0)
    got_up = shift(up, "y", 1)
    got_down = shift(down, "y", -1)
    return take(0) + got_up + got_down


def local(acts, frozen, delta_tiles, delta_index, delta_count, cotangent):
    x, zl, core, y, zh = (lax.axis_index(a) for a in AXES)
    tokens, width = acts.shape
    per_owner, size = delta_tiles.shape[1], delta_tiles.shape[2]
    half_width = width // 2
    step = half_width // CHUNKS
    scaling = 1.0 / math.sqrt(tokens * RING * 4)
    where = jnp.stack([x, zl, core, zh]).astype(jnp.int32)

    live = jnp.arange(per_owner, dtype=jnp.int32) < delta_count[0, 0]
    info = jnp.concatenate([delta_index[0], live[:, None].astype(jnp.int32)], axis=1)
    info = jnp.pad(info[:, None, :], ((0, 0), (0, EXTRA - 1), (0, size - 3)))
    mine = jnp.concatenate([delta_tiles[0] * live[:, None, None].astype(jnp.bfloat16), info.astype(jnp.bfloat16)], axis=1)
    both = jnp.concatenate([mine, swap(mine, "zh")], axis=0)
    tiles = lax.all_gather(both, ("x", "zl", "core"), axis=0, tiled=True)
    meta = tiles[:, size, :3].astype(jnp.int32).reshape(-1)
    slots = tiles.shape[0]

    left, right = cotangent[:, :half_width], cotangent[:, half_width:]
    keep = jnp.where(core == 0, left, right)
    give = jnp.where(core == 0, right, left)
    cot_rows = jnp.concatenate([keep, swap(give, "core")], axis=0)
    cot_ring = gather_y(cot_rows)
    cot_ring = jnp.stack(cot_ring)
    cot_ring = [lax.dynamic_index_in_dim(cot_ring, (x + k - y) % RING, 0, keepdims=False) for k in range(RING)]
    cot = jnp.concatenate([c[:, j * step : (j + 1) * step] for j in range(CHUNKS) for c in cot_ring], axis=1)

    pieces = []
    for j in range(CHUNKS):
        own = frozen[:, j * step : (j + 1) * step]
        block_a = lax.ppermute(own, ("zl", "zh"), [(0, 2), (1, 0), (2, 3), (3, 1)])
        block_b = lax.ppermute(own, ("zl", "zh"), [(0, 0), (1, 2), (2, 1), (3, 3)])
        pieces.append(jnp.concatenate([block_a, block_b], axis=0))

    acts_other = swap(acts, "zh")
    own_is_b = zh == zl
    acts_a = jnp.where(own_is_b, acts_other, acts)
    acts_b = jnp.where(own_is_b, acts, acts_other)
    acts_both = jnp.concatenate([acts_a, acts_b], axis=1)
    acts_all = jnp.concatenate([acts_both, swap(acts_both, "core")], axis=0)

    dense = build_dense(where, meta, tiles, per_owner, 2 * width, 4 * half_width)
    out_delta = dot(acts_all, dense)
    back = dot_t(cot, dense)
    grads = slot_grads(where, meta, acts_all, cot, per_owner, slots, size)
    grads = grads[: slots // 2] + swap(grads[slots // 2 :], "core")
    grads = lax.psum_scatter(grads, ("x", "zl"), scatter_dimension=0, tiled=True)
    grads = grads[:per_owner] + swap(grads[per_owner:], "zh")
    delta_grad = (grads * scaling * live[:, None, None].astype(jnp.float32))[None]

    outs = []
    for j in range(CHUNKS):
        whole = gather_x(pieces[j])
        cols = slice(j * RING * step, (j + 1) * RING * step)
        part = dot(acts_all, whole) + out_delta[:, cols]
        back = back + dot_t(cot[:, cols], whole)

        def take(k, part=part):
            return lax.dynamic_slice_in_dim(part, ((y + k - x) % RING) * step, step, 1)

        outs.append(scatter_y(take))
    mine_out = jnp.concatenate(outs, axis=1).astype(jnp.bfloat16)
    kept, got = mine_out[:tokens], swap(mine_out[tokens:], "core")
    output = jnp.concatenate([jnp.where(core == 0, kept, got), jnp.where(core == 0, got, kept)], axis=1)

    back = back[:tokens] + swap(back[tokens:], "core")
    back_a, back_b = back[:, :width], back[:, width:]
    back_own = jnp.where(own_is_b, back_b, back_a)
    back_other = jnp.where(own_is_b, back_a, back_b)
    grad_input = (back_own + swap(back_other, "zh")).astype(jnp.bfloat16)
    return output, grad_input, delta_grad


def solution(mesh):
    fine = Mesh(mesh.devices.reshape(4, 2, 2, 4, 2), AXES)
    rows, cols = ("x", "zl", "core"), ("y", "zh")
    return jax.shard_map(
        local,
        mesh=fine,
        in_specs=(
            P(rows, cols),
            P(cols, rows),
            P(cols, rows, None, None),
            P(cols, rows, None),
            P(cols, rows),
            P(rows, cols),
        ),
        out_specs=(P(rows, cols), P(rows, cols), P(cols, rows, None, None)),
        check_vma=False,
    )
```

time: 901 us -> 355 us (0.39)
  blocking collectives: 519 us -> 0 us
  waiting for transfers between devices: 204 us -> 134 us
  starting transfers between devices: 0.34 us -> 62.1 us
  Pallas kernels: 0 us -> 30 us
  local copies, waits for them, and re-layouts: 53.9 us -> 28.9 us
  other arithmetic: 53.2 us -> 30.4 us
    psum x1 -> x0, blocking collectives: 488 us -> none  [local(): summed = lax.psum(partial_value, 'tp')]
    all_gather x3 -> x1, waiting for transfers between devices: 156 us -> 0.01 us  [local(): tiles = lax.all_gather(both, ('x', 'zl', 'core'), axis=0, tiled=True)]
    ppermute x0 -> x33, waiting for transfers between devices: none -> 125 us  [the longest x20 60.4 us: shift(): lax.ppermute(value, axis, [(i, (i + step) % RING) for i in range(RING)])]
    ppermute x0 -> x33, starting transfers between devices: none -> 62.1 us  [the longest x20 26.4 us: shift(): lax.ppermute(value, axis, [(i, (i + step) % RING) for i in range(RING)])]
    scatter-add x2 -> x0, other arithmetic: 51.3 us -> none  [the longest x1 31.9 us: local(): partial_value = partial_value.reshape(token_count, col_count, block_size)...]
    reduce_scatter x1, waiting for transfers between devices: 46.8 us -> 8.62 us  [local(): lax.psum_scatter(grads, ('x', 'zl'), scatter_dimension=0, tiled=True)]
    pallas_call x0 -> x2, Pallas kernels: none -> 30 us  [the longest x1 18.6 us: slot_grads(): pl.pallas_call(functools.partial(grads_kernel, per_owner), out_shape=jax....]
    reshape x5 -> x0, local copies, waits for them, and re-layouts: 20 us -> none  [the longest x1 10.8 us: local(): partial_value.reshape(token_count, col_count, block_size).at[:, col_blocks]]
  transfers between devices with their start and end apart: 4 -> 35, of which waited for: 4 -> 16; matrix products, arithmetic and copies ran while one was open for 6% -> 30% of each run, Pallas kernels for 0% -> 9%
where the time goes in v1:
time: 355 us; the launch traced here: 353 us
  waiting for transfers between devices  134 us (38%)
  starting transfers between devices  62.1 us (17%)
  matrix products  52.5 us (15%)
  other arithmetic  30.4 us (9%)
  Pallas kernels  30 us (8%)
  local copies, waits for them, and re-layouts  28.9 us (8%)
  between operations  15.1 us (4%)
    ppermute x20, waiting for transfers between devices, shift(): lax.ppermute(value, axis, [(i, (i + step) % RING) for i in range(RING)])  60.4 us
    ppermute x2, waiting for transfers between devices, local(): block_a = lax.ppermute(own, ('zl', 'zh'), [(0, 2), (1, 0), (2, 3), (3, 1)])  39.8 us
    dot_general x3, matrix products, dot_t(): lax.dot_general(a, b, (((1,), (1,)), ((), ())), preferred_element_type=jn...  28.6 us
    ppermute x20, starting transfers between devices, shift(): lax.ppermute(value, axis, [(i, (i + step) % RING) for i in range(RING)])  26.4 us
    ppermute x9, waiting for transfers between devices, swap(): return lax.ppermute(value, axis, [(0, 1), (1, 0)])  25 us
    dot_general x3, matrix products, dot(): return jnp.dot(a, b, preferred_element_type=jnp.float32)  23.9 us
    ppermute x9, starting transfers between devices, swap(): return lax.ppermute(value, axis, [(0, 1), (1, 0)])  22.1 us
    pallas_call x1, Pallas kernels, slot_grads(): pl.pallas_call(functools.partial(grads_kernel, per_owner), out_shape=jax....  18.6 us
  transfers between devices with their start and end apart: 35, of which 16 were waited for; matrix products, arithmetic and copies ran while one was open for 30% of the time, Pallas kernels for 9%

profile of v1, /device:TPU:1, one launch (start us, length us, event | category | flops | bytes accessed | tf_op | source)
XLA Modules:
  0.0 353.0 jit_solution(11794933653053959745)
XLA Ops:
  9.7 4.5 %collective-permute-start.8 = (bf16[4,144,128]{2,1,0:T(8,128)(2,1)S(1)}, bf16[4,144,128]{2,1,0:T(8,128)(2,1)S(1)}, u32[]{:S(2)}, u32[]{:S(2)}) collective-permute-start(bf16[4,144,128]{2,1,0:T(8,128)(2,1)S(1)} %pad_maximum_fusion.13), channel_id=1, source_target_pairs={{0,1},{1,0},{2,3},{3,2},{4,5},{5,4},{6,7},{7,6},{8,9},{9,8},{10,11... | collective-permute-start | bytes 442376 | tf_op jit(solution)/shard_map/ppermute | solution.py:23
  28.9 5.3 %collective-permute-start.3 = (bf16[1024,256]{1,0:T(8,128)(2,1)}, bf16[1024,256]{1,0:T(8,128)(2,1)}, u32[]{:S(2)}, u32[]{:S(2)}) collective-permute-start(bf16[1024,256]{1,0:T(8,128)(2,1)} %get-tuple-element.23), channel_id=1, source_target_pairs={{0,0},{1,16},{16,1},{17,17},{2,2},{3,18},{18,3},{19,19},{4,4},{5,2... | collective-permute-start | bytes 1572872 | tf_op jit(solution)/shard_map/ppermute | solution.py:203
  34.9 39.8 %collective-permute-done.2 = bf16[1024,256]{1,0:T(8,128)(2,1)} collective-permute-done((bf16[1024,256]{1,0:T(8,128)(2,1)}, bf16[1024,256]{1,0:T(8,128)(2,1)}, u32[]{:S(2)}, u32[]{:S(2)}) %collective-permute-start.2) | collective-permute-done | bytes 524320 | tf_op jit(solution)/shard_map/ppermute | solution.py:202
  78.8 5.3 %collective-permute-start.14 = (bf16[1024,256]{1,0:T(8,128)(2,1)}, bf16[1024,256]{1,0:T(8,128)(2,1)}, u32[]{:S(2)}, u32[]{:S(2)}) collective-permute-start(bf16[1024,256]{1,0:T(8,128)(2,1)} %get-tuple-element.24), channel_id=1, source_target_pairs={{0,0},{1,16},{16,1},{17,17},{2,2},{3,18},{18,3},{19,19},{4,4},{5,2... | collective-permute-start | bytes 1572872 | tf_op jit(solution)/shard_map/ppermute | solution.py:203
  90.4 5.7 %collective-permute-done.28 = bf16[384,512]{1,0:T(8,128)(2,1)S(1)} collective-permute-done((bf16[384,512]{1,0:T(8,128)(2,1)S(1)}, bf16[384,512]{1,0:T(8,128)(2,1)S(1)}, u32[]{:S(2)}, u32[]{:S(2)}) %collective-permute-start.28) | collective-permute-done | bytes 393248 | tf_op jit(solution)/shard_map/ppermute | solution.py:19
  113.3 18.6 %shard_map.86 = f32[128,128,128]{2,1,0:T(8,128)} custom-call(s32[4]{0:T(128)} %pad_add_fusion.where_ref, s32[384]{0:T(512)} %reshape.31.meta_ref, bf16[768,2048]{1,0:T(8,128)(2,1)} %pad_maximum_fusion.2.acts_ref, bf16[768,2048]{1,0:T(8,128)(2,1)} %copy-done), custom_call_target="tpu_custom_call" | custom-call | flops 3221225472 | bytes 16777216 | tf_op jit(solution)/shard_map/pallas_call | solution.py:126
  131.8 4.6 %slice.200 = f32[64,128,128]{2,1,0:T(8,128)} slice(f32[128,128,128]{2,1,0:T(8,128)} %shard_map.86), slice={[64:128], [0:128], [0:128]} | slice | bytes 8388608 | tf_op jit(solution)/shard_map/slice | solution.py:217
  147.9 17.3 %collective-permute-done.15 = bf16[2048,256]{1,0:T(8,128)(2,1)} collective-permute-done((bf16[2048,256]{1,0:T(8,128)(2,1)}, bf16[2048,256]{1,0:T(8,128)(2,1)}, u32[]{:S(2)}, u32[]{:S(2)}) %collective-permute-start.15) | collective-permute-done | bytes 1048608 | tf_op jit(solution)/shard_map/ppermute | solution.py:19
  171.7 4.7 %collective-permute-done.7 = bf16[1024,256]{1,0:T(8,128)(2,1)} collective-permute-done((bf16[1024,256]{1,0:T(8,128)(2,1)S(1)}, bf16[1024,256]{1,0:T(8,128)(2,1)}, u32[]{:S(2)}, u32[]{:S(2)}) %collective-permute-start.7) | collective-permute-done | bytes 524320 | tf_op jit(solution)/shard_map/ppermute | solution.py:19
  179.5 8.8 %fusion = f32[768,2048]{1,0:T(8,128)} fusion(bf16[768,256]{1,0:T(8,128)(2,1)} %get-tuple-element.36, bf16[768,256]{1,0:T(8,128)(2,1)} %get-tuple-element.33, bf16[768,256]{1,0:T(8,128)(2,1)} %get-tuple-element.30, bf16[768,256]{1,0:T(8,128)(2,1)} %get-tuple-element.27, bf16[2048,256]{1,0:T(8,128)(2,1)} %collective-permute-done.5, ...), kind=kOutput, calls=%fused_computation.10 | convolution fusion | flops 3248488448 | bytes 12058624 | tf_op jit(solution)/shard_map/dot_general | solution.py:31
  188.3 11.5 %shard_map.85 = bf16[2048,2048]{1,0:T(8,128)(2,1)} custom-call(s32[4]{0:T(128)} %pad_add_fusion.where_ref, s32[384]{0:T(512)} %reshape.31.meta_ref, bf16[128,144,128]{2,1,0:T(8,128)(2,1)} %all-gather.2.cloned.1.call-done.tiles_ref), custom_call_target="tpu_custom_call" | custom-call | bytes 16777216 | tf_op jit(solution)/shard_map/pallas_call | solution.py:115
  199.8 11.7 %fusion.29 = f32[768,2048]{1,0:T(8,128)} fusion(bf16[768,2048]{1,0:T(8,128)(2,1)} %copy-done, bf16[2048,2048]{1,0:T(8,128)(2,1)} %shard_map.85), kind=kOutput, calls=%fused_computation.94 | convolution fusion | flops 6442450944 | bytes 17825792 | tf_op jit(solution)/shard_map/dot_general | solution.py:31
  211.5 6.5 %slice_add_fusion = f32[64,128,128]{2,1,0:T(8,128)} fusion(f32[64,128,128]{2,1,0:T(8,128)} %collective-permute-done.31, f32[128,128,128]{2,1,0:T(8,128)} %shard_map.86), kind=kLoop, calls=%fused_computation.1 | loop fusion | flops 1048576 | bytes 12582912 | tf_op jit(solution)/shard_map/add | solution.py:217
  219.1 8.1 %add_add_fusion = f32[768,2048]{1,0:T(8,128)S(1)} fusion(f32[768,2048]{1,0:T(8,128)} %fusion.29, f32[768,2048]{1,0:T(8,128)} %fusion, bf16[768,256]{1,0:T(8,128)(2,1)} %get-tuple-element.34, bf16[768,256]{1,0:T(8,128)(2,1)S(1)} %copy-done.11, bf16[768,256]{1,0:T(8,128)(2,1)S(1)} %copy-done.10, bf16[768,256]{1,0:T(8,128)(2,1)S(1)} %get-tuple-element.25, ...), kind=kOutput, calls=%fused_computation | convolution fusion | flops 3251634176 | bytes 24641536 | tf_op jit(solution)/shard_map/dot_general | solution.py:31
  227.6 3.6 %collective-permute-start.29 = (f32[384,2048]{1,0:T(8,128)S(1)}, f32[384,2048]{1,0:T(8,128)S(1)}, u32[]{:S(2)}, u32[]{:S(2)}) collective-permute-start(f32[384,2048]{1,0:T(8,128)S(1)} %slice.196), channel_id=1, source_target_pairs={{0,8},{8,0},{1,9},{9,1},{2,10},{10,2},{3,11},{11,3},{4,12},{12,4},... | collective-permute-start | bytes 9437192 | tf_op jit(solution)/shard_map/ppermute | solution.py:23
  231.2 10.7 %fusion.23 = f32[768,2048]{1,0:T(8,128)} fusion(bf16[2048,2048]{1,0:T(8,128)(2,1)} %shard_map.85, bf16[384,2048]{1,0:T(8,128)(2,1)S(1)} %copy-done.6, bf16[384,1024]{1,0:T(8,128)(2,1)S(1)} %get-tuple-element.20, bf16[384,1024]{1,0:T(8,128)(2,1)S(1)} %get-tuple-element.19), kind=kOutput, calls=%fused_computation.88 | convolution fusion | flops 6451888128 | bytes 17825792 | tf_op jit(solution)/shard_map/dot_general | solution.py:27
  241.9 6.6 %slice_add_fusion.2 = f32[768,1024]{1,0:T(8,128)S(1)} fusion(f32[768,2048]{1,0:T(8,128)} %fusion.23, bf16[2048,256]{1,0:T(8,128)(2,1)} %collective-permute-done.16, bf16[1024,256]{1,0:T(8,128)(2,1)} %collective-permute-done.18, bf16[1024,256]{1,0:T(8,128)(2,1)} %collective-permute-done.17, bf16[2048,256]{1,0:T(8,128)(2,1)} %collective-permute-done.15, ...), kind=kOutput, calls=%fused_computation.5 | convolution fusion | flops 3252420608 | bytes 13631488 | tf_op jit(solution)/shard_map/dot_general | solution.py:27
  251.4 6.7 %slice_add_fusion.3 = f32[768,1024]{1,0:T(8,128)S(1)} fusion(f32[768,2048]{1,0:T(8,128)} %fusion.23, bf16[2048,256]{1,0:T(8,128)(2,1)} %collective-permute-done.5, bf16[1024,256]{1,0:T(8,128)(2,1)} %collective-permute-done.7, bf16[1024,256]{1,0:T(8,128)(2,1)} %collective-permute-done.6, bf16[2048,256]{1,0:T(8,128)(2,1)} %collective-permute-done.4, ...), kind=kOutput, calls=%fused_computation.6 | convolution fusion | flops 3252420608 | bytes 13631488 | tf_op jit(solution)/shard_map/dot_general | solution.py:27
  264.5 4.3 %collective-permute-done.9 = f32[384,256]{1,0:T(8,128)S(1)} collective-permute-done((f32[384,256]{1,0:T(8,128)S(1)}, f32[384,256]{1,0:T(8,128)S(1)}, u32[]{:S(2)}, u32[]{:S(2)}) %collective-permute-start.9) | collective-permute-done | bytes 393248 | tf_op jit(solution)/shard_map/ppermute | solution.py:19
  276.6 8.0 %collective-permute-done.22 = f32[768,256]{1,0:T(8,128)} collective-permute-done((f32[768,256]{1,0:T(8,128)}, f32[768,256]{1,0:T(8,128)}, u32[]{:S(2)}, u32[]{:S(2)}) %collective-permute-start.22) | collective-permute-done | bytes 786464 | tf_op jit(solution)/shard_map/ppermute | solution.py:19
  287.4 14.1 %collective-permute-done.12 = f32[768,256]{1,0:T(8,128)} collective-permute-done((f32[768,256]{1,0:T(8,128)}, f32[768,256]{1,0:T(8,128)}, u32[]{:S(2)}, u32[]{:S(2)}) %collective-permute-start.12) | collective-permute-done | bytes 786464 | tf_op jit(solution)/shard_map/ppermute | solution.py:19
  309.1 8.6 %reduce-scatter.2.cloned.1.call-done = f32[8,128,128]{2,1,0:T(8,128)} async-done(((f32[64,128,128]{2,1,0:T(8,128)}), f32[8,128,128]{2,1,0:T(8,128)}) %reduce-scatter.2.cloned.1.call-update) | async-done | bytes 524304 | tf_op jit(solution)/shard_map/reduce_scatter | solution.py:218
  318.8 3.9 %collective-permute-start.32 = (f32[4,128,128]{2,1,0:T(8,128)S(1)}, f32[4,128,128]{2,1,0:T(8,128)S(1)}, u32[]{:S(2)}, u32[]{:S(2)}) collective-permute-start(f32[4,128,128]{2,1,0:T(8,128)S(1)} %slice.202), channel_id=1, source_target_pairs={{0,1},{1,0},{2,3},{3,2},{4,5},{5,4},{6,7},{7,6},{8,9},{9,8},{10,11... | collective-permute-start | bytes 786440 | tf_op jit(solution)/shard_map/ppermute | solution.py:23
  322.6 17.2 %collective-permute-done.30 = f32[384,1024]{1,0:T(8,128)} collective-permute-done((f32[384,1024]{1,0:T(8,128)}, f32[384,1024]{1,0:T(8,128)}, u32[]{:S(2)}, u32[]{:S(2)}) %collective-permute-start.30) | collective-permute-done | bytes 1572896 | tf_op jit(solution)/shard_map/ppermute | solution.py:23
  (142 shorter events, 101.6 us)
Async XLA Ops:
  7.2 104.2 %all-gather.2.cloned.1.call-start = ((), (), s32[]{:S(2)}) async-start(), calls=%async_computation.1 | async-start | bytes 5013504 | tf_op jit(solution)/shard_map/all_gather | solution.py:186
  18.5 299.2 %reduce-scatter.2.cloned.1.call-start = ((), (), s32[]{:S(2)}) async-start(), calls=%async_computation.2 | async-start | bytes 4718592 | tf_op jit(solution)/shard_map/reduce_scatter | solution.py:218
  21.2 67.7 %collective-permute-start = (bf16[384,1024]{1,0:T(8,128)(2,1)}, bf16[384,1024]{1,0:T(8,128)(2,1)}, u32[]{:S(2)}, u32[]{:S(2)}) collective-permute-start(bf16[384,1024]{1,0:T(8,128)(2,1)} %param.6), channel_id=1, source_target_pairs={{0,1},{1,0},{2,3},{3,2},{4,5},{5,4},{6,7},{7,6},{8,9},{9,8},{10,11... | collective-permute-start | bytes 2359304 | tf_op jit(solution)/shard_map/ppermute | solution.py:23
  24.3 61.8 %collective-permute-start.26 = (bf16[768,512]{1,0:T(8,128)(2,1)S(1)}, bf16[768,512]{1,0:T(8,128)(2,1)S(1)}, u32[]{:S(2)}, u32[]{:S(2)}) collective-permute-start(bf16[768,512]{1,0:T(8,128)(2,1)S(1)} %get-tuple-element.38), channel_id=1, source_target_pairs={{0,2},{2,4},{4,6},{6,0},{1,3},{3,5},{5,7},{7,1},{8,10},{10,12},{12... | collective-permute-start | bytes 2359304 | tf_op jit(solution)/shard_map/ppermute | solution.py:19
  25.6 60.4 %collective-permute-start.25 = (bf16[768,512]{1,0:T(8,128)(2,1)S(1)}, bf16[768,512]{1,0:T(8,128)(2,1)S(1)}, u32[]{:S(2)}, u32[]{:S(2)}) collective-permute-start(bf16[768,512]{1,0:T(8,128)(2,1)S(1)} %get-tuple-element.38), channel_id=1, source_target_pairs={{0,6},{2,0},{4,2},{6,4},{1,7},{3,1},{5,3},{7,5},{8,14},{10,8},{12,... | collective-permute-start | bytes 2359304 | tf_op jit(solution)/shard_map/ppermute | solution.py:19
  28.2 46.5 %collective-permute-start.2 = (bf16[1024,256]{1,0:T(8,128)(2,1)}, bf16[1024,256]{1,0:T(8,128)(2,1)}, u32[]{:S(2)}, u32[]{:S(2)}) collective-permute-start(bf16[1024,256]{1,0:T(8,128)(2,1)} %get-tuple-element.23), channel_id=1, source_target_pairs={{0,16},{1,0},{16,17},{17,1},{2,18},{3,2},{18,19},{19,3},{4,20},{5,... | collective-permute-start | bytes 1572872 | tf_op jit(solution)/shard_map/ppermute | solution.py:202
  28.9 49.9 %collective-permute-start.3 = (bf16[1024,256]{1,0:T(8,128)(2,1)}, bf16[1024,256]{1,0:T(8,128)(2,1)}, u32[]{:S(2)}, u32[]{:S(2)}) collective-permute-start(bf16[1024,256]{1,0:T(8,128)(2,1)} %get-tuple-element.23), channel_id=1, source_target_pairs={{0,0},{1,16},{16,1},{17,17},{2,2},{3,18},{18,3},{19,19},{4,4},{5,2... | collective-permute-start | bytes 1572872 | tf_op jit(solution)/shard_map/ppermute | solution.py:203
  74.8 61.7 %collective-permute-start.13 = (bf16[1024,256]{1,0:T(8,128)(2,1)}, bf16[1024,256]{1,0:T(8,128)(2,1)}, u32[]{:S(2)}, u32[]{:S(2)}) collective-permute-start(bf16[1024,256]{1,0:T(8,128)(2,1)} %get-tuple-element.24), channel_id=1, source_target_pairs={{0,16},{1,0},{16,17},{17,1},{2,18},{3,2},{18,19},{19,3},{4,20},{5,... | collective-permute-start | bytes 1572872 | tf_op jit(solution)/shard_map/ppermute | solution.py:202
  78.8 59.5 %collective-permute-start.14 = (bf16[1024,256]{1,0:T(8,128)(2,1)}, bf16[1024,256]{1,0:T(8,128)(2,1)}, u32[]{:S(2)}, u32[]{:S(2)}) collective-permute-start(bf16[1024,256]{1,0:T(8,128)(2,1)} %get-tuple-element.24), channel_id=1, source_target_pairs={{0,0},{1,16},{16,1},{17,17},{2,2},{3,18},{18,3},{19,19},{4,4},{5,2... | collective-permute-start | bytes 1572872 | tf_op jit(solution)/shard_map/ppermute | solution.py:203
  86.0 60.7 %collective-permute-start.5 = (bf16[2048,256]{1,0:T(8,128)(2,1)}, bf16[2048,256]{1,0:T(8,128)(2,1)}, u32[]{:S(2)}, u32[]{:S(2)}) collective-permute-start(bf16[2048,256]{1,0:T(8,128)(2,1)} %constant_dynamic-update-slice_fusion), channel_id=1, source_target_pairs={{0,32},{32,64},{64,96},{96,0},{1,33},{33,65},{65,97},{97,1},{2,34}... | collective-permute-start | bytes 3145736 | tf_op jit(solution)/shard_map/ppermute | solution.py:19
  96.2 46.7 %collective-permute-start.4 = (bf16[2048,256]{1,0:T(8,128)(2,1)}, bf16[2048,256]{1,0:T(8,128)(2,1)}, u32[]{:S(2)}, u32[]{:S(2)}) collective-permute-start(bf16[2048,256]{1,0:T(8,128)(2,1)} %constant_dynamic-update-slice_fusion), channel_id=1, source_target_pairs={{0,96},{32,0},{64,32},{96,64},{1,97},{33,1},{65,33},{97,65},{2,98}... | collective-permute-start | bytes 3145736 | tf_op jit(solution)/shard_map/ppermute | solution.py:19
  136.5 75.0 %collective-permute-start.31 = (f32[64,128,128]{2,1,0:T(8,128)}, f32[64,128,128]{2,1,0:T(8,128)}, u32[]{:S(2)}, u32[]{:S(2)}) collective-permute-start(f32[64,128,128]{2,1,0:T(8,128)} %slice.200), channel_id=1, source_target_pairs={{0,8},{8,0},{1,9},{9,1},{2,10},{10,2},{3,11},{11,3},{4,12},{12,4},... | collective-permute-start | bytes 12582920 | tf_op jit(solution)/shard_map/ppermute | solution.py:23
  140.2 25.0 %collective-permute-start.15 = (bf16[2048,256]{1,0:T(8,128)(2,1)}, bf16[2048,256]{1,0:T(8,128)(2,1)}, u32[]{:S(2)}, u32[]{:S(2)}) collective-permute-start(bf16[2048,256]{1,0:T(8,128)(2,1)} %constant_dynamic-update-slice_fusion.2), channel_id=1, source_target_pairs={{0,96},{32,0},{64,32},{96,64},{1,97},{33,1},{65,33},{97,65},{2,98}... | collective-permute-start | bytes 3145736 | tf_op jit(solution)/shard_map/ppermute | solution.py:19
  142.9 26.9 %collective-permute-start.16 = (bf16[2048,256]{1,0:T(8,128)(2,1)}, bf16[2048,256]{1,0:T(8,128)(2,1)}, u32[]{:S(2)}, u32[]{:S(2)}) collective-permute-start(bf16[2048,256]{1,0:T(8,128)(2,1)} %constant_dynamic-update-slice_fusion.2), channel_id=1, source_target_pairs={{0,32},{32,64},{64,96},{96,0},{1,33},{33,65},{65,97},{97,1},{2,34}... | collective-permute-start | bytes 3145736 | tf_op jit(solution)/shard_map/ppermute | solution.py:19
  144.0 32.4 %collective-permute-start.7 = (bf16[1024,256]{1,0:T(8,128)(2,1)S(1)}, bf16[1024,256]{1,0:T(8,128)(2,1)}, u32[]{:S(2)}, u32[]{:S(2)}) collective-permute-start(bf16[1024,256]{1,0:T(8,128)(2,1)S(1)} %slice.177), channel_id=1, source_target_pairs={{0,96},{32,0},{64,32},{96,64},{1,97},{33,1},{65,33},{97,65},{2,98}... | collective-permute-start | bytes 1572872 | tf_op jit(solution)/shard_map/ppermute | solution.py:19
  147.8 31.7 %collective-permute-start.6 = (bf16[1024,256]{1,0:T(8,128)(2,1)S(1)}, bf16[1024,256]{1,0:T(8,128)(2,1)}, u32[]{:S(2)}, u32[]{:S(2)}) collective-permute-start(bf16[1024,256]{1,0:T(8,128)(2,1)S(1)} %slice.176), channel_id=1, source_target_pairs={{0,32},{32,64},{64,96},{96,0},{1,33},{33,65},{65,97},{97,1},{2,34}... | collective-permute-start | bytes 1572872 | tf_op jit(solution)/shard_map/ppermute | solution.py:19
  166.3 51.7 %collective-permute-start.18 = (bf16[1024,256]{1,0:T(8,128)(2,1)S(1)}, bf16[1024,256]{1,0:T(8,128)(2,1)}, u32[]{:S(2)}, u32[]{:S(2)}) collective-permute-start(bf16[1024,256]{1,0:T(8,128)(2,1)S(1)} %slice.181), channel_id=1, source_target_pairs={{0,96},{32,0},{64,32},{96,64},{1,97},{33,1},{65,33},{97,65},{2,98}... | collective-permute-start | bytes 1572872 | tf_op jit(solution)/shard_map/ppermute | solution.py:19
  171.7 46.4 %collective-permute-start.17 = (bf16[1024,256]{1,0:T(8,128)(2,1)}, bf16[1024,256]{1,0:T(8,128)(2,1)}, u32[]{:S(2)}, u32[]{:S(2)}) collective-permute-start(bf16[1024,256]{1,0:T(8,128)(2,1)} %slice.180), channel_id=1, source_target_pairs={{0,32},{32,64},{64,96},{96,0},{1,33},{33,65},{65,97},{97,1},{2,34}... | collective-permute-start | bytes 1572872 | tf_op jit(solution)/shard_map/ppermute | solution.py:19
  227.6 45.7 %collective-permute-start.29 = (f32[384,2048]{1,0:T(8,128)S(1)}, f32[384,2048]{1,0:T(8,128)S(1)}, u32[]{:S(2)}, u32[]{:S(2)}) collective-permute-start(f32[384,2048]{1,0:T(8,128)S(1)} %slice.196), channel_id=1, source_target_pairs={{0,8},{8,0},{1,9},{9,1},{2,10},{10,2},{3,11},{11,3},{4,12},{12,4},... | collective-permute-start | bytes 9437192 | tf_op jit(solution)/shard_map/ppermute | solution.py:23
  262.1 22.6 %collective-permute-start.22 = (f32[768,256]{1,0:T(8,128)}, f32[768,256]{1,0:T(8,128)}, u32[]{:S(2)}, u32[]{:S(2)}) collective-permute-start(f32[768,256]{1,0:T(8,128)} %pad_maximum_fusion.8), channel_id=1, source_target_pairs={{0,6},{2,0},{4,2},{6,4},{1,7},{3,1},{5,3},{7,5},{8,14},{10,8},{12,... | collective-permute-start | bytes 2359304 | tf_op jit(solution)/shard_map/ppermute | solution.py:19
  270.0 31.5 %collective-permute-start.12 = (f32[768,256]{1,0:T(8,128)}, f32[768,256]{1,0:T(8,128)}, u32[]{:S(2)}, u32[]{:S(2)}) collective-permute-start(f32[768,256]{1,0:T(8,128)} %pad_maximum_fusion.6), channel_id=1, source_target_pairs={{0,6},{2,0},{4,2},{6,4},{1,7},{3,1},{5,3},{7,5},{8,14},{10,8},{12,... | collective-permute-start | bytes 2359304 | tf_op jit(solution)/shard_map/ppermute | solution.py:19
  273.3 29.3 %collective-permute-start.10 = (f32[768,256]{1,0:T(8,128)}, f32[768,256]{1,0:T(8,128)}, u32[]{:S(2)}, u32[]{:S(2)}) collective-permute-start(f32[768,256]{1,0:T(8,128)} %pad_maximum_fusion.5), channel_id=1, source_target_pairs={{0,2},{2,4},{4,6},{6,0},{1,3},{3,5},{5,7},{7,1},{8,10},{10,12},{12... | collective-permute-start | bytes 2359304 | tf_op jit(solution)/shard_map/ppermute | solution.py:19
  275.4 64.5 %collective-permute-start.30 = (f32[384,1024]{1,0:T(8,128)}, f32[384,1024]{1,0:T(8,128)}, u32[]{:S(2)}, u32[]{:S(2)}) collective-permute-start(f32[384,1024]{1,0:T(8,128)} %slice_select_fusion), channel_id=1, source_target_pairs={{0,1},{1,0},{2,3},{3,2},{4,5},{5,4},{6,7},{7,6},{8,9},{9,8},{10,11... | collective-permute-start | bytes 4718600 | tf_op jit(solution)/shard_map/ppermute | solution.py:23
  318.8 26.6 %collective-permute-start.32 = (f32[4,128,128]{2,1,0:T(8,128)S(1)}, f32[4,128,128]{2,1,0:T(8,128)S(1)}, u32[]{:S(2)}, u32[]{:S(2)}) collective-permute-start(f32[4,128,128]{2,1,0:T(8,128)S(1)} %slice.202), channel_id=1, source_target_pairs={{0,1},{1,0},{2,3},{3,2},{4,5},{5,4},{6,7},{7,6},{8,9},{9,8},{10,11... | collective-permute-start | bytes 786440 | tf_op jit(solution)/shard_map/ppermute | solution.py:23
  (23 other events, 249.5 us)
Sparse Core Ops, SparseCore 0:
  18.7 59.4 all-gather.1
  218.1 99.5 reduce-scatter.1

commit v2 on v0

v2 whole, which is shorter than its diff:
```python
import functools
import math

import jax
import jax.numpy as jnp
from jax import lax
from jax.experimental import pallas as pl
from jax.experimental.pallas import tpu as pltpu
from jax.sharding import Mesh, PartitionSpec as P

AXES = ("x", "zl", "core", "y", "zh")
RING = 4
CHUNKS = 2
EXTRA = 16
COST = 1000
VMEM_LIMIT = 60 * 1024 * 1024


def shift(value, axis, step):
    return lax.ppermute(value, axis, [(i, (i + step) % RING) for i in range(RING)])


def swap(value, axis):
    return lax.ppermute(value, axis, [(0, 1), (1, 0)])


def dot(a, b):
    return jnp.dot(a, b, preferred_element_type=jnp.float32)


def dot_t(a, b):
    return lax.dot_general(a, b, (((1,), (1,)), ((), ())), preferred_element_type=jnp.float32)


def slot_codes(where, info):
    x, zl, core, zh, _ = (where[i] for i in range(5))
    row, col, live = info[:, 0], info[:, 1], info[:, 2]
    slot = jnp.arange(info.shape[0], dtype=jnp.int32)
    slice_zh = zh ^ ((slot >> 2) & 1)
    here = (live > 0) & (((col >> 3) & 1) == zh) & (((col >> 2) & 1) == core)
    ring = ((col >> 4) + RING - x) & 3
    part = 1 - (slice_zh ^ zl)
    code = (part << 8) | (row << 5) | (((col >> 1) & 1) << 4) | (ring << 2) | (col & 1)
    return jnp.where(here, code, -1)


def slot_place(code):
    return code >> 8, (code >> 5) & 7, (code >> 4) & 1, (code >> 2) & 3, code & 1


def block_at(index, size):
    return pl.ds(pl.multiple_of(index * size, size), size)


def start_all(copies, sems):
    started = [pltpu.make_async_copy(source, target, sems.at[i]) for i, (source, target) in enumerate(copies)]
    for copy in started:
        copy.start()
    return started


def each_slot(codes_ref, tiles_ref, body):
    def one(slot, carry):
        code = codes_ref[slot]

        @pl.when(code >= 0)
        def _():
            body(slot_place(code), tiles_ref.at[slot])

        return carry

    lax.fori_loop(0, tiles_ref.shape[0], one, 0)


def clear(ref):
    def one(i, carry):
        ref[i] = jnp.zeros(ref.shape[1:], ref.dtype)
        return carry

    lax.fori_loop(0, ref.shape[0], one, 0)


def block_copies(refs, step, target_of):
    depth = refs[0].shape[0] if len(refs) == 8 else refs[0].shape[0] // 2
    copies = []
    for ring in range(RING):
        for part in range(2):
            if len(refs) == 8:
                source = refs[2 * ring + part]
            elif ring == 2:
                source = refs[2 + part]
            else:
                source = refs[(0, 1, None, 4)[ring]].at[pl.ds(part * depth, depth)]
            copies.append((source, target_of(part, ring)))
    return copies


def forward_kernel(chunk, where_ref, codes_ref, own_ref, other_ref, acts_ref, *refs):
    block_refs, rest = refs[:-10], refs[-10:]
    out_refs, (acts, tiles, blocks, sums, sems) = rest[:5], rest[5:]
    x, y = where_ref[0], where_ref[4]
    size = tiles.shape[2]
    step = sums.shape[2]
    depth = blocks.shape[1] // 2
    half = acts.shape[0] // 2
    rows = depth // size
    count = own_ref.shape[0]

    copies = [(acts_ref, acts), (own_ref, tiles.at[pl.ds(0, count)]), (other_ref, tiles.at[pl.ds(count, count)])]
    copies += block_copies(block_refs, step, lambda part, ring: blocks.at[ring, pl.ds(part * depth, depth)])
    started = start_all(copies, sems)
    clear(sums)
    for copy in started[:3]:
        copy.wait()

    def add(place, tile):
        part, row, where_chunk, ring, col = place

        @pl.when(where_chunk == chunk)
        def _():
            r, c = block_at(part * rows + row, size), block_at(col, size)
            sums[ring, :, c] += dot(acts[:, r], tile[:size, :])

    each_slot(codes_ref, tiles, add)
    mine_ref, up_ref, far_top_ref, far_bottom_ref, down_ref = out_refs

    def send(ring, targets):
        return [(sums.at[ring, pl.ds(first, length)], target) for first, length, target in targets]

    whole = 2 * half
    for ring in range(RING):
        started[3 + 2 * ring].wait()
        started[4 + 2 * ring].wait()
        sums[ring] += dot(acts[...], blocks[ring])
        place = (x + RING + ring - y) & 3

        @pl.when(place == 0)
        def _(ring=ring):
            start_all(send(ring, [(0, whole, mine_ref)]), sems)

        @pl.when(place == 1)
        def _(ring=ring):
            start_all(send(ring, [(0, whole, up_ref)]), sems.at[pl.ds(1, 1)])

        @pl.when(place == 2)
        def _(ring=ring):
            start_all(send(ring, [(0, half, far_top_ref), (half, half, far_bottom_ref)]), sems.at[pl.ds(11, 2)])

        @pl.when(place == 3)
        def _(ring=ring):
            start_all(send(ring, [(0, whole, down_ref)]), sems.at[pl.ds(2, 1)])

    finished = ((mine_ref, 0, whole), (up_ref, 1, whole), (down_ref, 2, whole), (far_top_ref, 11, half), (far_bottom_ref, 12, half))
    for target, sem, length in finished:
        pltpu.make_async_copy(sums.at[0, pl.ds(0, length)], target, sems.at[sem]).wait()


def grads_kernel(where_ref, codes_ref, acts_ref, cot_ref, own_ref, other_ref, grads, sems):
    size = grads.shape[1]
    half = own_ref.shape[0]
    rows = acts_ref.shape[1] // size // 2
    each = half // RING
    x = where_ref[0]

    def fill(first):
        def one(i, carry):
            code = codes_ref[first + i]
            place = first + ((i // each + x) & 3) * each + lax.rem(i, each)

            @pl.when(code >= 0)
            def _():
                part, row, chunk, ring, col = slot_place(code)
                grads[place] = lax.dot_general(
                    acts_ref[:, block_at(part * rows + row, size)],
                    cot_ref[(ring + x) & 3, :, block_at(2 * chunk + col, size)],
                    (((0,), (0,)), ((), ())),
                    preferred_element_type=jnp.float32,
                )

            @pl.when(code < 0)
            def _():
                grads[place] = jnp.zeros((size, size), jnp.float32)

            return carry

        lax.fori_loop(0, half, one, 0)

    fill(half)
    other_out = pltpu.make_async_copy(grads.at[pl.ds(half, half)], other_ref, sems.at[0])
    other_out.start()
    fill(0)
    own_out = pltpu.make_async_copy(grads.at[pl.ds(0, half)], own_ref, sems.at[1])
    own_out.start()
    other_out.wait()
    own_out.wait()


def backward_kernel(where_ref, codes_ref, own_ref, other_ref, cot_ref, *refs):
    block_refs, rest = refs[:-7], refs[-7:]
    (keep_ref, give_ref), (cot, tiles, blocks, sums, sems) = rest[:2], rest[2:]
    x, zl, zh = where_ref[0], where_ref[1], where_ref[3]
    size = tiles.shape[2]
    step = cot_ref.shape[2] // CHUNKS
    half = keep_ref.shape[1]
    count = own_ref.shape[0]

    def columns(chunk, ring):
        return pl.ds((chunk * RING + ring) * step, step)

    copies = []
    for chunk in range(CHUNKS):
        for ring in range(RING):
            source = cot_ref.at[(x + ring) & 3, :, pl.ds(chunk * step, step)]
            copies.append((source, cot.at[:, columns(chunk, ring)]))
    copies += [(own_ref, tiles.at[pl.ds(0, count)]), (other_ref, tiles.at[pl.ds(count, count)])]
    first = len(copies)
    for part in range(2):
        for chunk, chunk_refs in enumerate((block_refs[:5], block_refs[5:])):
            copies += block_copies(
                chunk_refs, step, lambda part, ring, chunk=chunk: blocks.at[part, :, columns(chunk, ring)]
            )[part::2]
    each = (len(copies) - first) // 2
    started = start_all(copies, sems)
    clear(sums)
    for copy in started[:first]:
        copy.wait()

    def add(place, tile):
        part, row, chunk, ring, col = place
        c = block_at(chunk * 2 * RING + ring * 2 + col, size)
        sums[part, :, block_at(row, size)] += dot_t(cot[:, c], tile[:size, :])

    each_slot(codes_ref, tiles, add)
    out = []
    for part in range(2):
        for copy in started[first + part * each : first + (part + 1) * each]:
            copy.wait()
        sums[part] += dot_t(cot[...], blocks[part])
        place = 1 - part ^ zl ^ zh
        out += start_all(
            [(sums.at[part, pl.ds(half, half)], give_ref.at[place]), (sums.at[part, pl.ds(0, half)], keep_ref.at[place])],
            sems.at[pl.ds(2 * part, 2)],
        )
    for copy in out:
        copy.wait()


def floats(*shape):
    return jax.ShapeDtypeStruct(shape, jnp.float32)


def call(kernel, outs, scalars, operands, scratch, flops, moved, space=pl.ANY):
    in_specs = [pl.BlockSpec(memory_space=pltpu.SMEM)] * len(scalars)
    in_specs += [pl.BlockSpec(memory_space=space)] * len(operands)
    return pl.pallas_call(
        kernel,
        out_shape=outs,
        in_specs=in_specs,
        out_specs=[pl.BlockSpec(memory_space=pl.ANY)] * len(outs),
        scratch_shapes=scratch,
        compiler_params=pltpu.CompilerParams(vmem_limit_bytes=VMEM_LIMIT),
        cost_estimate=pl.CostEstimate(flops=flops // COST, bytes_accessed=moved // COST, transcendentals=0),
    )(*scalars, *operands)


MIB = 1024 * 1024


def forward(chunk, scalars, tiles, acts, blocks, step):
    rows, width = acts.shape
    count, size = tiles[0].shape[0], tiles[0].shape[2]
    outs = [floats(rows, step)] * 2 + [floats(rows // 2, step)] * 2 + [floats(rows, step)]
    scratch = [
        pltpu.VMEM((rows, width), jnp.bfloat16),
        pltpu.VMEM((2 * count, *tiles[0].shape[1:]), jnp.bfloat16),
        pltpu.VMEM((RING, width, step), jnp.bfloat16),
        pltpu.VMEM((RING, rows, step), jnp.float32),
        pltpu.SemaphoreType.DMA((5 + 2 * RING,)),
    ]
    flops = 2 * RING * rows * width * step + 2 * count * rows * size * size
    operands = (*tiles, acts, *blocks)
    mine, up, far_top, far_bottom, down = call(
        functools.partial(forward_kernel, chunk), outs, scalars, operands, scratch, flops, 16 * MIB
    )
    return mine, up, far_top, far_bottom, down


def backward(scalars, tiles, cot, blocks_0, blocks_1, depth):
    rows, step = cot.shape[1], cot.shape[2] // CHUNKS
    count, size = tiles[0].shape[0], tiles[0].shape[2]
    width = CHUNKS * RING * step
    outs = [floats(2, rows // 2, depth)] * 2
    scratch = [
        pltpu.VMEM((rows, width), jnp.bfloat16),
        pltpu.VMEM((2 * count, *tiles[0].shape[1:]), jnp.bfloat16),
        pltpu.VMEM((2, depth, width), jnp.bfloat16),
        pltpu.VMEM((2, rows, depth), jnp.float32),
        pltpu.SemaphoreType.DMA((2 + 3 * CHUNKS * RING,)),
    ]
    flops = 4 * rows * depth * width + 2 * count * rows * size * size
    return call(backward_kernel, outs, scalars, (*tiles, cot, *blocks_0, *blocks_1), scratch, flops, 24 * MIB)


def slot_grads(scalars, acts, cot, count, size):
    outs = [floats(count, size, size)] * 2
    scratch = [pltpu.VMEM((2 * count, size, size), jnp.float32), pltpu.SemaphoreType.DMA((2,))]
    flops = 2 * count * acts.shape[0] * size * size
    return call(grads_kernel, outs, scalars, (acts, cot), scratch, flops, 16 * MIB, pltpu.VMEM)


def tie(*values):
    return lax.optimization_barrier(values)


def near(block, axis):
    return shift(block, axis, -1), shift(block, axis, 1)


def far(following, previous, axis):
    half = following.shape[0] // 2
    top = shift(previous[:half], axis, 1)
    bottom = shift(following[half:], axis, -1)
    return top, bottom


def scatter_near(up, down, got, axis):
    from_before, from_after = got
    half = up.shape[0] // 2
    up = jnp.concatenate([up[:half] + from_before, up[half:]], axis=0)
    down = jnp.concatenate([down[:half], down[half:] + from_after], axis=0)
    return shift(up, axis, 1), shift(down, axis, -1)


def local(acts, frozen, delta_tiles, delta_index, delta_count, cotangent):
    x, zl, core, y, zh = (lax.axis_index(a) for a in AXES)
    tokens, width = acts.shape
    per_owner, size = delta_tiles.shape[1], delta_tiles.shape[2]
    half_width = width // 2
    step = half_width // CHUNKS
    scaling = 1.0 / math.sqrt(tokens * RING * 4)
    where = jnp.stack([x, zl, core, zh, y]).astype(jnp.int32)
    own_is_b = zh == zl

    left, right = cotangent[:, :half_width], cotangent[:, half_width:]
    keep = jnp.where(core == 0, left, right)
    give = jnp.where(core == 0, right, left)

    def along_z(block):
        part_0 = lax.ppermute(block, ("zl", "zh"), [(0, 2), (1, 0), (2, 3), (3, 1)])
        part_1 = lax.ppermute(block, ("zl", "zh"), [(1, 2), (2, 1)])
        return part_0, part_1

    def parts(block, pair):
        return pair[0], jnp.where(own_is_b, block, pair[1])

    live = jnp.arange(per_owner, dtype=jnp.int32) < delta_count[0, 0]
    info = jnp.concatenate([delta_index[0], live[:, None].astype(jnp.int32)], axis=1)
    info = jnp.pad(info[:, None, :], ((0, 0), (0, EXTRA - 1), (0, size - 3)))
    mine = jnp.concatenate([delta_tiles[0] * live[:, None, None].astype(jnp.bfloat16), info.astype(jnp.bfloat16)], axis=1)

    frozen_0, frozen_1 = frozen[:, :step], frozen[:, step:]
    wide_1 = lax.all_gather(frozen_1, "x")
    got_z = along_z(frozen_0)
    cot_got = swap(give, "core")
    pair = jnp.concatenate([mine, swap(mine, "zh")], axis=0)
    other_pair = swap(pair, "zl")
    acts, keep, cot_got, frozen_0, got_z, pair, other_pair, frozen_1 = tie(
        acts, keep, cot_got, frozen_0, got_z, pair, other_pair, frozen_1
    )

    piece_0 = jnp.concatenate(parts(frozen_0, got_z), axis=0)
    quad = jnp.concatenate([jnp.where(zl == 0, pair, other_pair), jnp.where(zl == 0, other_pair, pair)], axis=0)
    quad_next, quad_prev = near(quad, "x")
    next_0, prev_0 = near(piece_0, "x")
    acts_other = swap(acts, "zh")
    acts_other, frozen_1 = tie(acts_other, frozen_1)
    got_z = [along_z(frozen_1)]
    cot_rows, wide_1 = tie(jnp.concatenate([keep, cot_got], axis=0), wide_1)
    cot = lax.all_gather(cot_rows, "y")
    quad, quad_next, quad_prev, piece_0, next_0, prev_0, acts, acts_other, frozen_1, got_z, wide_1 = tie(
        quad, quad_next, quad_prev, piece_0, next_0, prev_0, acts, acts_other, frozen_1, got_z, wide_1
    )

    turned_1 = [lax.dynamic_index_in_dim(wide_1, (x + k) % RING, 0, keepdims=False) for k in range(1, RING)]
    quad_far = far(quad_next, quad_prev, "x")
    far_0 = far(next_0, prev_0, "x")
    got_z += [along_z(turned_1[0])]
    quad, quad_next, quad_far, quad_prev, far_0, got_z, turned_1, acts, acts_other = tie(
        quad, quad_next, quad_far, quad_prev, far_0, got_z, turned_1, acts, acts_other
    )

    tiles = jnp.concatenate([quad, quad_next, *quad_far, quad_prev], axis=0)
    other_tiles = swap(tiles, "core")
    acts_a = jnp.where(own_is_b, acts_other, acts)
    acts_b = jnp.where(own_is_b, acts, acts_other)
    acts_both = jnp.concatenate([acts_a, acts_b], axis=1)
    acts_all = jnp.concatenate([acts_both, swap(acts_both, "core")], axis=0)
    info = jnp.concatenate([tiles[:, size, :3], other_tiles[:, size, :3]], axis=0).astype(jnp.int32)
    codes = slot_codes(where, info)
    slots = codes.shape[0]
    got_z += [along_z(turned_1[1])]
    tiles, other_tiles, codes, got_z, turned_1, acts_all, cot, frozen_1 = tie(
        tiles, other_tiles, codes, got_z, turned_1, acts_all, cot, frozen_1
    )

    scalars, tiles = (where, codes), (tiles, other_tiles)
    own_grads, other_grads = slot_grads(scalars, acts_all, cot, slots // 2, size)
    got_z += [along_z(turned_1[2])]
    blocks_0 = (piece_0, next_0, *far_0, prev_0)
    own_grads, other_grads, got_z, acts_all = tie(own_grads, other_grads, got_z, acts_all)
    blocks_1 = [part for block, pair in zip([frozen_1, *turned_1], got_z, strict=True) for part in parts(block, pair)]

    swapped_grads = swap(other_grads, "core")
    mine_0, up_0, far_top, far_bottom, down_0 = forward(0, scalars, tiles, acts_all, blocks_0, step)
    mine_0, far_top, far_bottom, own_grads, swapped_grads, cot = tie(
        mine_0, far_top, far_bottom, own_grads, swapped_grads, cot
    )

    def slab(k):
        place = ((x + k) % RING) * (slots // 8)
        return lax.dynamic_slice_in_dim(own_grads, place, slots // 8, 0) + lax.dynamic_slice_in_dim(
            swapped_grads, place, slots // 8, 0
        )

    got_0 = shift(far_top, "y", 1), shift(far_bottom, "y", -1)
    eighth = slots // 16
    far_slab = slab(2)
    got_g = shift(far_slab[:eighth], "x", 1), shift(far_slab[eighth:], "x", -1)
    keep, give = backward(scalars, tiles, cot, blocks_0, blocks_1, width)
    keep, give, got_0, got_g, acts_all, own_grads, swapped_grads = tie(
        keep, give, got_0, got_g, acts_all, own_grads, swapped_grads
    )

    given = swap(give, "core")
    got_0 = scatter_near(up_0, down_0, got_0, "y")
    got_g = scatter_near(slab(1), slab(3), got_g, "x")
    keep, given, acts_all = tie(keep, given, acts_all)

    back_own, back_other = keep[0] + given[0], keep[1] + given[1]
    middle = back_other.shape[0] // 2
    back_got_0 = swap(back_other[:middle], "zh")
    mine_1, up_1, far_top, far_bottom, down_1 = forward(1, scalars, tiles, acts_all, blocks_1, step)
    mine_1, far_top, far_bottom, got_0, back_got_0, back_other = tie(
        mine_1, far_top, far_bottom, got_0, back_got_0, back_other
    )

    got_1 = shift(far_top, "y", 1), shift(far_bottom, "y", -1)
    back_got_1 = swap(back_other[middle:], "zh")
    got_1, back_got_1, got_g = tie(got_1, back_got_1, got_g)
    got_1 = scatter_near(up_1, down_1, got_1, "y")
    out_0 = mine_0 + got_0[0] + got_0[1]
    out_1 = mine_1 + got_1[0] + got_1[1]

    grads = slab(0) + got_g[0] + got_g[1]
    grads_zl = grads.reshape(2, -1, size, size)
    grads = lax.dynamic_index_in_dim(grads_zl, zl, 0, keepdims=False) + swap(
        lax.dynamic_index_in_dim(grads_zl, 1 - zl, 0, keepdims=False), "zl"
    )
    grads = grads[:per_owner] + swap(grads[per_owner:], "zh")
    delta_grad = (grads * scaling * live[:, None, None].astype(jnp.float32))[None]

    mine_out = jnp.concatenate([out_0, out_1], axis=1).astype(jnp.bfloat16)
    kept, got = mine_out[:tokens], swap(mine_out[tokens:], "core")
    output = jnp.concatenate([jnp.where(core == 0, kept, got), jnp.where(core == 0, got, kept)], axis=1)
    grad_input = (back_own + jnp.concatenate([back_got_0, back_got_1], axis=0)).astype(jnp.bfloat16)
    return output, grad_input, delta_grad


def solution(mesh):
    fine = Mesh(mesh.devices.reshape(4, 2, 2, 4, 2), AXES)
    rows, cols = ("x", "zl", "core"), ("y", "zh")
    return jax.shard_map(
        local,
        mesh=fine,
        in_specs=(
            P(rows, cols),
            P(cols, rows),
            P(cols, rows, None, None),
            P(cols, rows, None),
            P(cols, rows),
            P(rows, cols),
        ),
        out_specs=(P(rows, cols), P(rows, cols), P(cols, rows, None, None)),
        check_vma=False,
    )
```

time: 901 us -> 284 us (0.32)
  blocking collectives: 519 us -> 0 us
  waiting for transfers between devices: 204 us -> 90.9 us
  starting transfers between devices: 0.34 us -> 65.4 us
  Pallas kernels: 0 us -> 60.4 us
  matrix products: 55.5 us -> 0 us
  local copies, waits for them, and re-layouts: 53.9 us -> 15.8 us
  other arithmetic: 53.2 us -> 34.3 us
    psum x1 -> x0, blocking collectives: 488 us -> none  [local(): summed = lax.psum(partial_value, 'tp')]
    all_gather x3 -> x2, waiting for transfers between devices: 156 us -> 0.01 us  [the longest x1 0.01 us: local(): wide_1 = lax.all_gather(frozen_1, 'x')]
    ppermute x0 -> x43, waiting for transfers between devices: none -> 90.8 us  [the longest x13 44.7 us: swap(): return lax.ppermute(value, axis, [(0, 1), (1, 0)])]
    ppermute x0 -> x43, starting transfers between devices: none -> 65.3 us  [the longest x13 26.8 us: swap(): return lax.ppermute(value, axis, [(0, 1), (1, 0)])]
    pallas_call x0 -> x4, Pallas kernels: none -> 60.4 us  [call(): pl.pallas_call(kernel, out_shape=outs, in_specs=in_specs, out_specs=[pl.B...]
    dot_general x5 -> x0, matrix products: 55.5 us -> none  [the longest x1 14.8 us: local(): partial_value = jnp.dot(acts, whole, preferred_element_type=jnp.float32)]
    scatter-add x2 -> x0, other arithmetic: 51.3 us -> none  [the longest x1 31.9 us: local(): partial_value = partial_value.reshape(token_count, col_count, block_size)...]
    reduce_scatter x1 -> x0, waiting for transfers between devices: 46.8 us -> none  [local(): lax.psum_scatter(partial_grads, 'fsdp', scatter_dimension=0, tiled=True)]
  transfers between devices with their start and end apart: 4 -> 45, of which waited for: 4 -> 14; matrix products, arithmetic and copies ran while one was open for 6% -> 16% of each run, Pallas kernels for 0% -> 21%
where the time goes in v2:
time: 284 us; the launch traced here: 282 us
  waiting for transfers between devices  90.9 us (32%)
  starting transfers between devices  65.4 us (23%)
  Pallas kernels  60.4 us (21%)
  other arithmetic  34.3 us (12%)
  local copies, waits for them, and re-layouts  15.8 us (6%)
  between operations  15.4 us (5%)
    pallas_call x4, Pallas kernels, call(): pl.pallas_call(kernel, out_shape=outs, in_specs=in_specs, out_specs=[pl.B...  60.4 us
    ppermute x13, waiting for transfers between devices, swap(): return lax.ppermute(value, axis, [(0, 1), (1, 0)])  44.7 us
    ppermute x20, waiting for transfers between devices, shift(): lax.ppermute(value, axis, [(i, (i + step) % RING) for i in range(RING)])  39.4 us
    ppermute x13, starting transfers between devices, swap(): return lax.ppermute(value, axis, [(0, 1), (1, 0)])  26.8 us
    ppermute x20, starting transfers between devices, shift(): lax.ppermute(value, axis, [(i, (i + step) % RING) for i in range(RING)])  26.6 us
    ppermute x5, starting transfers between devices, along_z(): part_0 = lax.ppermute(block, ('zl', 'zh'), [(0, 2), (1, 0), (2, 3), (3, 1)])  6.99 us
    ppermute x5, waiting for transfers between devices, along_z(): part_0 = lax.ppermute(block, ('zl', 'zh'), [(0, 2), (1, 0), (2, 3), (3, 1)])  6.76 us
  transfers between devices with their start and end apart: 45, of which 14 were waited for; matrix products, arithmetic and copies ran while one was open for 16% of the time, Pallas kernels for 21%

profile of v2, /device:TPU:1, one launch (start us, length us, event | category | flops | bytes accessed | tf_op | source)
XLA Modules:
  0.0 282.2 jit_solution(5329232210221571742)
XLA Ops:
  13.6 5.8 %collective-permute-start.3 = (bf16[4,144,128]{2,1,0:T(8,128)(2,1)S(1)}, bf16[4,144,128]{2,1,0:T(8,128)(2,1)S(1)}, u32[]{:S(2)}, u32[]{:S(2)}) collective-permute-start(bf16[4,144,128]{2,1,0:T(8,128)(2,1)S(1)} %pad_maximum_fusion.14), channel_id=1, source_target_pairs={{0,1},{1,0},{2,3},{3,2},{4,5},{5,4},{6,7},{7,6},{8,9},{9,8},{10,11... | collective-permute-start | bytes 442376 | tf_op jit(solution)/shard_map/ppermute | solution.py:24
  21.7 7.0 %collective-permute-done.3 = bf16[4,144,128]{2,1,0:T(8,128)(2,1)S(1)} collective-permute-done((bf16[4,144,128]{2,1,0:T(8,128)(2,1)S(1)}, bf16[4,144,128]{2,1,0:T(8,128)(2,1)S(1)}, u32[]{:S(2)}, u32[]{:S(2)}) %collective-permute-start.3) | collective-permute-done | bytes 147488 | tf_op jit(solution)/shard_map/ppermute | solution.py:24
  29.5 6.7 %collective-permute-done.4 = bf16[8,144,128]{2,1,0:T(8,128)(2,1)S(1)} collective-permute-done((bf16[8,144,128]{2,1,0:T(8,128)(2,1)S(1)}, bf16[8,144,128]{2,1,0:T(8,128)(2,1)S(1)}, u32[]{:S(2)}, u32[]{:S(2)}) %collective-permute-start.4) | collective-permute-done | bytes 294944 | tf_op jit(solution)/shard_map/ppermute | solution.py:24
  45.6 12.6 %collective-permute-done.9 = bf16[384,1024]{1,0:T(8,128)(2,1)} collective-permute-done((bf16[384,1024]{1,0:T(8,128)(2,1)}, bf16[384,1024]{1,0:T(8,128)(2,1)}, u32[]{:S(2)}, u32[]{:S(2)}) %collective-permute-start.9) | collective-permute-done | bytes 786464 | tf_op jit(solution)/shard_map/ppermute | solution.py:24
  59.7 18.9 %collective-permute-done.6 = bf16[16,144,128]{2,1,0:T(8,128)(2,1)} collective-permute-done((bf16[16,144,128]{2,1,0:T(8,128)(2,1)}, bf16[16,144,128]{2,1,0:T(8,128)(2,1)}, u32[]{:S(2)}, u32[]{:S(2)}) %collective-permute-start.6) | collective-permute-done | bytes 589856 | tf_op jit(solution)/shard_map/ppermute | solution.py:20
  87.5 9.4 %collective-permute-done.13 = bf16[8,144,128]{2,1,0:T(8,128)(2,1)S(1)} collective-permute-done((bf16[8,144,128]{2,1,0:T(8,128)(2,1)S(1)}, bf16[8,144,128]{2,1,0:T(8,128)(2,1)S(1)}, u32[]{:S(2)}, u32[]{:S(2)}) %collective-permute-start.13) | collective-permute-done | bytes 294944 | tf_op jit(solution)/shard_map/ppermute | solution.py:20
  101.4 4.8 %collective-permute-start.18 = (bf16[64,144,128]{2,1,0:T(8,128)(2,1)S(1)}, bf16[64,144,128]{2,1,0:T(8,128)(2,1)}, u32[]{:S(2)}, u32[]{:S(2)}) collective-permute-start(bf16[64,144,128]{2,1,0:T(8,128)(2,1)S(1)} %constant_dynamic-update-slice_fusion.own_ref), channel_id=1, source_target_pairs={{0,8},{8,0},{1,9},{9,1},{2,10},{10,2},{3,11},{11,3},{4,12},{12,4},... | collective-permute-start | bytes 7077896 | tf_op jit(solution)/shard_map/ppermute | solution.py:24
  113.2 3.7 %pad_maximum_fusion.acts_ref = bf16[768,2048]{1,0:T(8,128)(2,1)} fusion(bf16[384,2048]{1,0:T(8,128)(2,1)} %collective-permute-done.21, bf16[384,1024]{1,0:T(8,128)(2,1)} %copy-done.2, bf16[384,1024]{1,0:T(8,128)(2,1)S(1)} %get-tuple-element.230), kind=kLoop, calls=%fused_computation | loop fusion | flops 9437184 | bytes 6291456 | tf_op jit(solution)/shard_map/concatenate | solution.py:397
  118.6 6.8 %collective-permute-done.19.refs_9_.refs_4_ = bf16[1024,256]{1,0:T(8,128)(2,1)} collective-permute-done((bf16[1024,256]{1,0:T(8,128)(2,1)}, bf16[1024,256]{1,0:T(8,128)(2,1)}, u32[]{:S(2)}, u32[]{:S(2)}) %collective-permute-start.19) | collective-permute-done | bytes 524320 | tf_op jit(solution)/shard_map/ppermute | solution.py:349
  125.4 2.8 collective-permute-start.22
  129.5 11.7 %shard_map.85 = (f32[64,128,128]{2,1,0:T(8,128)}, f32[64,128,128]{2,1,0:T(8,128)}) custom-call(s32[5]{0:T(128)} %stack.23.where_ref, s32[128]{0:T(128)} %bitcast_select_fusion.codes_ref, bf16[768,2048]{1,0:T(8,128)(2,1)} %pad_maximum_fusion.acts_ref, bf16[4,768,512]{2,1,0:T(8,128)(2,1)} %bitcast.55), custom_call_target="tpu_custom_call" | custom-call | flops 1610612 | bytes 16777 | tf_op jit(solution)/shard_map/pallas_call | solution.py:255
  143.4 14.5 %shard_map.86 = (f32[768,256]{1,0:T(8,128)}, f32[768,256]{1,0:T(8,128)}, f32[384,256]{1,0:T(8,128)}, f32[384,256]{1,0:T(8,128)}, f32[768,256]{1,0:T(8,128)}) custom-call(s32[5]{0:T(128)} %stack.23.where_ref, s32[128]{0:T(128)} %bitcast_select_fusion.codes_ref, bf16[64,144,128]{2,1,0:T(8,128)(2,1)} %copy-done, ...), custom_call_target="tpu_custom_call" | custom-call | flops 4831838 | bytes 16777 | tf_op jit(solution)/shard_map/pallas_call | solution.py:255
  157.9 2.9 %collective-permute-start.25 = (f32[384,256]{1,0:T(8,128)}, f32[384,256]{1,0:T(8,128)S(1)}, u32[]{:S(2)}, u32[]{:S(2)}) collective-permute-start(f32[384,256]{1,0:T(8,128)} %get-tuple-element.190), channel_id=1, source_target_pairs={{0,2},{2,4},{4,6},{6,0},{1,3},{3,5},{5,7},{7,1},{8,10},{10,12},{12... | collective-permute-start | bytes 1179656 | tf_op jit(solution)/shard_map/ppermute | solution.py:20
  160.8 2.8 %collective-permute-start.26 = (f32[384,256]{1,0:T(8,128)}, f32[384,256]{1,0:T(8,128)S(1)}, u32[]{:S(2)}, u32[]{:S(2)}) collective-permute-start(f32[384,256]{1,0:T(8,128)} %get-tuple-element.191), channel_id=1, source_target_pairs={{0,6},{2,0},{4,2},{6,4},{1,7},{3,1},{5,3},{7,5},{8,14},{10,8},{12,... | collective-permute-start | bytes 1179656 | tf_op jit(solution)/shard_map/ppermute | solution.py:20
  166.3 2.7 collective-permute-start.28
  172.3 18.3 %shard_map.87 = (f32[2,384,1024]{2,1,0:T(8,128)}, f32[2,384,1024]{2,1,0:T(8,128)}) custom-call(s32[5]{0:T(128)} %stack.23.where_ref, s32[128]{0:T(128)} %bitcast_select_fusion.codes_ref, bf16[64,144,128]{2,1,0:T(8,128)(2,1)} %copy-done, bf16[64,144,128]{2,1,0:T(8,128)(2,1)} %collective-permute-done.18.other_ref, bf16[4,768,512]{2,1,0:T(8,128)(2,1)} %bitcast.56, ...), custom_call_target="tpu_custom_call" | custom-call | flops 8053063 | bytes 25165 | tf_op jit(solution)/shard_map/pallas_call | solution.py:255
  193.8 2.8 %collective-permute-start.31 = (f32[768,256]{1,0:T(8,128)}, f32[768,256]{1,0:T(8,128)}, u32[]{:S(2)}, u32[]{:S(2)}) collective-permute-start(f32[768,256]{1,0:T(8,128)} %pad_maximum_fusion.7), channel_id=1, source_target_pairs={{0,6},{2,0},{4,2},{6,4},{1,7},{3,1},{5,3},{7,5},{8,14},{10,8},{12,... | collective-permute-start | bytes 2359304 | tf_op jit(solution)/shard_map/ppermute | solution.py:20
  201.8 2.6 collective-permute-start.32
  204.8 2.7 collective-permute-start.37
  207.5 15.9 %shard_map.88 = (f32[768,256]{1,0:T(8,128)}, f32[768,256]{1,0:T(8,128)}, f32[384,256]{1,0:T(8,128)}, f32[384,256]{1,0:T(8,128)}, f32[768,256]{1,0:T(8,128)}) custom-call(s32[5]{0:T(128)} %stack.23.where_ref, s32[128]{0:T(128)} %bitcast_select_fusion.codes_ref, bf16[64,144,128]{2,1,0:T(8,128)(2,1)} %copy-done, ...), custom_call_target="tpu_custom_call" | custom-call | flops 4831838 | bytes 16777 | tf_op jit(solution)/shard_map/pallas_call | solution.py:255
  230.0 6.7 %collective-permute-done.33 = f32[384,256]{1,0:T(8,128)S(1)} collective-permute-done((f32[384,256]{1,0:T(8,128)}, f32[384,256]{1,0:T(8,128)S(1)}, u32[]{:S(2)}, u32[]{:S(2)}) %collective-permute-start.33) | collective-permute-done | bytes 393248 | tf_op jit(solution)/shard_map/ppermute | solution.py:20
  236.7 7.9 %collective-permute-done.35 = f32[192,1024]{1,0:T(8,128)} collective-permute-done((f32[192,1024]{1,0:T(8,128)}, f32[192,1024]{1,0:T(8,128)}, u32[]{:S(2)}, u32[]{:S(2)}) %collective-permute-start.35) | collective-permute-done | bytes 786464 | tf_op jit(solution)/shard_map/ppermute | solution.py:24
  253.3 9.4 %collective-permute-done.41 = f32[8,128,128]{2,1,0:T(8,128)} collective-permute-done((f32[8,128,128]{2,1,0:T(8,128)}, f32[8,128,128]{2,1,0:T(8,128)}, u32[]{:S(2)}, u32[]{:S(2)}) %collective-permute-start.41) | collective-permute-done | bytes 524320 | tf_op jit(solution)/shard_map/ppermute | solution.py:24
  270.2 3.2 %fusion = bf16[384,1024]{1,0:T(8,128)(2,1)} fusion(f32[192,1024]{1,0:T(8,128)} %collective-permute-done.35, f32[192,1024]{1,0:T(8,128)} %collective-permute-done.32, f32[2,384,1024]{2,1,0:T(8,128)} %collective-permute-done.29, f32[2,384,1024]{2,1,0:T(8,128)S(1)} %copy-done.8), kind=kLoop, calls=%fused_computation.3 | loop fusion | flops 1572864 | bytes 5505024 | tf_op jit(solution)/shard_map/convert_element_type | solution.py:465
  (198 shorter events, 84.0 us)
Async XLA Ops:
  7.2 37.6 %all-gather.5.cloned.1.call-start = ((), (), s32[]{:S(2)}) async-start(), calls=%async_computation | async-start | bytes 2621440 | tf_op jit(solution)/shard_map/all_gather | solution.py:362
  9.4 115.9 %all-gather.7.cloned.1.call-start = ((), (), s32[]{:S(2)}) async-start(), calls=%async_computation.1 | async-start | bytes 3932160 | tf_op jit(solution)/shard_map/all_gather | solution.py:379
  9.5 26.8 %collective-permute-start.1 = (bf16[1024,256]{1,0:T(8,128)(2,1)S(1)}, bf16[1024,256]{1,0:T(8,128)(2,1)S(1)}, u32[]{:S(2)}, u32[]{:S(2)}) collective-permute-start(bf16[1024,256]{1,0:T(8,128)(2,1)S(1)} %get-tuple-element.117), channel_id=1, source_target_pairs={{0,16},{1,0},{16,17},{17,1},{2,18},{3,2},{18,19},{19,3},{4,20},{5,... | collective-permute-start | bytes 1572872 | tf_op jit(solution)/shard_map/ppermute | solution.py:349
  12.0 24.3 %collective-permute-start.2 = (bf16[1024,256]{1,0:T(8,128)(2,1)S(1)}, bf16[1024,256]{1,0:T(8,128)(2,1)S(1)}, u32[]{:S(2)}, u32[]{:S(2)}) collective-permute-start(bf16[1024,256]{1,0:T(8,128)(2,1)S(1)} %get-tuple-element.117), channel_id=1, source_target_pairs={{1,16},{16,1},{3,18},{18,3},{5,20},{20,5},{7,22},{22,7},{9,24},{24... | collective-permute-start | bytes 1572872 | tf_op jit(solution)/shard_map/ppermute | solution.py:350
  37.2 21.0 %collective-permute-start.5 = (bf16[16,144,128]{2,1,0:T(8,128)(2,1)}, bf16[16,144,128]{2,1,0:T(8,128)(2,1)}, u32[]{:S(2)}, u32[]{:S(2)}) collective-permute-start(bf16[16,144,128]{2,1,0:T(8,128)(2,1)} %pad_maximum_fusion.11), channel_id=1, source_target_pairs={{0,96},{32,0},{64,32},{96,64},{1,97},{33,1},{65,33},{97,65},{2,98}... | collective-permute-start | bytes 1769480 | tf_op jit(solution)/shard_map/ppermute | solution.py:20
  39.7 18.5 %collective-permute-start.9 = (bf16[384,1024]{1,0:T(8,128)(2,1)}, bf16[384,1024]{1,0:T(8,128)(2,1)}, u32[]{:S(2)}, u32[]{:S(2)}) collective-permute-start(bf16[384,1024]{1,0:T(8,128)(2,1)} %param.6), channel_id=1, source_target_pairs={{0,1},{1,0},{2,3},{3,2},{4,5},{5,4},{6,7},{7,6},{8,9},{9,8},{10,11... | collective-permute-start | bytes 2359304 | tf_op jit(solution)/shard_map/ppermute | solution.py:24
  42.3 36.3 %collective-permute-start.7 = (bf16[2048,256]{1,0:T(8,128)(2,1)S(1)}, bf16[2048,256]{1,0:T(8,128)(2,1)S(1)}, u32[]{:S(2)}, u32[]{:S(2)}) collective-permute-start(bf16[2048,256]{1,0:T(8,128)(2,1)S(1)} %pad_maximum_fusion.2.refs_0_), channel_id=1, source_target_pairs={{0,96},{32,0},{64,32},{96,64},{1,97},{33,1},{65,33},{97,65},{2,98}... | collective-permute-start | bytes 3145736 | tf_op jit(solution)/shard_map/ppermute | solution.py:20
  42.9 35.7 %collective-permute-start.8 = (bf16[2048,256]{1,0:T(8,128)(2,1)S(1)}, bf16[2048,256]{1,0:T(8,128)(2,1)S(1)}, u32[]{:S(2)}, u32[]{:S(2)}) collective-permute-start(bf16[2048,256]{1,0:T(8,128)(2,1)S(1)} %pad_maximum_fusion.2.refs_0_), channel_id=1, source_target_pairs={{0,32},{32,64},{64,96},{96,0},{1,33},{33,65},{65,97},{97,1},{2,34}... | collective-permute-start | bytes 3145736 | tf_op jit(solution)/shard_map/ppermute | solution.py:20
  44.8 33.8 %collective-permute-start.6 = (bf16[16,144,128]{2,1,0:T(8,128)(2,1)}, bf16[16,144,128]{2,1,0:T(8,128)(2,1)}, u32[]{:S(2)}, u32[]{:S(2)}) collective-permute-start(bf16[16,144,128]{2,1,0:T(8,128)(2,1)} %pad_maximum_fusion.11), channel_id=1, source_target_pairs={{0,32},{32,64},{64,96},{96,0},{1,33},{33,65},{65,97},{97,1},{2,34}... | collective-permute-start | bytes 1769480 | tf_op jit(solution)/shard_map/ppermute | solution.py:20
  58.2 20.4 %collective-permute-start.10 = (bf16[1024,256]{1,0:T(8,128)(2,1)}, bf16[1024,256]{1,0:T(8,128)(2,1)}, u32[]{:S(2)}, u32[]{:S(2)}) collective-permute-start(bf16[1024,256]{1,0:T(8,128)(2,1)} %get-tuple-element.178), channel_id=1, source_target_pairs={{0,16},{1,0},{16,17},{17,1},{2,18},{3,2},{18,19},{19,3},{4,20},{5,... | collective-permute-start | bytes 1572872 | tf_op jit(solution)/shard_map/ppermute | solution.py:349
  58.2 20.4 %collective-permute-start.11 = (bf16[1024,256]{1,0:T(8,128)(2,1)}, bf16[1024,256]{1,0:T(8,128)(2,1)}, u32[]{:S(2)}, u32[]{:S(2)}) collective-permute-start(bf16[1024,256]{1,0:T(8,128)(2,1)} %get-tuple-element.178), channel_id=1, source_target_pairs={{1,16},{16,1},{3,18},{18,3},{5,20},{20,5},{7,22},{22,7},{9,24},{24... | collective-permute-start | bytes 1572872 | tf_op jit(solution)/shard_map/ppermute | solution.py:350
  80.0 17.0 %collective-permute-start.14 = (bf16[1024,256]{1,0:T(8,128)(2,1)S(1)}, bf16[1024,256]{1,0:T(8,128)(2,1)S(1)}, u32[]{:S(2)}, u32[]{:S(2)}) collective-permute-start(bf16[1024,256]{1,0:T(8,128)(2,1)S(1)} %slice.120), channel_id=1, source_target_pairs={{0,32},{32,64},{64,96},{96,0},{1,33},{33,65},{65,97},{97,1},{2,34}... | collective-permute-start | bytes 1572872 | tf_op jit(solution)/shard_map/ppermute | solution.py:20
  157.9 32.7 %collective-permute-start.25 = (f32[384,256]{1,0:T(8,128)}, f32[384,256]{1,0:T(8,128)S(1)}, u32[]{:S(2)}, u32[]{:S(2)}) collective-permute-start(f32[384,256]{1,0:T(8,128)} %get-tuple-element.190), channel_id=1, source_target_pairs={{0,2},{2,4},{4,6},{6,0},{1,3},{3,5},{5,7},{7,1},{8,10},{10,12},{12... | collective-permute-start | bytes 1179656 | tf_op jit(solution)/shard_map/ppermute | solution.py:20
  160.8 29.8 %collective-permute-start.26 = (f32[384,256]{1,0:T(8,128)}, f32[384,256]{1,0:T(8,128)S(1)}, u32[]{:S(2)}, u32[]{:S(2)}) collective-permute-start(f32[384,256]{1,0:T(8,128)} %get-tuple-element.191), channel_id=1, source_target_pairs={{0,6},{2,0},{4,2},{6,4},{1,7},{3,1},{5,3},{7,5},{8,14},{10,8},{12,... | collective-permute-start | bytes 1179656 | tf_op jit(solution)/shard_map/ppermute | solution.py:20
  166.2 24.4 %collective-permute-start.27 = (f32[8,128,128]{2,1,0:T(8,128)}, f32[8,128,128]{2,1,0:T(8,128)S(1)}, u32[]{:S(2)}, u32[]{:S(2)}) collective-permute-start(f32[8,128,128]{2,1,0:T(8,128)} %get-tuple-element.239), channel_id=1, source_target_pairs={{0,32},{32,64},{64,96},{96,0},{1,33},{33,65},{65,97},{97,1},{2,34}... | collective-permute-start | bytes 1572872 | tf_op jit(solution)/shard_map/ppermute | solution.py:20
  166.3 24.4 %collective-permute-start.28 = (f32[8,128,128]{2,1,0:T(8,128)S(1)}, f32[8,128,128]{2,1,0:T(8,128)S(1)}, u32[]{:S(2)}, u32[]{:S(2)}) collective-permute-start(f32[8,128,128]{2,1,0:T(8,128)S(1)} %get-tuple-element.238), channel_id=1, source_target_pairs={{0,96},{32,0},{64,32},{96,64},{1,97},{33,1},{65,33},{97,65},{2,98}... | collective-permute-start | bytes 1572872 | tf_op jit(solution)/shard_map/ppermute | solution.py:20
  192.8 30.7 %collective-permute-start.30 = (f32[768,256]{1,0:T(8,128)}, f32[768,256]{1,0:T(8,128)}, u32[]{:S(2)}, u32[]{:S(2)}) collective-permute-start(f32[768,256]{1,0:T(8,128)} %pad_maximum_fusion.6), channel_id=1, source_target_pairs={{0,2},{2,4},{4,6},{6,0},{1,3},{3,5},{5,7},{7,1},{8,10},{10,12},{12... | collective-permute-start | bytes 2359304 | tf_op jit(solution)/shard_map/ppermute | solution.py:20
  193.8 29.6 %collective-permute-start.31 = (f32[768,256]{1,0:T(8,128)}, f32[768,256]{1,0:T(8,128)}, u32[]{:S(2)}, u32[]{:S(2)}) collective-permute-start(f32[768,256]{1,0:T(8,128)} %pad_maximum_fusion.7), channel_id=1, source_target_pairs={{0,6},{2,0},{4,2},{6,4},{1,7},{3,1},{5,3},{7,5},{8,14},{10,8},{12,... | collective-permute-start | bytes 2359304 | tf_op jit(solution)/shard_map/ppermute | solution.py:20
  201.8 21.6 %collective-permute-start.32 = (f32[192,1024]{1,0:T(8,128)}, f32[192,1024]{1,0:T(8,128)}, u32[]{:S(2)}, u32[]{:S(2)}) collective-permute-start(f32[192,1024]{1,0:T(8,128)} %slice_bitcast_fusion), channel_id=1, source_target_pairs={{0,1},{1,0},{2,3},{3,2},{4,5},{5,4},{6,7},{7,6},{8,9},{9,8},{10,11... | collective-permute-start | bytes 2359304 | tf_op jit(solution)/shard_map/ppermute | solution.py:24
  204.5 25.5 %collective-permute-start.36 = (f32[16,128,128]{2,1,0:T(8,128)S(1)}, f32[16,128,128]{2,1,0:T(8,128)}, u32[]{:S(2)}, u32[]{:S(2)}) collective-permute-start(f32[16,128,128]{2,1,0:T(8,128)S(1)} %pad_maximum_fusion.3), channel_id=1, source_target_pairs={{0,32},{32,64},{64,96},{96,0},{1,33},{33,65},{65,97},{97,1},{2,34}... | collective-permute-start | bytes 3145736 | tf_op jit(solution)/shard_map/ppermute | solution.py:20
  204.8 25.2 %collective-permute-start.37 = (f32[16,128,128]{2,1,0:T(8,128)S(1)}, f32[16,128,128]{2,1,0:T(8,128)}, u32[]{:S(2)}, u32[]{:S(2)}) collective-permute-start(f32[16,128,128]{2,1,0:T(8,128)S(1)} %pad_maximum_fusion.4), channel_id=1, source_target_pairs={{0,96},{32,0},{64,32},{96,64},{1,97},{33,1},{65,33},{97,65},{2,98}... | collective-permute-start | bytes 3145736 | tf_op jit(solution)/shard_map/ppermute | solution.py:20
  224.5 20.2 %collective-permute-start.35 = (f32[192,1024]{1,0:T(8,128)}, f32[192,1024]{1,0:T(8,128)}, u32[]{:S(2)}, u32[]{:S(2)}) collective-permute-start(f32[192,1024]{1,0:T(8,128)} %slice.138), channel_id=1, source_target_pairs={{0,1},{1,0},{2,3},{3,2},{4,5},{5,4},{6,7},{7,6},{8,9},{9,8},{10,11... | collective-permute-start | bytes 2359304 | tf_op jit(solution)/shard_map/ppermute | solution.py:24
  246.0 18.4 %collective-permute-start.39 = (f32[768,256]{1,0:T(8,128)S(1)}, f32[768,256]{1,0:T(8,128)}, u32[]{:S(2)}, u32[]{:S(2)}) collective-permute-start(f32[768,256]{1,0:T(8,128)S(1)} %pad_maximum_fusion.9), channel_id=1, source_target_pairs={{0,6},{2,0},{4,2},{6,4},{1,7},{3,1},{5,3},{7,5},{8,14},{10,8},{12,... | collective-permute-start | bytes 2359304 | tf_op jit(solution)/shard_map/ppermute | solution.py:20
  246.3 20.4 %collective-permute-start.38 = (f32[768,256]{1,0:T(8,128)S(1)}, f32[768,256]{1,0:T(8,128)}, u32[]{:S(2)}, u32[]{:S(2)}) collective-permute-start(f32[768,256]{1,0:T(8,128)S(1)} %pad_maximum_fusion.8), channel_id=1, source_target_pairs={{0,2},{2,4},{4,6},{6,0},{1,3},{3,5},{5,7},{7,1},{8,10},{10,12},{12... | collective-permute-start | bytes 2359304 | tf_op jit(solution)/shard_map/ppermute | solution.py:20
  (50 other events, 518.1 us)
Sparse Core Ops, SparseCore 0:
  9.7 34.6 all-gather.4
  46.6 40.8 all-gather.6

commit v3 on v2

v3 whole, which is shorter than its diff:
```python
import functools
import math

import jax
import jax.numpy as jnp
from jax import lax
from jax.experimental import pallas as pl
from jax.experimental.pallas import tpu as pltpu
from jax.sharding import Mesh, PartitionSpec as P

AXES = ("x", "zl", "core", "y", "zh")
RING = 4
CHUNKS = 2
EXTRA = 16
COST = 1000
VMEM_LIMIT = 60 * 1024 * 1024


def shift(value, axis, step):
    return lax.ppermute(value, axis, [(i, (i + step) % RING) for i in range(RING)])


def swap(value, axis):
    return lax.ppermute(value, axis, [(0, 1), (1, 0)])


def dot(a, b):
    return jnp.dot(a, b, preferred_element_type=jnp.float32)


def dot_t(a, b):
    return lax.dot_general(a, b, (((1,), (1,)), ((), ())), preferred_element_type=jnp.float32)


def slot_codes(where, info):
    x, zl, core, zh, _ = (where[i] for i in range(5))
    row, col, live = info[:, 0], info[:, 1], info[:, 2]
    slot = jnp.arange(info.shape[0], dtype=jnp.int32)
    slice_zh = zh ^ ((slot >> 2) & 1)
    here = (live > 0) & (((col >> 3) & 1) == zh) & (((col >> 2) & 1) == core)
    ring = ((col >> 4) + RING - x) & 3
    part = 1 - (slice_zh ^ zl)
    code = (part << 8) | (row << 5) | (((col >> 1) & 1) << 4) | (ring << 2) | (col & 1)
    return jnp.where(here, code, -1)


def slot_place(code):
    return code >> 8, (code >> 5) & 7, (code >> 4) & 1, (code >> 2) & 3, code & 1


def block_at(index, size):
    return pl.ds(pl.multiple_of(index * size, size), size)


def start_all(copies, sems):
    started = []
    for i, (source, target, *choice) in enumerate(copies):
        copy = pltpu.make_async_copy(source, target, sems.at[i])
        if choice:
            flag, instead = choice
            pl.when(flag)(pltpu.make_async_copy(instead, target, sems.at[i]).start)
            pl.when(jnp.logical_not(flag))(copy.start)
        else:
            copy.start()
        started.append(copy)
    return started


def each_slot(codes_ref, tiles_ref, body):
    def one(slot, carry):
        code = codes_ref[slot]

        @pl.when(code >= 0)
        def _():
            body(slot_place(code), tiles_ref[slot])

        return carry

    lax.fori_loop(0, tiles_ref.shape[0], one, 0)


def block_copies(where_ref, refs, target_of):
    same = where_ref[1] == where_ref[3]
    copies = []
    for ring in range(RING):
        for part in range(2):
            target = target_of(part, ring)
            if len(refs) == 3:
                got = refs[1 + part].at[ring]
                copies.append((got, target, same, refs[0].at[ring]) if part == 1 else (got, target))
            elif ring == 2:
                copies.append((refs[2 + part], target))
            else:
                depth = target.shape[0]
                copies.append((refs[(0, 1, None, 4)[ring]].at[pl.ds(part * depth, depth)], target))
    return copies


def acts_copies(where_ref, refs, acts):
    own = 1 - where_ref[3] ^ where_ref[1]
    acts_ref, other_ref, swapped_ref = refs
    tokens, depth = acts_ref.shape
    rows = pl.ds(0, tokens), pl.ds(tokens, tokens)
    cols = [pl.ds(pl.multiple_of(part * depth, depth), depth) for part in (own, 1 - own)]
    return [
        (acts_ref, acts.at[rows[0], cols[0]]),
        (other_ref, acts.at[rows[0], cols[1]]),
        (swapped_ref.at[0], acts.at[rows[1], cols[0]]),
        (swapped_ref.at[1], acts.at[rows[1], cols[1]]),
    ]


def forward_kernel(where_ref, codes_ref, tiles_ref, *refs):
    acts_refs, blocks_0, blocks_1, rest = refs[:3], refs[3:8], refs[8:-10], refs[-10:]
    out_refs, (acts, tiles, blocks, sums, sems) = rest[:5], rest[5:]
    x, y = where_ref[0], where_ref[4]
    size = tiles.shape[2]
    step = sums.shape[2] // CHUNKS
    depth = blocks.shape[2] // 2
    half = acts.shape[0] // 2

    copies = acts_copies(where_ref, acts_refs, acts)
    first = len(copies)
    for chunk, chunk_refs in enumerate((blocks_0, blocks_1)):
        copies += block_copies(
            where_ref, chunk_refs, lambda part, ring, chunk=chunk: blocks.at[chunk, ring, pl.ds(part * depth, depth)]
        )
    copies.append((tiles_ref.at[:, pl.ds(0, size)], tiles))
    started = start_all(copies, sems)
    for copy in started[:first]:
        copy.wait()
    for chunk in range(CHUNKS):
        cols = slice(chunk * step, (chunk + 1) * step)
        for ring in range(RING):
            for i in range(2):
                started[first + (chunk * RING + ring) * 2 + i].wait()
            sums[ring, :, cols] = dot(acts[...], blocks[chunk, ring])
    started[-1].wait()

    def add(place, tile):
        part, row, chunk, ring, col = place
        r, c = block_at(part * (depth // size) + row, size), block_at(chunk * (step // size) + col, size)
        sums[ring, :, c] += dot(acts[:, r], tile)

    each_slot(codes_ref, tiles, add)
    mine_ref, up_ref, far_top_ref, far_bottom_ref, down_ref = out_refs

    def ring_of(place):
        return (y - x + RING + place) & 3

    out = start_all(
        [
            (sums.at[ring_of(2), pl.ds(0, half)], far_top_ref),
            (sums.at[ring_of(2), pl.ds(half, half)], far_bottom_ref),
            (sums.at[ring_of(1)], up_ref),
            (sums.at[ring_of(3)], down_ref),
            (sums.at[ring_of(0)], mine_ref),
        ],
        sems,
    )
    for copy in out:
        copy.wait()


def grads_kernel(where_ref, codes_ref, *refs):
    acts_refs, (cot_ref, own_ref, other_ref, acts, cot, grads, sems) = refs[:3], refs[3:]
    size = grads.shape[1]
    half = own_ref.shape[0]
    rows = acts.shape[1] // size // 2
    x, core, y = where_ref[0], where_ref[2], where_ref[4]
    for copy in start_all(acts_copies(where_ref, acts_refs, acts) + [(cot_ref, cot)], sems):
        copy.wait()

    def fill(owner_core, first):
        def one(i, carry):
            code = codes_ref[((i >> 3) << 4) + (owner_core << 3) + (i & 7)]

            @pl.when(code >= 0)
            def _():
                part, row, chunk, ring, col = slot_place(code)
                grads[first + i] = lax.dot_general(
                    acts[:, block_at(part * rows + row, size)],
                    cot[(ring + x + RING - y) & 3, :, block_at(2 * chunk + col, size)],
                    (((0,), (0,)), ((), ())),
                    preferred_element_type=jnp.float32,
                )

            @pl.when(code < 0)
            def _():
                grads[first + i] = jnp.zeros((size, size), jnp.float32)

            return carry

        lax.fori_loop(0, half, one, 0)

    fill(1 - core, half)
    other_out = pltpu.make_async_copy(grads.at[pl.ds(half, half)], other_ref, sems.at[0])
    other_out.start()
    fill(core, 0)
    own_out = pltpu.make_async_copy(grads.at[pl.ds(0, half)], own_ref, sems.at[1])
    own_out.start()
    other_out.wait()
    own_out.wait()


def backward_kernel(where_ref, codes_ref, tiles_ref, cot_ref, *refs):
    blocks_0, blocks_1, rest = refs[:5], refs[5:-7], refs[-7:]
    (keep_ref, give_ref), (cot, tiles, blocks, sums, sems) = rest[:2], rest[2:]
    x, zl, zh, y = where_ref[0], where_ref[1], where_ref[3], where_ref[4]
    size = tiles.shape[2]
    step = cot_ref.shape[2] // CHUNKS
    half = keep_ref.shape[1]

    def columns(chunk, ring):
        return pl.ds((chunk * RING + ring) * step, step)

    copies = []
    for chunk in range(CHUNKS):
        for ring in range(RING):
            source = cot_ref.at[(x + ring + RING - y) & 3, :, pl.ds(chunk * step, step)]
            copies.append((source, cot.at[:, columns(chunk, ring)]))
    first = len(copies)
    for part in range(2):
        for chunk, chunk_refs in enumerate((blocks_0, blocks_1)):
            copies += block_copies(
                where_ref, chunk_refs, lambda part, ring, chunk=chunk: blocks.at[part, :, columns(chunk, ring)]
            )[part::2]
    copies.append((tiles_ref.at[:, pl.ds(0, size)], tiles))
    each = CHUNKS * RING
    started = start_all(copies, sems)
    for copy in started[:first]:
        copy.wait()
    for part in range(2):
        for copy in started[first + part * each : first + (part + 1) * each]:
            copy.wait()
        sums[part] = dot_t(cot[...], blocks[part])
    started[-1].wait()

    def add(place, tile):
        part, row, chunk, ring, col = place
        c = block_at(chunk * 2 * RING + ring * 2 + col, size)
        sums[part, :, block_at(row, size)] += dot_t(cot[:, c], tile)

    each_slot(codes_ref, tiles, add)
    out = []
    for part in range(2):
        place = 1 - part ^ zl ^ zh
        out += start_all(
            [(sums.at[part, pl.ds(half, half)], give_ref.at[place]), (sums.at[part, pl.ds(0, half)], keep_ref.at[place])],
            sems.at[pl.ds(2 * part, 2)],
        )
    for copy in out:
        copy.wait()


def floats(*shape):
    return jax.ShapeDtypeStruct(shape, jnp.float32)


def call(kernel, outs, scalars, operands, scratch, flops, moved):
    in_specs = [pl.BlockSpec(memory_space=pltpu.SMEM)] * len(scalars)
    in_specs += [pl.BlockSpec(memory_space=pl.ANY)] * len(operands)
    return pl.pallas_call(
        kernel,
        out_shape=outs,
        in_specs=in_specs,
        out_specs=[pl.BlockSpec(memory_space=pl.ANY)] * len(outs),
        scratch_shapes=scratch,
        compiler_params=pltpu.CompilerParams(vmem_limit_bytes=VMEM_LIMIT),
        cost_estimate=pl.CostEstimate(flops=flops // COST, bytes_accessed=moved // COST, transcendentals=0),
    )(*scalars, *operands)


MIB = 1024 * 1024


def forward(scalars, tiles, acts, blocks_0, blocks_1, step):
    rows, depth = 2 * acts[0].shape[0], acts[0].shape[1]
    count, size = tiles.shape[0], tiles.shape[2]
    width = CHUNKS * step
    outs = [floats(rows, width)] * 2 + [floats(rows // 2, width)] * 2 + [floats(rows, width)]
    scratch = [
        pltpu.VMEM((rows, 2 * depth), jnp.bfloat16),
        pltpu.VMEM((count, size, size), jnp.bfloat16),
        pltpu.VMEM((CHUNKS, RING, 2 * depth, step), jnp.bfloat16),
        pltpu.VMEM((RING, rows, width), jnp.float32),
        pltpu.SemaphoreType.DMA((5 + 2 * CHUNKS * RING,)),
    ]
    flops = 4 * RING * rows * depth * width + count * rows * size * size
    operands = (tiles, *acts, *blocks_0, *blocks_1)
    return call(forward_kernel, outs, scalars, operands, scratch, flops, 24 * MIB)


def backward(scalars, tiles, cot, blocks_0, blocks_1, depth):
    rows, step = cot.shape[1], cot.shape[2] // CHUNKS
    count, size = tiles.shape[0], tiles.shape[2]
    width = CHUNKS * RING * step
    outs = [floats(2, rows // 2, depth)] * 2
    scratch = [
        pltpu.VMEM((rows, width), jnp.bfloat16),
        pltpu.VMEM((count, size, size), jnp.bfloat16),
        pltpu.VMEM((2, depth, width), jnp.bfloat16),
        pltpu.VMEM((2, rows, depth), jnp.float32),
        pltpu.SemaphoreType.DMA((1 + 3 * CHUNKS * RING,)),
    ]
    flops = 4 * rows * depth * width + count * rows * size * size
    return call(backward_kernel, outs, scalars, (tiles, cot, *blocks_0, *blocks_1), scratch, flops, 24 * MIB)


def slot_grads(scalars, acts, cot, count, size):
    outs = [floats(count, size, size)] * 2
    scratch = [
        pltpu.VMEM((cot.shape[1], 2 * acts[0].shape[1]), jnp.bfloat16),
        pltpu.VMEM(cot.shape, jnp.bfloat16),
        pltpu.VMEM((2 * count, size, size), jnp.float32),
        pltpu.SemaphoreType.DMA((5,)),
    ]
    flops = 2 * count * cot.shape[1] * size * size
    return call(grads_kernel, outs, scalars, (*acts, cot), scratch, flops, 16 * MIB)


def tie(*values):
    return lax.optimization_barrier(values)


def near(block, axis):
    return shift(block, axis, -1), shift(block, axis, 1)


def far(following, previous, axis):
    half = following.shape[0] // 2
    top = shift(previous[:half], axis, 1)
    bottom = shift(following[half:], axis, -1)
    return top, bottom


def merge(up, down, got):
    from_before, from_after = got
    half = up.shape[0] // 2
    up = jnp.concatenate([up[:half] + from_before, up[half:]], axis=0)
    down = jnp.concatenate([down[:half], down[half:] + from_after], axis=0)
    return up, down


def local(acts, frozen, delta_tiles, delta_index, delta_count, cotangent):
    x, zl, core, y, zh = (lax.axis_index(a) for a in AXES)
    tokens, width = acts.shape
    per_owner, size = delta_tiles.shape[1], delta_tiles.shape[2]
    half_width = width // 2
    step = half_width // CHUNKS
    scaling = 1.0 / math.sqrt(tokens * RING * 4)
    where = jnp.stack([x, zl, core, zh, y]).astype(jnp.int32)
    own_is_b = zh == zl

    left, right = cotangent[:, :half_width], cotangent[:, half_width:]
    keep = jnp.where(core == 0, left, right)
    give = jnp.where(core == 0, right, left)

    def along_z(block):
        part_0 = lax.ppermute(block, ("zl", "zh"), [(0, 2), (1, 0), (2, 3), (3, 1)])
        part_1 = lax.ppermute(block, ("zl", "zh"), [(1, 2), (2, 1)])
        return part_0, part_1

    def parts(block, pair):
        return pair[0], jnp.where(own_is_b, block, pair[1])

    live = jnp.arange(per_owner, dtype=jnp.int32) < delta_count[0, 0]
    info = jnp.concatenate([delta_index[0], live[:, None].astype(jnp.int32)], axis=1)
    info = jnp.pad(info[:, None, :], ((0, 0), (0, EXTRA - 1), (0, size - 3)))
    mine = jnp.concatenate([delta_tiles[0] * live[:, None, None].astype(jnp.bfloat16), info.astype(jnp.bfloat16)], axis=1)

    frozen_0, frozen_1 = frozen[:, :step], frozen[:, step:]
    got_z = along_z(frozen_0)
    next_1, prev_1 = near(frozen_1, "x")
    cot_rows = jnp.concatenate([keep, swap(give, "core")], axis=0)
    other_mine = swap(mine, "zh")
    acts, frozen_0, got_z, mine, other_mine, cot_rows, next_1, prev_1 = tie(
        acts, frozen_0, got_z, mine, other_mine, cot_rows, next_1, prev_1
    )

    tiles = lax.all_gather(jnp.concatenate([mine, other_mine], axis=0), ("x", "zl", "core"), axis=0, tiled=True)
    cot_next, cot_prev = near(cot_rows, "y")
    acts_other = swap(acts, "zh")
    wide_1 = jnp.stack([frozen_1, next_1, jnp.concatenate(far(next_1, prev_1, "x"), axis=0), prev_1])
    got_1 = along_z(wide_1)
    cot_far = jnp.concatenate(far(cot_next, cot_prev, "y"), axis=0)
    cot_rows, cot_next, cot_far, cot_prev, acts, acts_other, frozen_0, got_z = tie(
        cot_rows, cot_next, cot_far, cot_prev, acts, acts_other, frozen_0, got_z
    )

    piece_0 = jnp.concatenate(parts(frozen_0, got_z), axis=0)
    next_0, prev_0 = near(piece_0, "x")
    swapped = swap(jnp.stack([acts, acts_other]), "core")
    cot = jnp.stack([cot_rows, cot_next, cot_far, cot_prev])
    next_0, prev_0, swapped, cot = tie(next_0, prev_0, swapped, cot)
    far_0 = far(next_0, prev_0, "x")
    codes = slot_codes(where, tiles[:, size, :3].astype(jnp.int32))
    slots = codes.shape[0]
    acts_all = (acts, acts_other, swapped)
    scalars = (where, codes)
    own_grads, other_grads = slot_grads(scalars, acts_all, cot, slots // 2, size)
    own_grads, other_grads, far_0, got_1, acts_all, cot = tie(own_grads, other_grads, far_0, got_1, acts_all, cot)

    blocks_0 = (piece_0, next_0, *far_0, prev_0)
    blocks_1 = (wide_1, *got_1)
    swapped_grads = swap(other_grads, "core")
    mine_out, up, far_top, far_bottom, down = forward(scalars, tiles, acts_all, blocks_0, blocks_1, step)
    mine_out, up, far_top, far_bottom, down, own_grads, swapped_grads, cot = tie(
        mine_out, up, far_top, far_bottom, down, own_grads, swapped_grads, cot
    )

    def slab(k):
        place = ((x + k) % RING) * (slots // 8)
        return lax.dynamic_slice_in_dim(own_grads, place, slots // 8, 0) + lax.dynamic_slice_in_dim(
            swapped_grads, place, slots // 8, 0
        )

    got = shift(far_top, "y", 1), shift(far_bottom, "y", -1)
    eighth = slots // 16
    far_slab = slab(2)
    got_g = shift(far_slab[:eighth], "x", 1), shift(far_slab[eighth:], "x", -1)
    keep, give = backward(scalars, tiles, cot, blocks_0, blocks_1, width)
    keep, give, got, got_g, up, down, own_grads, swapped_grads = tie(
        keep, give, got, got_g, up, down, own_grads, swapped_grads
    )

    given = swap(give, "core")
    up, down = merge(up, down, got)
    up_g, down_g = merge(slab(1), slab(3), got_g)
    keep, given, up, down, up_g, down_g = tie(keep, given, up, down, up_g, down_g)
    back_own, back_other = keep[0] + given[0], keep[1] + given[1]
    back_got = swap(back_other, "zh")
    got = shift(up, "y", 1), shift(down, "y", -1)
    got_g = shift(up_g, "x", 1), shift(down_g, "x", -1)

    grads = slab(0) + got_g[0] + got_g[1]
    grads_zl = grads.reshape(2, -1, size, size)
    grads = lax.dynamic_index_in_dim(grads_zl, zl, 0, keepdims=False) + swap(
        lax.dynamic_index_in_dim(grads_zl, 1 - zl, 0, keepdims=False), "zl"
    )
    grads = grads[:per_owner] + swap(grads[per_owner:], "zh")
    delta_grad = (grads * scaling * live[:, None, None].astype(jnp.float32))[None]

    mine_out = (mine_out + got[0] + got[1]).astype(jnp.bfloat16)
    kept, got = mine_out[:tokens], swap(mine_out[tokens:], "core")
    output = jnp.concatenate([jnp.where(core == 0, kept, got), jnp.where(core == 0, got, kept)], axis=1)
    grad_input = (back_own + back_got).astype(jnp.bfloat16)
    return output, grad_input, delta_grad


def solution(mesh):
    fine = Mesh(mesh.devices.reshape(4, 2, 2, 4, 2), AXES)
    rows, cols = ("x", "zl", "core"), ("y", "zh")
    return jax.shard_map(
        local,
        mesh=fine,
        in_specs=(
            P(rows, cols),
            P(cols, rows),
            P(cols, rows, None, None),
            P(cols, rows, None),
            P(cols, rows),
            P(rows, cols),
        ),
        out_specs=(P(rows, cols), P(rows, cols), P(cols, rows, None, None)),
        check_vma=False,
    )
```

time: 284 us -> 264 us (0.930)
  waiting for transfers between devices: 90.9 us -> 85.4 us
  local copies, waits for them, and re-layouts: 15.8 us -> 10.6 us
  other arithmetic: 34.3 us -> 29.9 us
    ppermute x20, waiting for transfers between devices: 39.4 us -> 68.1 us  [shift(): lax.ppermute(value, axis, [(i, (i + step) % RING) for i in range(RING)])]
    ppermute x13 -> x10, waiting for transfers between devices: 44.7 us -> 16.1 us  [swap(): return lax.ppermute(value, axis, [(0, 1), (1, 0)])]
    ppermute x5 -> x2, waiting for transfers between devices: 6.76 us -> 1.2 us  [along_z(): part_0 = lax.ppermute(block, ('zl', 'zh'), [(0, 2), (1, 0), (2, 3), (3, 1)])]
    slice x7 -> x2, local copies, waits for them, and re-layouts: 5.19 us -> 1.01 us  [the longest x1 0.99 us: local(): codes = slot_codes(where, tiles[:, size, :3].astype(jnp.int32))]
    select_n x3 -> x1, other arithmetic: 3.4 us -> 0.06 us  [parts(): return (pair[0], jnp.where(own_is_b, block, pair[1]))]
    ppermute x5 -> x2, starting transfers between devices: 6.99 us -> 3.82 us  [along_z(): part_0 = lax.ppermute(block, ('zl', 'zh'), [(0, 2), (1, 0), (2, 3), (3, 1)])]
    ppermute x13 -> x10, starting transfers between devices: 26.8 us -> 29.6 us  [swap(): return lax.ppermute(value, axis, [(0, 1), (1, 0)])]
    pallas_call x4 -> x3, Pallas kernels: 60.4 us -> 57.6 us  [call(): pl.pallas_call(kernel, out_shape=outs, in_specs=in_specs, out_specs=[pl.B...]
  transfers between devices with their start and end apart: 45 -> 35, of which waited for: 14 -> 15; matrix products, arithmetic and copies ran while one was open for 16% -> 13% of each run, Pallas kernels for 21% -> 22%
where the time goes in v3:
time: 264 us; the launch traced here: 262 us
  waiting for transfers between devices  85.4 us (32%)
  starting transfers between devices  62.9 us (24%)
  Pallas kernels  57.6 us (22%)
  other arithmetic  29.9 us (11%)
  between operations  15.2 us (6%)
  local copies, waits for them, and re-layouts  10.6 us (4%)
    ppermute x20, waiting for transfers between devices, shift(): lax.ppermute(value, axis, [(i, (i + step) % RING) for i in range(RING)])  68.1 us
    pallas_call x3, Pallas kernels, call(): pl.pallas_call(kernel, out_shape=outs, in_specs=in_specs, out_specs=[pl.B...  57.6 us
    ppermute x10, starting transfers between devices, swap(): return lax.ppermute(value, axis, [(0, 1), (1, 0)])  29.6 us
    ppermute x20, starting transfers between devices, shift(): lax.ppermute(value, axis, [(i, (i + step) % RING) for i in range(RING)])  25.9 us
    ppermute x10, waiting for transfers between devices, swap(): return lax.ppermute(value, axis, [(0, 1), (1, 0)])  16.1 us
  transfers between devices with their start and end apart: 35, of which 15 were waited for; matrix products, arithmetic and copies ran while one was open for 13% of the time, Pallas kernels for 22%

profile of v3, /device:TPU:1, one launch (start us, length us, event | category | flops | bytes accessed | tf_op | source)
XLA Modules:
  0.0 261.5 jit_solution(9408972425934454858)
XLA Ops:
  19.7 5.3 %collective-permute-start.2 = (bf16[4,144,128]{2,1,0:T(8,128)(2,1)S(1)}, bf16[4,144,128]{2,1,0:T(8,128)(2,1)S(1)}, u32[]{:S(2)}, u32[]{:S(2)}) collective-permute-start(bf16[4,144,128]{2,1,0:T(8,128)(2,1)S(1)} %fusion.4), channel_id=1, source_target_pairs={{0,1},{1,0},{2,3},{3,2},{4,5},{5,4},{6,7},{7,6},{8,9},{9,8},{10,11... | collective-permute-start | bytes 442376 | tf_op jit(solution)/shard_map/ppermute | solution.py:24
  25.0 4.4 %collective-permute-done.2 = bf16[4,144,128]{2,1,0:T(8,128)(2,1)S(1)} collective-permute-done((bf16[4,144,128]{2,1,0:T(8,128)(2,1)S(1)}, bf16[4,144,128]{2,1,0:T(8,128)(2,1)S(1)}, u32[]{:S(2)}, u32[]{:S(2)}) %collective-permute-start.2) | collective-permute-done | bytes 147488 | tf_op jit(solution)/shard_map/ppermute | solution.py:24
  30.5 2.8 %collective-permute-start.6 = (bf16[768,512]{1,0:T(8,128)(2,1)S(1)}, bf16[768,512]{1,0:T(8,128)(2,1)S(1)}, u32[]{:S(2)}, u32[]{:S(2)}) collective-permute-start(bf16[768,512]{1,0:T(8,128)(2,1)S(1)} %pad_maximum_fusion.8), channel_id=1, source_target_pairs={{0,6},{2,0},{4,2},{6,4},{1,7},{3,1},{5,3},{7,5},{8,14},{10,8},{12,... | collective-permute-start | bytes 2359304 | tf_op jit(solution)/shard_map/ppermute | solution.py:20
  33.3 4.7 %collective-permute-start.10 = (bf16[384,1024]{1,0:T(8,128)(2,1)S(1)}, bf16[384,1024]{1,0:T(8,128)(2,1)S(1)}, u32[]{:S(2)}, u32[]{:S(2)}) collective-permute-start(bf16[384,1024]{1,0:T(8,128)(2,1)S(1)} %copy-done.2), channel_id=1, source_target_pairs={{0,1},{1,0},{2,3},{3,2},{4,5},{5,4},{6,7},{7,6},{8,9},{9,8},{10,11... | collective-permute-start | bytes 2359304 | tf_op jit(solution)/shard_map/ppermute | solution.py:24
  38.0 10.0 %collective-permute-done.6 = bf16[768,512]{1,0:T(8,128)(2,1)S(1)} collective-permute-done((bf16[768,512]{1,0:T(8,128)(2,1)S(1)}, bf16[768,512]{1,0:T(8,128)(2,1)S(1)}, u32[]{:S(2)}, u32[]{:S(2)}) %collective-permute-start.6) | collective-permute-done | bytes 786464 | tf_op jit(solution)/shard_map/ppermute | solution.py:20
  48.0 3.5 %collective-permute-start.9 = (bf16[384,512]{1,0:T(8,128)(2,1)S(1)}, bf16[384,512]{1,0:T(8,128)(2,1)S(1)}, u32[]{:S(2)}, u32[]{:S(2)}) collective-permute-start(bf16[384,512]{1,0:T(8,128)(2,1)S(1)} %slice.130), channel_id=1, source_target_pairs={{0,6},{2,0},{4,2},{6,4},{1,7},{3,1},{5,3},{7,5},{8,14},{10,8},{12,... | collective-permute-start | bytes 1179656 | tf_op jit(solution)/shard_map/ppermute | solution.py:20
  51.7 3.6 %collective-permute-start.17 = (bf16[512,256]{1,0:T(8,128)(2,1)S(1)}, bf16[512,256]{1,0:T(8,128)(2,1)S(1)}, u32[]{:S(2)}, u32[]{:S(2)}) collective-permute-start(bf16[512,256]{1,0:T(8,128)(2,1)S(1)} %slice.109), channel_id=1, source_target_pairs={{0,96},{32,0},{64,32},{96,64},{1,97},{33,1},{65,33},{97,65},{2,98}... | collective-permute-start | bytes 786440 | tf_op jit(solution)/shard_map/ppermute | solution.py:20
  56.3 5.6 %collective-permute-done.17 = bf16[512,256]{1,0:T(8,128)(2,1)S(1)} collective-permute-done((bf16[512,256]{1,0:T(8,128)(2,1)S(1)}, bf16[512,256]{1,0:T(8,128)(2,1)S(1)}, u32[]{:S(2)}, u32[]{:S(2)}) %collective-permute-start.17) | collective-permute-done | bytes 262176 | tf_op jit(solution)/shard_map/ppermute | solution.py:20
  61.9 3.2 %collective-permute-done.16 = bf16[512,256]{1,0:T(8,128)(2,1)S(1)} collective-permute-done((bf16[512,256]{1,0:T(8,128)(2,1)S(1)}, bf16[512,256]{1,0:T(8,128)(2,1)S(1)}, u32[]{:S(2)}, u32[]{:S(2)}) %collective-permute-start.16) | collective-permute-done | bytes 262176 | tf_op jit(solution)/shard_map/ppermute | solution.py:20
  67.6 5.5 %collective-permute-start.13 = (bf16[2,384,1024]{2,1,0:T(8,128)(2,1)}, bf16[2,384,1024]{2,1,0:T(8,128)(2,1)}, u32[]{:S(2)}, u32[]{:S(2)}) collective-permute-start(bf16[2,384,1024]{2,1,0:T(8,128)(2,1)} %pad_maximum_fusion.2), channel_id=1, source_target_pairs={{0,8},{8,0},{1,9},{9,1},{2,10},{10,2},{3,11},{11,3},{4,12},{12,4},... | collective-permute-start | bytes 4718600 | tf_op jit(solution)/shard_map/ppermute | solution.py:24
  83.4 20.8 %collective-permute-done.11.refs_4_.refs_1_ = bf16[2048,256]{1,0:T(8,128)(2,1)S(1)} collective-permute-done((bf16[2048,256]{1,0:T(8,128)(2,1)S(1)}, bf16[2048,256]{1,0:T(8,128)(2,1)S(1)}, u32[]{:S(2)}, u32[]{:S(2)}) %collective-permute-start.11) | collective-permute-done | bytes 1048608 | tf_op jit(solution)/shard_map/ppermute | solution.py:20
  111.2 13.0 %shard_map.85 = (f32[64,128,128]{2,1,0:T(8,128)}, f32[64,128,128]{2,1,0:T(8,128)}) custom-call(s32[5]{0:T(128)} %stack.62.where_ref, s32[128]{0:T(128)} %bitcast_select_fusion.codes_ref, bf16[384,1024]{1,0:T(8,128)(2,1)} %refs_0_.1, bf16[384,1024]{1,0:T(8,128)(2,1)} %copy-done.3, bf16[2,384,1024]{2,1,0:T(8,128)(2,1)} %collective-permute-done.13.refs_2_, ...), custom_call_target="tpu_custom_call" | custom-call | flops 1610612 | bytes 16777 | tf_op jit(solution)/shard_map/pallas_call | solution.py:263
  127.7 25.3 %shard_map.86 = (f32[768,512]{1,0:T(8,128)}, f32[768,512]{1,0:T(8,128)}, f32[384,512]{1,0:T(8,128)}, f32[384,512]{1,0:T(8,128)}, f32[768,512]{1,0:T(8,128)}) custom-call(s32[5]{0:T(128)} %stack.62.where_ref, s32[128]{0:T(128)} %bitcast_select_fusion.codes_ref, bf16[128,144,128]{2,1,0:T(8,128)(2,1)} %all-gather.2.cloned.1.call-done.tiles_ref, ...), custom_call_target="tpu_custom_call" | custom-call | flops 8053063 | bytes 25165 | tf_op jit(solution)/shard_map/pallas_call | solution.py:263
  157.6 2.7 %collective-permute-start.24 = (f32[8,128,128]{2,1,0:T(8,128)S(1)}, f32[8,128,128]{2,1,0:T(8,128)S(1)}, u32[]{:S(2)}, u32[]{:S(2)}) collective-permute-start(f32[8,128,128]{2,1,0:T(8,128)S(1)} %get-tuple-element.145), channel_id=1, source_target_pairs={{0,96},{32,0},{64,32},{96,64},{1,97},{33,1},{65,33},{97,65},{2,98}... | collective-permute-start | bytes 1572872 | tf_op jit(solution)/shard_map/ppermute | solution.py:20
  160.2 19.3 %shard_map.87 = (f32[2,384,1024]{2,1,0:T(8,128)}, f32[2,384,1024]{2,1,0:T(8,128)}) custom-call(s32[5]{0:T(128)} %stack.62.where_ref, s32[128]{0:T(128)} %bitcast_select_fusion.codes_ref, bf16[128,144,128]{2,1,0:T(8,128)(2,1)} %all-gather.2.cloned.1.call-done.tiles_ref, bf16[4,768,512]{2,1,0:T(8,128)(2,1)} %pad_maximum_fusion.refs_3_.cot_ref, ...), custom_call_target="tpu_custom_call" | custom-call | flops 8053063 | bytes 25165 | tf_op jit(solution)/shard_map/pallas_call | solution.py:263
  181.0 3.1 %collective-permute-start.25 = (f32[2,384,1024]{2,1,0:T(8,128)}, f32[2,384,1024]{2,1,0:T(8,128)S(1)}, u32[]{:S(2)}, u32[]{:S(2)}) collective-permute-start(f32[2,384,1024]{2,1,0:T(8,128)} %get-tuple-element.118), channel_id=1, source_target_pairs={{0,8},{8,0},{1,9},{9,1},{2,10},{10,2},{3,11},{11,3},{4,12},{12,4},... | collective-permute-start | bytes 9437192 | tf_op jit(solution)/shard_map/ppermute | solution.py:24
  184.1 2.5 dynamic-slice_add_fusion
  197.6 20.7 %collective-permute-done.31 = f32[16,128,128]{2,1,0:T(8,128)} collective-permute-done((f32[16,128,128]{2,1,0:T(8,128)}, f32[16,128,128]{2,1,0:T(8,128)}, u32[]{:S(2)}, u32[]{:S(2)}) %collective-permute-start.31) | collective-permute-done | bytes 1048608 | tf_op jit(solution)/shard_map/ppermute | solution.py:20
  219.6 2.6 add_add_fusion
  223.0 2.7 %collective-permute-start.32 = (f32[8,128,128]{2,1,0:T(8,128)}, f32[8,128,128]{2,1,0:T(8,128)S(1)}, u32[]{:S(2)}, u32[]{:S(2)}) collective-permute-start(f32[8,128,128]{2,1,0:T(8,128)} %dynamic-slice_bitcast_fusion), channel_id=1, source_target_pairs={{0,16},{16,0},{1,17},{17,1},{2,18},{18,2},{3,19},{19,3},{4,20},{20... | collective-permute-start | bytes 1572872 | tf_op jit(solution)/shard_map/ppermute | solution.py:24
  225.7 4.7 %collective-permute-done.27 = f32[768,512]{1,0:T(8,128)} collective-permute-done((f32[768,512]{1,0:T(8,128)}, f32[768,512]{1,0:T(8,128)}, u32[]{:S(2)}, u32[]{:S(2)}) %collective-permute-start.27) | collective-permute-done | bytes 1572896 | tf_op jit(solution)/shard_map/ppermute | solution.py:20
  235.6 9.7 %collective-permute-done.32 = f32[8,128,128]{2,1,0:T(8,128)S(1)} collective-permute-done((f32[8,128,128]{2,1,0:T(8,128)}, f32[8,128,128]{2,1,0:T(8,128)S(1)}, u32[]{:S(2)}, u32[]{:S(2)}) %collective-permute-start.32) | collective-permute-done | bytes 524320 | tf_op jit(solution)/shard_map/ppermute | solution.py:24
  245.4 3.3 %collective-permute-start.33 = (f32[4,128,128]{2,1,0:T(8,128)S(1)}, f32[4,128,128]{2,1,0:T(8,128)S(1)}, u32[]{:S(2)}, u32[]{:S(2)}) collective-permute-start(f32[4,128,128]{2,1,0:T(8,128)S(1)} %slice.140), channel_id=1, source_target_pairs={{0,1},{1,0},{2,3},{3,2},{4,5},{5,4},{6,7},{7,6},{8,9},{9,8},{10,11... | collective-permute-start | bytes 786440 | tf_op jit(solution)/shard_map/ppermute | solution.py:24
  248.8 2.7 %fusion = bf16[384,1024]{1,0:T(8,128)(2,1)} fusion(f32[384,1024]{1,0:T(8,128)} %collective-permute-done.29, f32[2,384,1024]{2,1,0:T(8,128)S(1)} %copy-done.10, f32[2,384,1024]{2,1,0:T(8,128)S(1)} %copy-done.8), kind=kLoop, calls=%fused_computation.6 | loop fusion | flops 1179648 | bytes 5505024 | tf_op jit(solution)/shard_map/convert_element_type | solution.py:447
  (169 shorter events, 64.7 us)
Async XLA Ops:
  7.2 102.4 %all-gather.2.cloned.1.call-start = ((), (), s32[]{:S(2)}) async-start(), calls=%async_computation | async-start | bytes 5013504 | tf_op jit(solution)/shard_map/all_gather | solution.py:381
  9.6 19.8 %collective-permute-start = (bf16[1024,256]{1,0:T(8,128)(2,1)S(1)}, bf16[1024,256]{1,0:T(8,128)(2,1)}, u32[]{:S(2)}, u32[]{:S(2)}) collective-permute-start(bf16[1024,256]{1,0:T(8,128)(2,1)S(1)} %get-tuple-element.78), channel_id=1, source_target_pairs={{0,16},{1,0},{16,17},{17,1},{2,18},{3,2},{18,19},{19,3},{4,20},{5,... | collective-permute-start | bytes 1572872 | tf_op jit(solution)/shard_map/ppermute | solution.py:360
  30.5 17.5 %collective-permute-start.6 = (bf16[768,512]{1,0:T(8,128)(2,1)S(1)}, bf16[768,512]{1,0:T(8,128)(2,1)S(1)}, u32[]{:S(2)}, u32[]{:S(2)}) collective-permute-start(bf16[768,512]{1,0:T(8,128)(2,1)S(1)} %pad_maximum_fusion.8), channel_id=1, source_target_pairs={{0,6},{2,0},{4,2},{6,4},{1,7},{3,1},{5,3},{7,5},{8,14},{10,8},{12,... | collective-permute-start | bytes 2359304 | tf_op jit(solution)/shard_map/ppermute | solution.py:20
  33.3 18.2 %collective-permute-start.7 = (bf16[768,512]{1,0:T(8,128)(2,1)S(1)}, bf16[768,512]{1,0:T(8,128)(2,1)S(1)}, u32[]{:S(2)}, u32[]{:S(2)}) collective-permute-start(bf16[768,512]{1,0:T(8,128)(2,1)S(1)} %pad_maximum_fusion.8), channel_id=1, source_target_pairs={{0,2},{2,4},{4,6},{6,0},{1,3},{3,5},{5,7},{7,1},{8,10},{10,12},{12... | collective-permute-start | bytes 2359304 | tf_op jit(solution)/shard_map/ppermute | solution.py:20
  33.3 32.8 %collective-permute-start.10 = (bf16[384,1024]{1,0:T(8,128)(2,1)S(1)}, bf16[384,1024]{1,0:T(8,128)(2,1)S(1)}, u32[]{:S(2)}, u32[]{:S(2)}) collective-permute-start(bf16[384,1024]{1,0:T(8,128)(2,1)S(1)} %copy-done.2), channel_id=1, source_target_pairs={{0,1},{1,0},{2,3},{3,2},{4,5},{5,4},{6,7},{7,6},{8,9},{9,8},{10,11... | collective-permute-start | bytes 2359304 | tf_op jit(solution)/shard_map/ppermute | solution.py:24
  67.6 36.9 %collective-permute-start.13 = (bf16[2,384,1024]{2,1,0:T(8,128)(2,1)}, bf16[2,384,1024]{2,1,0:T(8,128)(2,1)}, u32[]{:S(2)}, u32[]{:S(2)}) collective-permute-start(bf16[2,384,1024]{2,1,0:T(8,128)(2,1)} %pad_maximum_fusion.2), channel_id=1, source_target_pairs={{0,8},{8,0},{1,9},{9,1},{2,10},{10,2},{3,11},{11,3},{4,12},{12,4},... | collective-permute-start | bytes 4718600 | tf_op jit(solution)/shard_map/ppermute | solution.py:24
  74.4 51.0 %collective-permute-start.18 = (bf16[4,1024,256]{2,1,0:T(8,128)(2,1)S(1)}, bf16[4,1024,256]{2,1,0:T(8,128)(2,1)}, u32[]{:S(2)}, u32[]{:S(2)}) collective-permute-start(bf16[4,1024,256]{2,1,0:T(8,128)(2,1)S(1)} %pad_maximum_fusion.1.refs_8_.refs_5_), channel_id=1, source_target_pairs={{0,16},{1,0},{16,17},{17,1},{2,18},{3,2},{18,19},{19,3},{4,20},{5,... | collective-permute-start | bytes 6291464 | tf_op jit(solution)/shard_map/ppermute | solution.py:360
  75.7 49.7 %collective-permute-start.19 = (bf16[4,1024,256]{2,1,0:T(8,128)(2,1)S(1)}, bf16[4,1024,256]{2,1,0:T(8,128)(2,1)}, u32[]{:S(2)}, u32[]{:S(2)}) collective-permute-start(bf16[4,1024,256]{2,1,0:T(8,128)(2,1)S(1)} %pad_maximum_fusion.1.refs_8_.refs_5_), channel_id=1, source_target_pairs={{1,16},{16,1},{3,18},{18,3},{5,20},{20,5},{7,22},{22,7},{9,24},{24... | collective-permute-start | bytes 6291464 | tf_op jit(solution)/shard_map/ppermute | solution.py:361
  79.1 25.1 %collective-permute-start.11 = (bf16[2048,256]{1,0:T(8,128)(2,1)S(1)}, bf16[2048,256]{1,0:T(8,128)(2,1)S(1)}, u32[]{:S(2)}, u32[]{:S(2)}) collective-permute-start(bf16[2048,256]{1,0:T(8,128)(2,1)S(1)} %pad_maximum_fusion.5.refs_3_.refs_0_), channel_id=1, source_target_pairs={{0,96},{32,0},{64,32},{96,64},{1,97},{33,1},{65,33},{97,65},{2,98}... | collective-permute-start | bytes 3145736 | tf_op jit(solution)/shard_map/ppermute | solution.py:20
  79.6 24.8 %collective-permute-start.12 = (bf16[2048,256]{1,0:T(8,128)(2,1)S(1)}, bf16[2048,256]{1,0:T(8,128)(2,1)S(1)}, u32[]{:S(2)}, u32[]{:S(2)}) collective-permute-start(bf16[2048,256]{1,0:T(8,128)(2,1)S(1)} %pad_maximum_fusion.5.refs_3_.refs_0_), channel_id=1, source_target_pairs={{0,32},{32,64},{64,96},{96,0},{1,33},{33,65},{65,97},{97,1},{2,34}... | collective-permute-start | bytes 3145736 | tf_op jit(solution)/shard_map/ppermute | solution.py:20
  105.4 20.0 %collective-permute-start.14 = (bf16[1024,256]{1,0:T(8,128)(2,1)}, bf16[1024,256]{1,0:T(8,128)(2,1)S(1)}, u32[]{:S(2)}, u32[]{:S(2)}) collective-permute-start(bf16[1024,256]{1,0:T(8,128)(2,1)} %slice.106), channel_id=1, source_target_pairs={{0,32},{32,64},{64,96},{96,0},{1,33},{33,65},{65,97},{97,1},{2,34}... | collective-permute-start | bytes 1572872 | tf_op jit(solution)/shard_map/ppermute | solution.py:20
  107.2 18.2 %collective-permute-start.15 = (bf16[1024,256]{1,0:T(8,128)(2,1)}, bf16[1024,256]{1,0:T(8,128)(2,1)S(1)}, u32[]{:S(2)}, u32[]{:S(2)}) collective-permute-start(bf16[1024,256]{1,0:T(8,128)(2,1)} %slice.107), channel_id=1, source_target_pairs={{0,96},{32,0},{64,32},{96,64},{1,97},{33,1},{65,33},{97,65},{2,98}... | collective-permute-start | bytes 1572872 | tf_op jit(solution)/shard_map/ppermute | solution.py:20
  125.4 27.5 %collective-permute-start.20 = (f32[64,128,128]{2,1,0:T(8,128)}, f32[64,128,128]{2,1,0:T(8,128)}, u32[]{:S(2)}, u32[]{:S(2)}) collective-permute-start(f32[64,128,128]{2,1,0:T(8,128)} %get-tuple-element.105), channel_id=1, source_target_pairs={{0,8},{8,0},{1,9},{9,1},{2,10},{10,2},{3,11},{11,3},{4,12},{12,4},... | collective-permute-start | bytes 12582920 | tf_op jit(solution)/shard_map/ppermute | solution.py:24
  153.0 26.6 %collective-permute-start.21 = (f32[384,512]{1,0:T(8,128)}, f32[384,512]{1,0:T(8,128)S(1)}, u32[]{:S(2)}, u32[]{:S(2)}) collective-permute-start(f32[384,512]{1,0:T(8,128)} %get-tuple-element.111), channel_id=1, source_target_pairs={{0,2},{2,4},{4,6},{6,0},{1,3},{3,5},{5,7},{7,1},{8,10},{10,12},{12... | collective-permute-start | bytes 2359304 | tf_op jit(solution)/shard_map/ppermute | solution.py:20
  153.4 26.2 %collective-permute-start.22 = (f32[384,512]{1,0:T(8,128)}, f32[384,512]{1,0:T(8,128)S(1)}, u32[]{:S(2)}, u32[]{:S(2)}) collective-permute-start(f32[384,512]{1,0:T(8,128)} %get-tuple-element.112), channel_id=1, source_target_pairs={{0,6},{2,0},{4,2},{6,4},{1,7},{3,1},{5,3},{7,5},{8,14},{10,8},{12,... | collective-permute-start | bytes 2359304 | tf_op jit(solution)/shard_map/ppermute | solution.py:20
  157.5 22.1 %collective-permute-start.23 = (f32[8,128,128]{2,1,0:T(8,128)S(1)}, f32[8,128,128]{2,1,0:T(8,128)S(1)}, u32[]{:S(2)}, u32[]{:S(2)}) collective-permute-start(f32[8,128,128]{2,1,0:T(8,128)S(1)} %get-tuple-element.146), channel_id=1, source_target_pairs={{0,32},{32,64},{64,96},{96,0},{1,33},{33,65},{65,97},{97,1},{2,34}... | collective-permute-start | bytes 1572872 | tf_op jit(solution)/shard_map/ppermute | solution.py:20
  157.6 22.0 %collective-permute-start.24 = (f32[8,128,128]{2,1,0:T(8,128)S(1)}, f32[8,128,128]{2,1,0:T(8,128)S(1)}, u32[]{:S(2)}, u32[]{:S(2)}) collective-permute-start(f32[8,128,128]{2,1,0:T(8,128)S(1)} %get-tuple-element.145), channel_id=1, source_target_pairs={{0,96},{32,0},{64,32},{96,64},{1,97},{33,1},{65,33},{97,65},{2,98}... | collective-permute-start | bytes 1572872 | tf_op jit(solution)/shard_map/ppermute | solution.py:20
  193.2 25.1 %collective-permute-start.31 = (f32[16,128,128]{2,1,0:T(8,128)}, f32[16,128,128]{2,1,0:T(8,128)}, u32[]{:S(2)}, u32[]{:S(2)}) collective-permute-start(f32[16,128,128]{2,1,0:T(8,128)} %pad_maximum_fusion.7), channel_id=1, source_target_pairs={{0,96},{32,0},{64,32},{96,64},{1,97},{33,1},{65,33},{97,65},{2,98}... | collective-permute-start | bytes 3145736 | tf_op jit(solution)/shard_map/ppermute | solution.py:20
  193.2 26.4 %collective-permute-start.30 = (f32[16,128,128]{2,1,0:T(8,128)}, f32[16,128,128]{2,1,0:T(8,128)}, u32[]{:S(2)}, u32[]{:S(2)}) collective-permute-start(f32[16,128,128]{2,1,0:T(8,128)} %pad_maximum_fusion.6), channel_id=1, source_target_pairs={{0,32},{32,64},{64,96},{96,0},{1,33},{33,65},{65,97},{97,1},{2,34}... | collective-permute-start | bytes 3145736 | tf_op jit(solution)/shard_map/ppermute | solution.py:20
  194.6 35.7 %collective-permute-start.27 = (f32[768,512]{1,0:T(8,128)}, f32[768,512]{1,0:T(8,128)}, u32[]{:S(2)}, u32[]{:S(2)}) collective-permute-start(f32[768,512]{1,0:T(8,128)} %pad_maximum_fusion.4), channel_id=1, source_target_pairs={{0,6},{2,0},{4,2},{6,4},{1,7},{3,1},{5,3},{7,5},{8,14},{10,8},{12,... | collective-permute-start | bytes 4718600 | tf_op jit(solution)/shard_map/ppermute | solution.py:20
  194.7 36.9 %collective-permute-start.26 = (f32[768,512]{1,0:T(8,128)}, f32[768,512]{1,0:T(8,128)}, u32[]{:S(2)}, u32[]{:S(2)}) collective-permute-start(f32[768,512]{1,0:T(8,128)} %pad_maximum_fusion.3), channel_id=1, source_target_pairs={{0,2},{2,4},{4,6},{6,0},{1,3},{3,5},{5,7},{7,1},{8,10},{10,12},{12... | collective-permute-start | bytes 4718600 | tf_op jit(solution)/shard_map/ppermute | solution.py:20
  197.6 51.2 %collective-permute-start.29 = (f32[384,1024]{1,0:T(8,128)}, f32[384,1024]{1,0:T(8,128)}, u32[]{:S(2)}, u32[]{:S(2)}) collective-permute-start(f32[384,1024]{1,0:T(8,128)} %add_bitcast_fusion), channel_id=1, source_target_pairs={{0,1},{1,0},{2,3},{3,2},{4,5},{5,4},{6,7},{7,6},{8,9},{9,8},{10,11... | collective-permute-start | bytes 4718600 | tf_op jit(solution)/shard_map/ppermute | solution.py:24
  223.0 22.4 %collective-permute-start.32 = (f32[8,128,128]{2,1,0:T(8,128)}, f32[8,128,128]{2,1,0:T(8,128)S(1)}, u32[]{:S(2)}, u32[]{:S(2)}) collective-permute-start(f32[8,128,128]{2,1,0:T(8,128)} %dynamic-slice_bitcast_fusion), channel_id=1, source_target_pairs={{0,16},{16,0},{1,17},{17,1},{2,18},{18,2},{3,19},{19,3},{4,20},{20... | collective-permute-start | bytes 1572872 | tf_op jit(solution)/shard_map/ppermute | solution.py:24
  234.1 19.5 %collective-permute-start.28 = (bf16[384,512]{1,0:T(8,128)(2,1)S(1)}, bf16[384,512]{1,0:T(8,128)(2,1)S(1)}, u32[]{:S(2)}, u32[]{:S(2)}) collective-permute-start(bf16[384,512]{1,0:T(8,128)(2,1)S(1)} %slice.138), channel_id=1, source_target_pairs={{0,8},{8,0},{1,9},{9,1},{2,10},{10,2},{3,11},{11,3},{4,12},{12,4},... | collective-permute-start | bytes 1179656 | tf_op jit(solution)/shard_map/ppermute | solution.py:24
  (45 other events, 350.1 us)
Sparse Core Ops, SparseCore 0:
  30.6 51.2 all-gather.1

commit v4 on v3

v4 whole, which is shorter than its diff:
```python
import functools
import math

import jax
import jax.numpy as jnp
from jax import lax
from jax.experimental import pallas as pl
from jax.experimental.pallas import tpu as pltpu
from jax.sharding import Mesh, PartitionSpec as P

AXES = ("x", "zl", "core", "y", "zh")
RING = 4
CHUNKS = 2
EXTRA = 16
COST = 1000
VMEM_LIMIT = 60 * 1024 * 1024


def shift(value, axis, step):
    return lax.ppermute(value, axis, [(i, (i + step) % RING) for i in range(RING)])


def swap(value, axis):
    return lax.ppermute(value, axis, [(0, 1), (1, 0)])


def dot(a, b):
    return jnp.dot(a, b, preferred_element_type=jnp.float32)


def dot_t(a, b):
    return lax.dot_general(a, b, (((1,), (1,)), ((), ())), preferred_element_type=jnp.float32)


def slot_codes(where, info):
    x, zl, core, zh, _ = (where[i] for i in range(5))
    row, col, live = info[:, 0], info[:, 1], info[:, 2]
    slot = jnp.arange(info.shape[0], dtype=jnp.int32)
    slice_zh = zh ^ ((slot >> 2) & 1)
    here = (live > 0) & (((col >> 3) & 1) == zh) & (((col >> 2) & 1) == core)
    ring = ((col >> 4) + RING - x) & 3
    part = 1 - (slice_zh ^ zl)
    code = (part << 8) | (row << 5) | (((col >> 1) & 1) << 4) | (ring << 2) | (col & 1)
    return jnp.where(here, code, -1)


def slot_place(code):
    return code >> 8, (code >> 5) & 7, (code >> 4) & 1, (code >> 2) & 3, code & 1


def block_at(index, size):
    return pl.ds(pl.multiple_of(index * size, size), size)


def start_all(copies, sems):
    started = []
    for i, (source, target, *choice) in enumerate(copies):
        copy = pltpu.make_async_copy(source, target, sems.at[i])
        if choice:
            flag, instead = choice
            pl.when(flag)(pltpu.make_async_copy(instead, target, sems.at[i]).start)
            pl.when(jnp.logical_not(flag))(copy.start)
        else:
            copy.start()
        started.append(copy)
    return started


def each_slot(codes_ref, tiles_ref, body):
    def one(slot, carry):
        code = codes_ref[slot]

        @pl.when(code >= 0)
        def _():
            body(slot_place(code), tiles_ref[slot])

        return carry

    lax.fori_loop(0, tiles_ref.shape[0], one, 0)


def block_copies(where_ref, refs, part, rows, target_of):
    same = where_ref[1] == where_ref[3]
    first, length = rows
    copies = []
    for ring in range(RING):
        target = target_of(ring)
        if len(refs) == 6:
            sent, got = (
                ref.at[ring % 2, pl.ds(first, length)] for ref in (refs[ring // 2], refs[2 + ring // 2 * 2 + part])
            )
            copies.append((got, target, same, sent) if part == 1 else (got, target))
        elif ring == 2:
            copies.append((refs[2 + part].at[pl.ds(first, length)], target))
        else:
            depth = refs[0].shape[0] // 2
            copies.append((refs[(0, 1, None, 4)[ring]].at[pl.ds(part * depth + first, length)], target))
    return copies


def clear(ref):
    def one(i, carry):
        ref[i] = jnp.zeros(ref.shape[1:], ref.dtype)
        return carry

    lax.fori_loop(0, ref.shape[0], one, 0)


def acts_copies(where_ref, refs, acts):
    own = 1 - where_ref[3] ^ where_ref[1]
    acts_ref, other_ref, swapped_ref = refs
    tokens, depth = acts_ref.shape
    rows = pl.ds(0, tokens), pl.ds(tokens, tokens)
    cols = [pl.ds(pl.multiple_of(part * depth, depth), depth) for part in (own, 1 - own)]
    return [
        (acts_ref, acts.at[rows[0], cols[0]]),
        (other_ref, acts.at[rows[0], cols[1]]),
        (swapped_ref.at[0], acts.at[rows[1], cols[0]]),
        (swapped_ref.at[1], acts.at[rows[1], cols[1]]),
    ]


def slot_forward_kernel(where_ref, codes_ref, tiles_ref, *refs):
    acts_refs, (out_ref, acts, tiles, sums, sems) = refs[:3], refs[3:]
    size = tiles.shape[2]
    rows = acts.shape[1] // size // 2
    per_chunk = sums.shape[2] // size // CHUNKS
    started = start_all([*acts_copies(where_ref, acts_refs, acts), (tiles_ref.at[:, pl.ds(0, size)], tiles)], sems)
    clear(sums)
    for copy in started:
        copy.wait()

    def add(place, tile):
        part, row, chunk, ring, col = place
        r, c = block_at(part * rows + row, size), block_at(chunk * per_chunk + col, size)
        sums[ring, :, c] += dot(acts[:, r], tile)

    each_slot(codes_ref, tiles, add)
    for copy in start_all([(sums, out_ref)], sems):
        copy.wait()


def slot_backward_kernel(where_ref, codes_ref, tiles_ref, cot_ref, *refs):
    acts_refs, (back_ref, own_ref, other_ref, acts, cot, tiles, sums, grads, sems) = refs[:3], refs[3:]
    size = tiles.shape[2]
    half = own_ref.shape[0]
    rows = acts.shape[1] // size // 2
    x, core, y = where_ref[0], where_ref[2], where_ref[4]
    copies = [*acts_copies(where_ref, acts_refs, acts), (cot_ref, cot), (tiles_ref.at[:, pl.ds(0, size)], tiles)]
    started = start_all(copies, sems)
    clear(sums)
    for copy in started:
        copy.wait()

    def fill(owner_core, first):
        def one(i, carry):
            slot = ((i >> 4) << 5) + (owner_core << 4) + (i & 15)
            code = codes_ref[slot]

            @pl.when(code >= 0)
            def _():
                part, row, chunk, ring, col = slot_place(code)
                cots = cot[(ring + x + RING - y) & 3, :, block_at(2 * chunk + col, size)]
                sums[part, :, block_at(row, size)] += dot_t(cots, tiles[slot])
                grads[first + i] = lax.dot_general(
                    acts[:, block_at(part * rows + row, size)],
                    cots,
                    (((0,), (0,)), ((), ())),
                    preferred_element_type=jnp.float32,
                )

            @pl.when(code < 0)
            def _():
                grads[first + i] = jnp.zeros((size, size), jnp.float32)

            return carry

        lax.fori_loop(0, half, one, 0)

    fill(1 - core, half)
    other_out = pltpu.make_async_copy(grads.at[pl.ds(half, half)], other_ref, sems.at[0])
    other_out.start()
    fill(core, 0)
    last = [
        pltpu.make_async_copy(grads.at[pl.ds(0, half)], own_ref, sems.at[1]),
        pltpu.make_async_copy(sums, back_ref, sems.at[2]),
    ]
    for copy in last:
        copy.start()
    for copy in (other_out, *last):
        copy.wait()


def forward_kernel(where_ref, delta_ref, *refs):
    acts_refs, blocks_0, blocks_1, rest = refs[:3], refs[3:8], refs[8:14], refs[14:]
    (mine_ref, up_ref, far_top_ref, far_bottom_ref, down_ref), (acts, blocks, sums, sems, out_sems) = rest[:5], rest[5:]
    x, y = where_ref[0], where_ref[4]
    step = sums.shape[2] // CHUNKS
    depth = blocks.shape[1] // 2
    half = acts.shape[0] // 2

    rings = [[(delta_ref.at[ring], sums.at[ring])] for ring in range(RING)]
    for chunk, chunk_refs in enumerate((blocks_0, blocks_1)):
        for part in range(2):

            def target(ring, chunk=chunk, part=part):
                return blocks.at[ring, pl.ds(part * depth, depth), pl.ds(chunk * step, step)]

            for ring, copy in enumerate(block_copies(where_ref, chunk_refs, part, (0, depth), target)):
                rings[ring].append(copy)
    each = len(rings[0])
    started = start_all(acts_copies(where_ref, acts_refs, acts) + rings[0], sems)
    for ring in range(RING):
        for copy in started:
            copy.wait()
        if ring + 1 < RING:
            started = start_all(rings[ring + 1], sems.at[pl.ds((ring % 2 + 1) * 9, each)])
        sums[ring] += dot(acts[...], blocks[ring])
        place = (x + RING + ring - y) & 3
        for k, ref in ((0, mine_ref), (1, up_ref), (3, down_ref)):
            pl.when(place == k)(pltpu.make_async_copy(sums.at[ring], ref, out_sems.at[k]).start)
        for i, ref in enumerate((far_top_ref, far_bottom_ref)):
            source = sums.at[ring, pl.ds(i * half, half)]
            pl.when(place == 2)(pltpu.make_async_copy(source, ref, out_sems.at[2 + 2 * i]).start)
    for k, ref in ((0, mine_ref), (1, up_ref), (3, down_ref), (2, far_top_ref), (4, far_bottom_ref)):
        pltpu.make_async_copy(sums.at[0, pl.ds(0, ref.shape[0])], ref, out_sems.at[k]).wait()


def backward_kernel(own, where_ref, delta_ref, cot_ref, *refs):
    blocks_0, blocks_1, rest = refs[:5], refs[5:11], refs[11:]
    (keep_ref, give_ref), (cot, blocks, sums, sems, out_sems) = rest[:2], rest[2:]
    x, zl, zh, y = where_ref[0], where_ref[1], where_ref[3], where_ref[4]
    mine = 1 - zh ^ zl if own else zh ^ zl
    step = cot_ref.shape[2] // CHUNKS
    tokens = keep_ref.shape[0]
    half = blocks.shape[0] // 2
    each = CHUNKS * RING

    def columns(n):
        return pl.ds(n * step, step)

    cots = []
    for chunk in range(CHUNKS):
        for ring in range(RING):
            source = cot_ref.at[(x + ring + RING - y) & 3, :, pl.ds(chunk * step, step)]
            cots.append((source, cot.at[:, columns(chunk * RING + ring)]))

    def start_piece(i):
        rows = pl.ds(i * half, half)
        for part in range(2):

            @pl.when(mine == part)
            def _(part=part):
                copies = []
                for chunk, chunk_refs in enumerate((blocks_0, blocks_1)):

                    def target(ring, chunk=chunk):
                        return blocks.at[rows, columns(chunk * RING + ring)]

                    copies += block_copies(where_ref, chunk_refs, part, (i * half, half), target)
                start_all(copies, sems.at[pl.ds(each * (1 + i), each)])

        waits = [pltpu.make_async_copy(delta_ref.at[mine, :, rows], sums.at[:, rows], out_sems.at[i])]
        waits[0].start()
        for n in range(each):
            target = blocks.at[rows, columns(n)]
            waits.append(pltpu.make_async_copy(target, target, sems.at[each * (1 + i) + n]))
        return waits

    started = start_all(cots, sems) + start_piece(0)
    for i in range(2):
        for copy in started:
            copy.wait()
        if i == 0:
            started = start_piece(1)
        rows = slice(i * half, (i + 1) * half)
        sums[:, rows] += dot_t(cot[...], blocks[rows])
    out = start_all([(sums.at[pl.ds(tokens, tokens)], give_ref), (sums.at[pl.ds(0, tokens)], keep_ref)], out_sems)
    for copy in out:
        copy.wait()


def floats(*shape):
    return jax.ShapeDtypeStruct(shape, jnp.float32)


def call(kernel, outs, scalars, operands, scratch, flops, moved):
    in_specs = [pl.BlockSpec(memory_space=pltpu.SMEM)] * len(scalars)
    in_specs += [pl.BlockSpec(memory_space=pl.ANY)] * len(operands)
    return pl.pallas_call(
        kernel,
        out_shape=outs,
        in_specs=in_specs,
        out_specs=[pl.BlockSpec(memory_space=pl.ANY)] * len(outs),
        scratch_shapes=scratch,
        compiler_params=pltpu.CompilerParams(vmem_limit_bytes=VMEM_LIMIT),
        cost_estimate=pl.CostEstimate(flops=flops // COST, bytes_accessed=moved // COST, transcendentals=0),
    )(*scalars, *operands)


MIB = 1024 * 1024


def slot_forward(scalars, tiles, acts, width):
    rows, depth = 2 * acts[0].shape[0], acts[0].shape[1]
    count, size = tiles.shape[0], tiles.shape[2]
    scratch = [
        pltpu.VMEM((rows, 2 * depth), jnp.bfloat16),
        pltpu.VMEM((count, size, size), jnp.bfloat16),
        pltpu.VMEM((RING, rows, width), jnp.float32),
        pltpu.SemaphoreType.DMA((5,)),
    ]
    flops = count * rows * size * size
    return call(slot_forward_kernel, [floats(RING, rows, width)], scalars, (tiles, *acts), scratch, flops, 16 * MIB)[0]


def slot_backward(scalars, tiles, cot, acts):
    rows, depth = 2 * acts[0].shape[0], acts[0].shape[1]
    count, size = tiles.shape[0], tiles.shape[2]
    outs = [floats(2, rows, depth)] + [floats(count // 2, size, size)] * 2
    scratch = [
        pltpu.VMEM((rows, 2 * depth), jnp.bfloat16),
        pltpu.VMEM(cot.shape, jnp.bfloat16),
        pltpu.VMEM((count, size, size), jnp.bfloat16),
        pltpu.VMEM((2, rows, depth), jnp.float32),
        pltpu.VMEM((count, size, size), jnp.float32),
        pltpu.SemaphoreType.DMA((6,)),
    ]
    flops = 2 * count * rows * size * size
    return call(slot_backward_kernel, outs, scalars, (tiles, cot, *acts), scratch, flops, 24 * MIB)


def forward(where, delta, acts, blocks_0, blocks_1):
    rows, depth = 2 * acts[0].shape[0], acts[0].shape[1]
    width = delta.shape[2]
    outs = [floats(rows, width)] * 2 + [floats(rows // 2, width)] * 2 + [floats(rows, width)]
    scratch = [
        pltpu.VMEM((rows, 2 * depth), jnp.bfloat16),
        pltpu.VMEM((RING, 2 * depth, width), jnp.bfloat16),
        pltpu.VMEM((RING, rows, width), jnp.float32),
        pltpu.SemaphoreType.DMA((27,)),
        pltpu.SemaphoreType.DMA((5,)),
    ]
    flops = 4 * RING * rows * depth * width
    operands = (delta, *acts, *blocks_0, *blocks_1)
    return call(forward_kernel, outs, (where,), operands, scratch, flops, 24 * MIB)


def backward(own, where, delta, cot, blocks_0, blocks_1):
    _, rows, depth = delta.shape
    width = RING * cot.shape[2]
    outs = [floats(rows // 2, depth)] * 2
    scratch = [
        pltpu.VMEM((rows, width), jnp.bfloat16),
        pltpu.VMEM((depth, width), jnp.bfloat16),
        pltpu.VMEM((rows, depth), jnp.float32),
        pltpu.SemaphoreType.DMA((3 * CHUNKS * RING,)),
        pltpu.SemaphoreType.DMA((2,)),
    ]
    flops = 2 * rows * depth * width
    operands = (delta, cot, *blocks_0, *blocks_1)
    return call(functools.partial(backward_kernel, own), outs, (where,), operands, scratch, flops, 16 * MIB)


def tie(*values):
    return lax.optimization_barrier(values)


def near(block, axis):
    return shift(block, axis, -1), shift(block, axis, 1)


def far(following, previous, axis):
    half = following.shape[0] // 2
    top = shift(previous[:half], axis, 1)
    bottom = shift(following[half:], axis, -1)
    return top, bottom


def merge(up, down, got):
    from_before, from_after = got
    half = up.shape[0] // 2
    up = up.at[:half].add(from_before)
    down = down.at[half:].add(from_after)
    return up, down


def local(acts, frozen, delta_tiles, delta_index, delta_count, cotangent):
    x, zl, core, y, zh = (lax.axis_index(a) for a in AXES)
    tokens, width = acts.shape
    per_owner, size = delta_tiles.shape[1], delta_tiles.shape[2]
    half_width = width // 2
    step = half_width // CHUNKS
    scaling = 1.0 / math.sqrt(tokens * RING * 4)
    where = jnp.stack([x, zl, core, zh, y]).astype(jnp.int32)
    own_is_b = zh == zl

    left, right = cotangent[:, :half_width], cotangent[:, half_width:]
    keep = jnp.where(core == 0, left, right)
    give = jnp.where(core == 0, right, left)

    def along_z(block):
        part_0 = lax.ppermute(block, ("zl", "zh"), [(0, 2), (1, 0), (2, 3), (3, 1)])
        part_1 = lax.ppermute(block, ("zl", "zh"), [(1, 2), (2, 1)])
        return part_0, part_1

    def parts(block, pair):
        return pair[0], jnp.where(own_is_b, block, pair[1])

    live = jnp.arange(per_owner, dtype=jnp.int32) < delta_count[0, 0]
    info = jnp.concatenate([delta_index[0], live[:, None].astype(jnp.int32)], axis=1)
    info = jnp.pad(info[:, None, :], ((0, 0), (0, EXTRA - 1), (0, size - 3)))
    mine = jnp.concatenate([delta_tiles[0] * live[:, None, None].astype(jnp.bfloat16), info.astype(jnp.bfloat16)], axis=1)

    frozen_0, frozen_1 = frozen[:, :step], frozen[:, step:]
    got_z = along_z(frozen_0)
    next_1, prev_1 = near(frozen_1, "x")
    far_1 = far(next_1, prev_1, "x")
    cot_rows = jnp.concatenate([keep, swap(give, "core")], axis=0)
    pair = jnp.concatenate([mine, swap(mine, "zh")], axis=0)
    other_pair = swap(pair, "zl")
    acts, frozen_0, got_z, pair, other_pair, cot_rows, frozen_1, next_1, far_1, prev_1 = tie(
        acts, frozen_0, got_z, pair, other_pair, cot_rows, frozen_1, next_1, far_1, prev_1
    )

    quad = jnp.concatenate([jnp.where(zl == 0, pair, other_pair), jnp.where(zl == 0, other_pair, pair)], axis=0)
    tiles = lax.all_gather(quad, ("x", "core"), axis=0, tiled=True)
    first_1 = jnp.stack([frozen_1, next_1])
    second_1 = jnp.stack([jnp.concatenate(far_1, axis=0), prev_1])
    got_first = along_z(first_1)
    acts_other = swap(acts, "zh")
    cot_next, cot_prev = near(cot_rows, "y")
    cot_far = jnp.concatenate(far(cot_next, cot_prev, "y"), axis=0)
    cot_rows, cot_next, cot_far, cot_prev, frozen_0, got_z, got_first, second_1 = tie(
        cot_rows, cot_next, cot_far, cot_prev, frozen_0, got_z, got_first, second_1
    )

    piece_0 = jnp.concatenate(parts(frozen_0, got_z), axis=0)
    next_0, prev_0 = near(piece_0, "x")
    got_second = along_z(second_1)
    swapped = swap(jnp.stack([acts, acts_other]), "core")
    cot = jnp.stack([cot_rows, cot_next, cot_far, cot_prev])
    codes = slot_codes(where, tiles[:, size, :3].astype(jnp.int32))
    slots = codes.shape[0]
    acts_all = (acts, acts_other, swapped)
    scalars = (where, codes)
    delta_back, own_grads, other_grads = slot_backward(scalars, tiles, cot, acts_all)
    next_0, prev_0, got_second, delta_back, own_grads, other_grads, cot, acts_all = tie(
        next_0, prev_0, got_second, delta_back, own_grads, other_grads, cot, acts_all
    )
    far_0 = far(next_0, prev_0, "x")
    swapped_grads = swap(other_grads, "core")
    delta_out = slot_forward(scalars, tiles, acts_all, half_width)
    delta_out, own_grads, swapped_grads, far_0, acts_all = tie(delta_out, own_grads, swapped_grads, far_0, acts_all)

    def slab(k):
        place = ((x + k) % RING) * (slots // 8)
        return lax.dynamic_slice_in_dim(own_grads, place, slots // 8, 0) + lax.dynamic_slice_in_dim(
            swapped_grads, place, slots // 8, 0
        )

    eighth = slots // 16
    blocks_0 = (piece_0, next_0, *far_0, prev_0)
    blocks_1 = (first_1, second_1, *got_first, *got_second)
    other_keep, other_give = backward(False, where, delta_back, cot, blocks_0, blocks_1)
    other_keep, other_give, delta_out, own_grads, swapped_grads = tie(
        other_keep, other_give, delta_out, own_grads, swapped_grads
    )

    other_given = swap(other_give, "core")
    far_slab = slab(2)
    other_keep, other_given, delta_out, far_slab = tie(other_keep, other_given, delta_out, far_slab)
    back_got = swap(other_keep + other_given, "zh")
    got_g = shift(far_slab[:eighth], "x", 1), shift(far_slab[eighth:], "x", -1)
    mine_out, up, far_top, far_bottom, down = forward(where, delta_out, acts_all, blocks_0, blocks_1)
    mine_out, up, far_top, far_bottom, down, cot, got_g = tie(mine_out, up, far_top, far_bottom, down, cot, got_g)

    got = shift(far_top, "y", 1), shift(far_bottom, "y", -1)
    up_g, down_g = merge(slab(1), slab(3), got_g)
    got_g = shift(up_g, "x", 1), shift(down_g, "x", -1)
    own_keep, own_give = backward(True, where, delta_back, cot, blocks_0, blocks_1)
    own_keep, own_give, got, up, down, back_got = tie(own_keep, own_give, got, up, down, back_got)

    up, down = merge(up, down, got)
    got = shift(up, "y", 1), shift(down, "y", -1)
    back_own = own_keep + swap(own_give, "core")

    grads = slab(0) + got_g[0] + got_g[1]
    grads_zl = grads.reshape(2, -1, size, size)
    grads = lax.dynamic_index_in_dim(grads_zl, zl, 0, keepdims=False) + swap(
        lax.dynamic_index_in_dim(grads_zl, 1 - zl, 0, keepdims=False), "zl"
    )
    grads = grads[:per_owner] + swap(grads[per_owner:], "zh")
    delta_grad = (grads * scaling * live[:, None, None].astype(jnp.float32))[None]

    mine_out = (mine_out + got[0] + got[1]).astype(jnp.bfloat16)
    kept, got = mine_out[:tokens], swap(mine_out[tokens:], "core")
    output = jnp.concatenate([jnp.where(core == 0, kept, got), jnp.where(core == 0, got, kept)], axis=1)
    grad_input = (back_own + back_got).astype(jnp.bfloat16)
    return output, grad_input, delta_grad


def solution(mesh):
    fine = Mesh(mesh.devices.reshape(4, 2, 2, 4, 2), AXES)
    rows, cols = ("x", "zl", "core"), ("y", "zh")
    return jax.shard_map(
        local,
        mesh=fine,
        in_specs=(
            P(rows, cols),
            P(cols, rows),
            P(cols, rows, None, None),
            P(cols, rows, None),
            P(cols, rows),
            P(rows, cols),
        ),
        out_specs=(P(rows, cols), P(rows, cols), P(cols, rows, None, None)),
        check_vma=False,
    )
```

time: 264 us -> 250 us (0.947)
  waiting for transfers between devices: 85.4 us -> 59.6 us
  other arithmetic: 29.9 us -> 36.6 us
  Pallas kernels: 57.6 us -> 62.4 us
    ppermute x20, waiting for transfers between devices: 68.1 us -> 24.5 us  [shift(): lax.ppermute(value, axis, [(i, (i + step) % RING) for i in range(RING)])]
    ppermute x2 -> x3, waiting for transfers between devices: 1.2 us -> 11.9 us  [along_z(): part_0 = lax.ppermute(block, ('zl', 'zh'), [(0, 2), (1, 0), (2, 3), (3, 1)])]
    ppermute x10 -> x12, waiting for transfers between devices: 16.1 us -> 23.2 us  [swap(): return lax.ppermute(value, axis, [(0, 1), (1, 0)])]
    ppermute x10 -> x12, starting transfers between devices: 29.6 us -> 23 us  [swap(): return lax.ppermute(value, axis, [(0, 1), (1, 0)])]
    scatter-add x0 -> x4, other arithmetic: none -> 5.09 us  [the longest x2 2.55 us: merge(): down = down.at[half:].add(from_after)]
    pallas_call x3 -> x5, Pallas kernels: 57.6 us -> 62.4 us  [call(): pl.pallas_call(kernel, out_shape=outs, in_specs=in_specs, out_specs=[pl.B...]
    ppermute x2 -> x3, starting transfers between devices: 3.82 us -> 7.35 us  [along_z(): part_0 = lax.ppermute(block, ('zl', 'zh'), [(0, 2), (1, 0), (2, 3), (3, 1)])]
    concatenate x5 -> x2, other arithmetic: 5.52 us -> 2.51 us  [the longest x1 1.64 us: local(): pair = jnp.concatenate([mine, swap(mine, 'zh')], axis=0)]
  transfers between devices with their start and end apart: 35 -> 39, of which waited for: 15 -> 9; matrix products, arithmetic and copies ran while one was open for 13% -> 16% of each run, Pallas kernels for 22% -> 21%
where the time goes in v4:
time: 250 us; the launch traced here: 248 us
  starting transfers between devices  62.9 us (25%)
  Pallas kernels  62.4 us (25%)
  waiting for transfers between devices  59.6 us (24%)
  other arithmetic  36.6 us (15%)
  between operations  15.3 us (6%)
  local copies, waits for them, and re-layouts  10.9 us (4%)
    pallas_call x5, Pallas kernels, call(): pl.pallas_call(kernel, out_shape=outs, in_specs=in_specs, out_specs=[pl.B...  62.4 us
    ppermute x20, starting transfers between devices, shift(): lax.ppermute(value, axis, [(i, (i + step) % RING) for i in range(RING)])  27.7 us
    ppermute x20, waiting for transfers between devices, shift(): lax.ppermute(value, axis, [(i, (i + step) % RING) for i in range(RING)])  24.5 us
    ppermute x12, waiting for transfers between devices, swap(): return lax.ppermute(value, axis, [(0, 1), (1, 0)])  23.2 us
    ppermute x12, starting transfers between devices, swap(): return lax.ppermute(value, axis, [(0, 1), (1, 0)])  23 us
    ppermute x3, waiting for transfers between devices, along_z(): part_0 = lax.ppermute(block, ('zl', 'zh'), [(0, 2), (1, 0), (2, 3), (3, 1)])  11.9 us
    ppermute x3, starting transfers between devices, along_z(): part_0 = lax.ppermute(block, ('zl', 'zh'), [(0, 2), (1, 0), (2, 3), (3, 1)])  7.35 us
  transfers between devices with their start and end apart: 39, of which 9 were waited for; matrix products, arithmetic and copies ran while one was open for 16% of the time, Pallas kernels for 21%

profile of v4, /device:TPU:1, one launch (start us, length us, event | category | flops | bytes accessed | tf_op | source)
XLA Modules:
  0.0 247.8 jit_solution(15544527856951272877)
XLA Ops:
  13.7 3.7 %collective-permute-start.2 = (bf16[4,144,128]{2,1,0:T(8,128)(2,1)}, bf16[4,144,128]{2,1,0:T(8,128)(2,1)}, u32[]{:S(2)}, u32[]{:S(2)}) collective-permute-start(bf16[4,144,128]{2,1,0:T(8,128)(2,1)} %pad_maximum_fusion.10), channel_id=1, source_target_pairs={{0,1},{1,0},{2,3},{3,2},{4,5},{5,4},{6,7},{7,6},{8,9},{9,8},{10,11... | collective-permute-start | bytes 442376 | tf_op jit(solution)/shard_map/ppermute | solution.py:24
  23.7 2.9 %collective-permute-start.3 = (bf16[8,144,128]{2,1,0:T(8,128)(2,1)}, bf16[8,144,128]{2,1,0:T(8,128)(2,1)}, u32[]{:S(2)}, u32[]{:S(2)}) collective-permute-start(bf16[8,144,128]{2,1,0:T(8,128)(2,1)} %pad_maximum_fusion.9), channel_id=1, source_target_pairs={{0,16},{16,0},{1,17},{17,1},{2,18},{18,2},{3,19},{19,3},{4,20},{20... | collective-permute-start | bytes 884744 | tf_op jit(solution)/shard_map/ppermute | solution.py:24
  30.3 8.7 %collective-permute-done.3 = bf16[8,144,128]{2,1,0:T(8,128)(2,1)} collective-permute-done((bf16[8,144,128]{2,1,0:T(8,128)(2,1)}, bf16[8,144,128]{2,1,0:T(8,128)(2,1)}, u32[]{:S(2)}, u32[]{:S(2)}) %collective-permute-start.3) | collective-permute-done | bytes 294944 | tf_op jit(solution)/shard_map/ppermute | solution.py:24
  50.0 10.3 %collective-permute-done.10 = bf16[768,512]{1,0:T(8,128)(2,1)} collective-permute-done((bf16[768,512]{1,0:T(8,128)(2,1)S(1)}, bf16[768,512]{1,0:T(8,128)(2,1)}, u32[]{:S(2)}, u32[]{:S(2)}) %collective-permute-start.10) | collective-permute-done | bytes 786464 | tf_op jit(solution)/shard_map/ppermute | solution.py:20
  62.4 2.8 %collective-permute-start.12 = (bf16[384,512]{1,0:T(8,128)(2,1)S(1)}, bf16[384,512]{1,0:T(8,128)(2,1)S(1)}, u32[]{:S(2)}, u32[]{:S(2)}) collective-permute-start(bf16[384,512]{1,0:T(8,128)(2,1)S(1)} %slice.173), channel_id=1, source_target_pairs={{0,6},{2,0},{4,2},{6,4},{1,7},{3,1},{5,3},{7,5},{8,14},{10,8},{12,... | collective-permute-start | bytes 1179656 | tf_op jit(solution)/shard_map/ppermute | solution.py:20
  66.4 2.9 %pad_maximum_fusion.1 = bf16[2,384,1024]{2,1,0:T(8,128)(2,1)} fusion(bf16[1,384,1024]{2,1,0:T(8,128)(2,1)} %bitcast.25, bf16[1,384,1024]{2,1,0:T(8,128)(2,1)S(1)} %bitcast.53), kind=kLoop, calls=%fused_computation.1 | loop fusion | flops 786432 | bytes 3145728 | tf_op jit(solution)/shard_map/stack | solution.py:441
  69.2 3.3 %collective-permute-start.20 = (bf16[2,384,1024]{2,1,0:T(8,128)(2,1)}, bf16[2,384,1024]{2,1,0:T(8,128)(2,1)}, u32[]{:S(2)}, u32[]{:S(2)}) collective-permute-start(bf16[2,384,1024]{2,1,0:T(8,128)(2,1)} %pad_maximum_fusion.1), channel_id=1, source_target_pairs={{0,8},{8,0},{1,9},{9,1},{2,10},{10,2},{3,11},{11,3},{4,12},{12,4},... | collective-permute-start | bytes 4718600 | tf_op jit(solution)/shard_map/ppermute | solution.py:24
  73.5 11.9 %collective-permute-done.13.refs_7_.refs_10_ = bf16[2,1024,256]{2,1,0:T(8,128)(2,1)} collective-permute-done((bf16[2,1024,256]{2,1,0:T(8,128)(2,1)S(1)}, bf16[2,1024,256]{2,1,0:T(8,128)(2,1)}, u32[]{:S(2)}, u32[]{:S(2)}) %collective-permute-start.13) | collective-permute-done | bytes 1048608 | tf_op jit(solution)/shard_map/ppermute | solution.py:403
  88.1 4.9 %collective-permute-start.17 = (bf16[2,1024,256]{2,1,0:T(8,128)(2,1)S(1)}, bf16[2,1024,256]{2,1,0:T(8,128)(2,1)}, u32[]{:S(2)}, u32[]{:S(2)}) collective-permute-start(bf16[2,1024,256]{2,1,0:T(8,128)(2,1)S(1)} %pad_maximum_fusion.3.refs_6_.refs_9_), channel_id=1, source_target_pairs={{0,16},{1,0},{16,17},{17,1},{2,18},{3,2},{18,19},{19,3},{4,20},{5,... | collective-permute-start | bytes 3145736 | tf_op jit(solution)/shard_map/ppermute | solution.py:403
  95.4 3.2 %pad_maximum_fusion.cot_ref = bf16[4,768,512]{2,1,0:T(8,128)(2,1)} fusion(bf16[1,768,512]{2,1,0:T(8,128)(2,1)} %bitcast.23, bf16[1,768,512]{2,1,0:T(8,128)(2,1)} %bitcast.57, bf16[1,768,512]{2,1,0:T(8,128)(2,1)} %bitcast.21, bf16[1,768,512]{2,1,0:T(8,128)(2,1)} %bitcast.56), kind=kLoop, calls=%fused_computation | loop fusion | flops 4718592 | bytes 6291456 | tf_op jit(solution)/shard_map/stack | solution.py:442
  100.2 17.6 %shard_map.85 = (f32[2,768,1024]{2,1,0:T(8,128)}, f32[64,128,128]{2,1,0:T(8,128)}, f32[64,128,128]{2,1,0:T(8,128)}) custom-call(s32[5]{0:T(128)} %stack.65.where_ref, s32[128]{0:T(128)} %bitcast_select_fusion.codes_ref, bf16[128,144,128]{2,1,0:T(8,128)(2,1)} %all-gather.2.cloned.1.call-done.tiles_ref, bf16[4,768,512]{2,1,0:T(8,128)(2,1)} %pad_maximum_fusion.cot_ref, ...), custom_call_target="tpu_custom_call" | custom-call | flops 3221225 | bytes 25165 | tf_op jit(solution)/shard_map/pallas_call | solution.py:290
  119.4 2.9 %collective-permute-start.23 = (bf16[1024,256]{1,0:T(8,128)(2,1)S(1)}, bf16[1024,256]{1,0:T(8,128)(2,1)S(1)}, u32[]{:S(2)}, u32[]{:S(2)}) collective-permute-start(bf16[1024,256]{1,0:T(8,128)(2,1)S(1)} %slice.159), channel_id=1, source_target_pairs={{0,96},{32,0},{64,32},{96,64},{1,97},{33,1},{65,33},{97,65},{2,98}... | collective-permute-start | bytes 1572872 | tf_op jit(solution)/shard_map/ppermute | solution.py:20
  122.3 12.7 %shard_map.86.delta_ref = f32[4,768,512]{2,1,0:T(8,128)} custom-call(s32[5]{0:T(128)} %stack.65.where_ref, s32[128]{0:T(128)} %bitcast_select_fusion.codes_ref, bf16[128,144,128]{2,1,0:T(8,128)(2,1)} %all-gather.2.cloned.1.call-done.tiles_ref, bf16[384,1024]{1,0:T(8,128)(2,1)} %refs_0_.2, bf16[384,1024]{1,0:T(8,128)(2,1)} %collective-permute-done.19.refs_1_, ...), custom_call_target="tpu_custom_call" | custom-call | flops 1610612 | bytes 16777 | tf_op jit(solution)/shard_map/pallas_call | solution.py:290
  136.1 9.4 %shard_map.87 = (f32[384,1024]{1,0:T(8,128)}, f32[384,1024]{1,0:T(8,128)}) custom-call(s32[5]{0:T(128)} %stack.65.where_ref, f32[2,768,1024]{2,1,0:T(8,128)} %get-tuple-element.151.delta_ref, bf16[4,768,512]{2,1,0:T(8,128)(2,1)} %pad_maximum_fusion.cot_ref, bf16[2048,256]{1,0:T(8,128)(2,1)} %copy-done.2, bf16[2048,256]{1,0:T(8,128)(2,1)} %copy-done.3, ...), custom_call_target="tpu_custom_call" | custom-call | flops 3221225 | bytes 16777 | tf_op jit(solution)/shard_map/pallas_call | solution.py:290
  145.7 3.5 %dynamic-slice_add_fusion.1 = (f32[16,128,128]{2,1,0:T(8,128)S(1)}, f32[16,128,128]{2,1,0:T(8,128)S(1)}, f32[16,128,128]{2,1,0:T(8,128)S(1)}) fusion(f32[64,128,128]{2,1,0:T(8,128)} %collective-permute-done.21, s32[]{:T(128)S(6)} %select_n.102, f32[64,128,128]{2,1,0:T(8,128)} %get-tuple-element.174, s32[]{:T(128)S(6)} %select_n.104, s32[]{:T(128)S(6)} %select_n.96), kind=kLoop, calls=%fused_computation.9 | loop fusion | flops 786432 | bytes 9437196 | tf_op jit(solution)/shard_map/add | solution.py:458
  149.4 2.9 %add.124 = f32[384,1024]{1,0:T(8,128)} add(f32[384,1024]{1,0:T(8,128)S(1)} %copy-done.11, f32[384,1024]{1,0:T(8,128)} %collective-permute-done.24) | non-fusion elementwise | flops 393216 | bytes 4718592 | tf_op jit(solution)/shard_map/add | solution.py:473
  158.2 13.1 %shard_map.88 = (f32[768,512]{1,0:T(8,128)}, f32[768,512]{1,0:T(8,128)}, f32[384,512]{1,0:T(8,128)}, f32[384,512]{1,0:T(8,128)}, f32[768,512]{1,0:T(8,128)}) custom-call(s32[5]{0:T(128)} %stack.65.where_ref, f32[4,768,512]{2,1,0:T(8,128)} %shard_map.86.delta_ref, bf16[384,1024]{1,0:T(8,128)(2,1)} %refs_0_.2, ...), custom_call_target="tpu_custom_call" | custom-call | flops 6442450 | bytes 25165 | tf_op jit(solution)/shard_map/pallas_call | solution.py:290
  174.5 2.9 %collective-permute-start.35 = (f32[16,128,128]{2,1,0:T(8,128)S(1)}, f32[16,128,128]{2,1,0:T(8,128)}, u32[]{:S(2)}, u32[]{:S(2)}) collective-permute-start(f32[16,128,128]{2,1,0:T(8,128)S(1)} %fusion), channel_id=1, source_target_pairs={{0,96},{32,0},{64,32},{96,64},{1,97},{33,1},{65,33},{97,65},{2,98}... | collective-permute-start | bytes 3145736 | tf_op jit(solution)/shard_map/ppermute | solution.py:20
  177.4 9.5 %shard_map.89 = (f32[384,1024]{1,0:T(8,128)}, f32[384,1024]{1,0:T(8,128)}) custom-call(s32[5]{0:T(128)} %stack.65.where_ref, f32[2,768,1024]{2,1,0:T(8,128)} %get-tuple-element.151.delta_ref, bf16[4,768,512]{2,1,0:T(8,128)(2,1)} %pad_maximum_fusion.cot_ref, bf16[2048,256]{1,0:T(8,128)(2,1)} %copy-done.2, bf16[2048,256]{1,0:T(8,128)(2,1)} %copy-done.3, ...), custom_call_target="tpu_custom_call" | custom-call | flops 3221225 | bytes 16777 | tf_op jit(solution)/shard_map/pallas_call | solution.py:290
  186.9 4.1 %collective-permute-done.27 = f32[384,512]{1,0:T(8,128)} collective-permute-done((f32[384,512]{1,0:T(8,128)}, f32[384,512]{1,0:T(8,128)}, u32[]{:S(2)}, u32[]{:S(2)}) %collective-permute-start.27) | collective-permute-done | bytes 786464 | tf_op jit(solution)/shard_map/ppermute | solution.py:20
  204.3 13.5 %collective-permute-done.36 = f32[8,128,128]{2,1,0:T(8,128)S(1)} collective-permute-done((f32[8,128,128]{2,1,0:T(8,128)}, f32[8,128,128]{2,1,0:T(8,128)S(1)}, u32[]{:S(2)}, u32[]{:S(2)}) %collective-permute-start.36) | collective-permute-done | bytes 524320 | tf_op jit(solution)/shard_map/ppermute | solution.py:24
  220.3 8.7 %collective-permute-done.30 = f32[768,512]{1,0:T(8,128)} collective-permute-done((f32[768,512]{1,0:T(8,128)}, f32[768,512]{1,0:T(8,128)}, u32[]{:S(2)}, u32[]{:S(2)}) %collective-permute-start.30) | collective-permute-done | bytes 1572896 | tf_op jit(solution)/shard_map/ppermute | solution.py:20
  232.7 3.2 %collective-permute-start.32 = (bf16[384,512]{1,0:T(8,128)(2,1)S(1)}, bf16[384,512]{1,0:T(8,128)(2,1)S(1)}, u32[]{:S(2)}, u32[]{:S(2)}) collective-permute-start(bf16[384,512]{1,0:T(8,128)(2,1)S(1)} %slice.176), channel_id=1, source_target_pairs={{0,8},{8,0},{1,9},{9,1},{2,10},{10,2},{3,11},{11,3},{4,12},{12,4},... | collective-permute-start | bytes 1179656 | tf_op jit(solution)/shard_map/ppermute | solution.py:24
  236.7 3.1 %add_convert_fusion = bf16[384,1024]{1,0:T(8,128)(2,1)} fusion(f32[384,1024]{1,0:T(8,128)} %collective-permute-done.29, f32[384,1024]{1,0:T(8,128)S(1)} %copy-done.10, f32[384,1024]{1,0:T(8,128)} %collective-permute-done.33), kind=kLoop, calls=%fused_computation.2 | loop fusion | flops 1179648 | bytes 5505024 | tf_op jit(solution)/shard_map/convert_element_type | solution.py:499
  (152 shorter events, 70.7 us)
Async XLA Ops:
  7.2 91.4 %all-gather.2.cloned.1.call-start = ((), (), s32[]{:S(2)}) async-start(), calls=%async_computation | async-start | bytes 5308416 | tf_op jit(solution)/shard_map/all_gather | solution.py:427
  10.7 16.6 %collective-permute-start.5 = (bf16[1024,256]{1,0:T(8,128)(2,1)S(1)}, bf16[1024,256]{1,0:T(8,128)(2,1)S(1)}, u32[]{:S(2)}, u32[]{:S(2)}) collective-permute-start(bf16[1024,256]{1,0:T(8,128)(2,1)S(1)} %get-tuple-element.132), channel_id=1, source_target_pairs={{0,96},{32,0},{64,32},{96,64},{1,97},{33,1},{65,33},{97,65},{2,98}... | collective-permute-start | bytes 1572872 | tf_op jit(solution)/shard_map/ppermute | solution.py:20
  19.0 19.9 %collective-permute-start = (bf16[1024,256]{1,0:T(8,128)(2,1)S(1)}, bf16[1024,256]{1,0:T(8,128)(2,1)}, u32[]{:S(2)}, u32[]{:S(2)}) collective-permute-start(bf16[1024,256]{1,0:T(8,128)(2,1)S(1)} %get-tuple-element.138), channel_id=1, source_target_pairs={{0,16},{1,0},{16,17},{17,1},{2,18},{3,2},{18,19},{19,3},{4,20},{5,... | collective-permute-start | bytes 1572872 | tf_op jit(solution)/shard_map/ppermute | solution.py:403
  20.6 18.3 %collective-permute-start.1 = (bf16[1024,256]{1,0:T(8,128)(2,1)S(1)}, bf16[1024,256]{1,0:T(8,128)(2,1)}, u32[]{:S(2)}, u32[]{:S(2)}) collective-permute-start(bf16[1024,256]{1,0:T(8,128)(2,1)S(1)} %get-tuple-element.138), channel_id=1, source_target_pairs={{1,16},{16,1},{3,18},{18,3},{5,20},{20,5},{7,22},{22,7},{9,24},{24... | collective-permute-start | bytes 1572872 | tf_op jit(solution)/shard_map/ppermute | solution.py:404
  41.7 18.6 %collective-permute-start.10 = (bf16[768,512]{1,0:T(8,128)(2,1)S(1)}, bf16[768,512]{1,0:T(8,128)(2,1)}, u32[]{:S(2)}, u32[]{:S(2)}) collective-permute-start(bf16[768,512]{1,0:T(8,128)(2,1)S(1)} %pad_maximum_fusion.5), channel_id=1, source_target_pairs={{0,2},{2,4},{4,6},{6,0},{1,3},{3,5},{5,7},{7,1},{8,10},{10,12},{12... | collective-permute-start | bytes 2359304 | tf_op jit(solution)/shard_map/ppermute | solution.py:20
  43.0 18.4 %collective-permute-start.9 = (bf16[768,512]{1,0:T(8,128)(2,1)S(1)}, bf16[768,512]{1,0:T(8,128)(2,1)}, u32[]{:S(2)}, u32[]{:S(2)}) collective-permute-start(bf16[768,512]{1,0:T(8,128)(2,1)S(1)} %pad_maximum_fusion.5), channel_id=1, source_target_pairs={{0,6},{2,0},{4,2},{6,4},{1,7},{3,1},{5,3},{7,5},{8,14},{10,8},{12,... | collective-permute-start | bytes 2359304 | tf_op jit(solution)/shard_map/ppermute | solution.py:20
  44.6 21.8 %collective-permute-start.19 = (bf16[384,1024]{1,0:T(8,128)(2,1)S(1)}, bf16[384,1024]{1,0:T(8,128)(2,1)}, u32[]{:S(2)}, u32[]{:S(2)}) collective-permute-start(bf16[384,1024]{1,0:T(8,128)(2,1)S(1)} %copy-done.4), channel_id=1, source_target_pairs={{0,1},{1,0},{2,3},{3,2},{4,5},{5,4},{6,7},{7,6},{8,9},{9,8},{10,11... | collective-permute-start | bytes 2359304 | tf_op jit(solution)/shard_map/ppermute | solution.py:24
  46.7 38.6 %collective-permute-start.13 = (bf16[2,1024,256]{2,1,0:T(8,128)(2,1)S(1)}, bf16[2,1024,256]{2,1,0:T(8,128)(2,1)}, u32[]{:S(2)}, u32[]{:S(2)}) collective-permute-start(bf16[2,1024,256]{2,1,0:T(8,128)(2,1)S(1)} %pad_maximum_fusion.2.refs_5_.refs_8_), channel_id=1, source_target_pairs={{0,16},{1,0},{16,17},{17,1},{2,18},{3,2},{18,19},{19,3},{4,20},{5,... | collective-permute-start | bytes 3145736 | tf_op jit(solution)/shard_map/ppermute | solution.py:403
  48.4 37.0 %collective-permute-start.14 = (bf16[2,1024,256]{2,1,0:T(8,128)(2,1)S(1)}, bf16[2,1024,256]{2,1,0:T(8,128)(2,1)}, u32[]{:S(2)}, u32[]{:S(2)}) collective-permute-start(bf16[2,1024,256]{2,1,0:T(8,128)(2,1)S(1)} %pad_maximum_fusion.2.refs_5_.refs_8_), channel_id=1, source_target_pairs={{1,16},{16,1},{3,18},{18,3},{5,20},{20,5},{7,22},{22,7},{9,24},{24... | collective-permute-start | bytes 3145736 | tf_op jit(solution)/shard_map/ppermute | solution.py:404
  69.2 31.0 %collective-permute-start.20 = (bf16[2,384,1024]{2,1,0:T(8,128)(2,1)}, bf16[2,384,1024]{2,1,0:T(8,128)(2,1)}, u32[]{:S(2)}, u32[]{:S(2)}) collective-permute-start(bf16[2,384,1024]{2,1,0:T(8,128)(2,1)} %pad_maximum_fusion.1), channel_id=1, source_target_pairs={{0,8},{8,0},{1,9},{9,1},{2,10},{10,2},{3,11},{11,3},{4,12},{12,4},... | collective-permute-start | bytes 4718600 | tf_op jit(solution)/shard_map/ppermute | solution.py:24
  86.5 31.3 %collective-permute-start.15 = (bf16[2048,256]{1,0:T(8,128)(2,1)S(1)}, bf16[2048,256]{1,0:T(8,128)(2,1)S(1)}, u32[]{:S(2)}, u32[]{:S(2)}) collective-permute-start(bf16[2048,256]{1,0:T(8,128)(2,1)S(1)} %pad_maximum_fusion.4.refs_0_.refs_3_), channel_id=1, source_target_pairs={{0,96},{32,0},{64,32},{96,64},{1,97},{33,1},{65,33},{97,65},{2,98}... | collective-permute-start | bytes 3145736 | tf_op jit(solution)/shard_map/ppermute | solution.py:20
  87.9 30.0 %collective-permute-start.16 = (bf16[2048,256]{1,0:T(8,128)(2,1)S(1)}, bf16[2048,256]{1,0:T(8,128)(2,1)}, u32[]{:S(2)}, u32[]{:S(2)}) collective-permute-start(bf16[2048,256]{1,0:T(8,128)(2,1)S(1)} %pad_maximum_fusion.4.refs_0_.refs_3_), channel_id=1, source_target_pairs={{0,32},{32,64},{64,96},{96,0},{1,33},{33,65},{65,97},{97,1},{2,34}... | collective-permute-start | bytes 3145736 | tf_op jit(solution)/shard_map/ppermute | solution.py:20
  88.1 29.8 %collective-permute-start.17 = (bf16[2,1024,256]{2,1,0:T(8,128)(2,1)S(1)}, bf16[2,1024,256]{2,1,0:T(8,128)(2,1)}, u32[]{:S(2)}, u32[]{:S(2)}) collective-permute-start(bf16[2,1024,256]{2,1,0:T(8,128)(2,1)S(1)} %pad_maximum_fusion.3.refs_6_.refs_9_), channel_id=1, source_target_pairs={{0,16},{1,0},{16,17},{17,1},{2,18},{3,2},{18,19},{19,3},{4,20},{5,... | collective-permute-start | bytes 3145736 | tf_op jit(solution)/shard_map/ppermute | solution.py:403
  93.0 24.9 %collective-permute-start.18 = (bf16[2,1024,256]{2,1,0:T(8,128)(2,1)S(1)}, bf16[2,1024,256]{2,1,0:T(8,128)(2,1)}, u32[]{:S(2)}, u32[]{:S(2)}) collective-permute-start(bf16[2,1024,256]{2,1,0:T(8,128)(2,1)S(1)} %pad_maximum_fusion.3.refs_6_.refs_9_), channel_id=1, source_target_pairs={{1,16},{16,1},{3,18},{18,3},{5,20},{20,5},{7,22},{22,7},{9,24},{24... | collective-permute-start | bytes 3145736 | tf_op jit(solution)/shard_map/ppermute | solution.py:404
  117.9 17.3 %collective-permute-start.21 = (f32[64,128,128]{2,1,0:T(8,128)}, f32[64,128,128]{2,1,0:T(8,128)}, u32[]{:S(2)}, u32[]{:S(2)}) collective-permute-start(f32[64,128,128]{2,1,0:T(8,128)} %get-tuple-element.158), channel_id=1, source_target_pairs={{0,8},{8,0},{1,9},{9,1},{2,10},{10,2},{3,11},{11,3},{4,12},{12,4},... | collective-permute-start | bytes 12582920 | tf_op jit(solution)/shard_map/ppermute | solution.py:24
  152.3 38.7 %collective-permute-start.29 = (f32[384,1024]{1,0:T(8,128)}, f32[384,1024]{1,0:T(8,128)}, u32[]{:S(2)}, u32[]{:S(2)}) collective-permute-start(f32[384,1024]{1,0:T(8,128)} %add.124), channel_id=1, source_target_pairs={{0,1},{1,0},{2,3},{3,2},{4,5},{5,4},{6,7},{7,6},{8,9},{9,8},{10,11... | collective-permute-start | bytes 4718600 | tf_op jit(solution)/shard_map/ppermute | solution.py:24
  171.4 19.6 %collective-permute-start.27 = (f32[384,512]{1,0:T(8,128)}, f32[384,512]{1,0:T(8,128)}, u32[]{:S(2)}, u32[]{:S(2)}) collective-permute-start(f32[384,512]{1,0:T(8,128)} %get-tuple-element.190), channel_id=1, source_target_pairs={{0,2},{2,4},{4,6},{6,0},{1,3},{3,5},{5,7},{7,1},{8,10},{10,12},{12... | collective-permute-start | bytes 2359304 | tf_op jit(solution)/shard_map/ppermute | solution.py:20
  171.5 19.6 %collective-permute-start.28 = (f32[384,512]{1,0:T(8,128)}, f32[384,512]{1,0:T(8,128)}, u32[]{:S(2)}, u32[]{:S(2)}) collective-permute-start(f32[384,512]{1,0:T(8,128)} %get-tuple-element.191), channel_id=1, source_target_pairs={{0,6},{2,0},{4,2},{6,4},{1,7},{3,1},{5,3},{7,5},{8,14},{10,8},{12,... | collective-permute-start | bytes 2359304 | tf_op jit(solution)/shard_map/ppermute | solution.py:20
  174.3 26.8 %collective-permute-start.34 = (f32[16,128,128]{2,1,0:T(8,128)S(1)}, f32[16,128,128]{2,1,0:T(8,128)S(1)}, u32[]{:S(2)}, u32[]{:S(2)}) collective-permute-start(f32[16,128,128]{2,1,0:T(8,128)S(1)} %fusion.1), channel_id=1, source_target_pairs={{0,32},{32,64},{64,96},{96,0},{1,33},{33,65},{65,97},{97,1},{2,34}... | collective-permute-start | bytes 3145736 | tf_op jit(solution)/shard_map/ppermute | solution.py:20
  174.5 26.6 %collective-permute-start.35 = (f32[16,128,128]{2,1,0:T(8,128)S(1)}, f32[16,128,128]{2,1,0:T(8,128)}, u32[]{:S(2)}, u32[]{:S(2)}) collective-permute-start(f32[16,128,128]{2,1,0:T(8,128)S(1)} %fusion), channel_id=1, source_target_pairs={{0,96},{32,0},{64,32},{96,64},{1,97},{33,1},{65,33},{97,65},{2,98}... | collective-permute-start | bytes 3145736 | tf_op jit(solution)/shard_map/ppermute | solution.py:20
  193.4 35.5 %collective-permute-start.30 = (f32[768,512]{1,0:T(8,128)}, f32[768,512]{1,0:T(8,128)}, u32[]{:S(2)}, u32[]{:S(2)}) collective-permute-start(f32[768,512]{1,0:T(8,128)} %add_dynamic-update-slice_fusion.1), channel_id=1, source_target_pairs={{0,2},{2,4},{4,6},{6,0},{1,3},{3,5},{5,7},{7,1},{8,10},{10,12},{12... | collective-permute-start | bytes 4718600 | tf_op jit(solution)/shard_map/ppermute | solution.py:20
  195.9 34.5 %collective-permute-start.31 = (f32[768,512]{1,0:T(8,128)}, f32[768,512]{1,0:T(8,128)}, u32[]{:S(2)}, u32[]{:S(2)}) collective-permute-start(f32[768,512]{1,0:T(8,128)} %add_dynamic-update-slice_fusion), channel_id=1, source_target_pairs={{0,6},{2,0},{4,2},{6,4},{1,7},{3,1},{5,3},{7,5},{8,14},{10,8},{12,... | collective-permute-start | bytes 4718600 | tf_op jit(solution)/shard_map/ppermute | solution.py:20
  198.5 38.2 %collective-permute-start.33 = (f32[384,1024]{1,0:T(8,128)}, f32[384,1024]{1,0:T(8,128)}, u32[]{:S(2)}, u32[]{:S(2)}) collective-permute-start(f32[384,1024]{1,0:T(8,128)} %get-tuple-element.201), channel_id=1, source_target_pairs={{0,8},{8,0},{1,9},{9,1},{2,10},{10,2},{3,11},{11,3},{4,12},{12,4},... | collective-permute-start | bytes 4718600 | tf_op jit(solution)/shard_map/ppermute | solution.py:24
  217.9 18.0 %collective-permute-start.37 = (f32[4,128,128]{2,1,0:T(8,128)S(1)}, f32[4,128,128]{2,1,0:T(8,128)S(1)}, u32[]{:S(2)}, u32[]{:S(2)}) collective-permute-start(f32[4,128,128]{2,1,0:T(8,128)S(1)} %slice.180), channel_id=1, source_target_pairs={{0,1},{1,0},{2,3},{3,2},{4,5},{5,4},{6,7},{7,6},{8,9},{9,8},{10,11... | collective-permute-start | bytes 786440 | tf_op jit(solution)/shard_map/ppermute | solution.py:24
  (35 other events, 409.3 us)
Sparse Core Ops, SparseCore 0:
  41.8 34.2 all-gather.1

commit v5 on v4

--- a/solution.py
+++ b/solution.py
@@ -85,9 +85,11 @@
     copies = []
     for ring in range(RING):
         target = target_of(ring)
-        if len(refs) == 6:
+        if len(refs) == 9:
+            piece = (0, 1, 1, 2)[ring]
             sent, got = (
-                ref.at[ring % 2, pl.ds(first, length)] for ref in (refs[ring // 2], refs[2 + ring // 2 * 2 + part])
+                (ref.at[ring - 1] if piece == 1 else ref).at[pl.ds(first, length)]
+                for ref in (refs[piece], refs[3 + 2 * piece + part])
             )
             copies.append((got, target, same, sent) if part == 1 else (got, target))
         elif ring == 2:
@@ -192,7 +194,7 @@
 
 
 def forward_kernel(where_ref, delta_ref, *refs):
-    acts_refs, blocks_0, blocks_1, rest = refs[:3], refs[3:8], refs[8:14], refs[14:]
+    acts_refs, blocks_0, blocks_1, rest = refs[:3], refs[3:8], refs[8:17], refs[17:]
     (mine_ref, up_ref, far_top_ref, far_bottom_ref, down_ref), (acts, blocks, sums, sems, out_sems) = rest[:5], rest[5:]
     x, y = where_ref[0], where_ref[4]
     step = sums.shape[2] // CHUNKS
@@ -227,7 +229,7 @@
 
 
 def backward_kernel(own, where_ref, delta_ref, cot_ref, *refs):
-    blocks_0, blocks_1, rest = refs[:5], refs[5:11], refs[11:]
+    blocks_0, blocks_1, rest = refs[:5], refs[5:14], refs[14:]
     (keep_ref, give_ref), (cot, blocks, sums, sems, out_sems) = rest[:2], rest[2:]
     x, zl, zh, y = where_ref[0], where_ref[1], where_ref[3], where_ref[4]
     mine = 1 - zh ^ zl if own else zh ^ zl
@@ -425,19 +427,18 @@
 
     quad = jnp.concatenate([jnp.where(zl == 0, pair, other_pair), jnp.where(zl == 0, other_pair, pair)], axis=0)
     tiles = lax.all_gather(quad, ("x", "core"), axis=0, tiled=True)
-    first_1 = jnp.stack([frozen_1, next_1])
-    second_1 = jnp.stack([jnp.concatenate(far_1, axis=0), prev_1])
-    got_first = along_z(first_1)
+    rest_1 = jnp.stack([next_1, jnp.concatenate(far_1, axis=0)])
+    got_first = along_z(frozen_1)
     acts_other = swap(acts, "zh")
     cot_next, cot_prev = near(cot_rows, "y")
     cot_far = jnp.concatenate(far(cot_next, cot_prev, "y"), axis=0)
-    cot_rows, cot_next, cot_far, cot_prev, frozen_0, got_z, got_first, second_1 = tie(
-        cot_rows, cot_next, cot_far, cot_prev, frozen_0, got_z, got_first, second_1
+    cot_rows, cot_next, cot_far, cot_prev, frozen_0, got_z, got_first, rest_1 = tie(
+        cot_rows, cot_next, cot_far, cot_prev, frozen_0, got_z, got_first, rest_1
     )
 
     piece_0 = jnp.concatenate(parts(frozen_0, got_z), axis=0)
     next_0, prev_0 = near(piece_0, "x")
-    got_second = along_z(second_1)
+    got_rest = along_z(rest_1)
     swapped = swap(jnp.stack([acts, acts_other]), "core")
     cot = jnp.stack([cot_rows, cot_next, cot_far, cot_prev])
     codes = slot_codes(where, tiles[:, size, :3].astype(jnp.int32))
@@ -445,13 +446,16 @@
     acts_all = (acts, acts_other, swapped)
     scalars = (where, codes)
     delta_back, own_grads, other_grads = slot_backward(scalars, tiles, cot, acts_all)
-    next_0, prev_0, got_second, delta_back, own_grads, other_grads, cot, acts_all = tie(
-        next_0, prev_0, got_second, delta_back, own_grads, other_grads, cot, acts_all
+    next_0, prev_0, got_rest, prev_1, delta_back, own_grads, other_grads, cot, acts_all = tie(
+        next_0, prev_0, got_rest, prev_1, delta_back, own_grads, other_grads, cot, acts_all
     )
     far_0 = far(next_0, prev_0, "x")
+    got_last = along_z(prev_1)
     swapped_grads = swap(other_grads, "core")
     delta_out = slot_forward(scalars, tiles, acts_all, half_width)
-    delta_out, own_grads, swapped_grads, far_0, acts_all = tie(delta_out, own_grads, swapped_grads, far_0, acts_all)
+    delta_out, own_grads, swapped_grads, far_0, got_last, acts_all = tie(
+        delta_out, own_grads, swapped_grads, far_0, got_last, acts_all
+    )
 
     def slab(k):
         place = ((x + k) % RING) * (slots // 8)
@@ -461,42 +465,42 @@
 
     eighth = slots // 16
     blocks_0 = (piece_0, next_0, *far_0, prev_0)
-    blocks_1 = (first_1, second_1, *got_first, *got_second)
+    blocks_1 = (frozen_1, rest_1, prev_1, *got_first, *got_rest, *got_last)
+    far_slab = slab(2)
+    got_g = shift(far_slab[:eighth], "x", 1), shift(far_slab[eighth:], "x", -1)
     other_keep, other_give = backward(False, where, delta_back, cot, blocks_0, blocks_1)
-    other_keep, other_give, delta_out, own_grads, swapped_grads = tie(
-        other_keep, other_give, delta_out, own_grads, swapped_grads
-    )
-
+    other_keep, other_give, delta_out = tie(other_keep, other_give, delta_out)
     other_given = swap(other_give, "core")
-    far_slab = slab(2)
-    other_keep, other_given, delta_out, far_slab = tie(other_keep, other_given, delta_out, far_slab)
-    back_got = swap(other_keep + other_given, "zh")
-    got_g = shift(far_slab[:eighth], "x", 1), shift(far_slab[eighth:], "x", -1)
     mine_out, up, far_top, far_bottom, down = forward(where, delta_out, acts_all, blocks_0, blocks_1)
-    mine_out, up, far_top, far_bottom, down, cot, got_g = tie(mine_out, up, far_top, far_bottom, down, cot, got_g)
+    mine_out, up, far_top, far_bottom, down, got_g, other_keep, other_given = tie(
+        mine_out, up, far_top, far_bottom, down, got_g, other_keep, other_given
+    )
 
     got = shift(far_top, "y", 1), shift(far_bottom, "y", -1)
     up_g, down_g = merge(slab(1), slab(3), got_g)
     got_g = shift(up_g, "x", 1), shift(down_g, "x", -1)
+    back_got = swap(other_keep + other_given, "zh")
     own_keep, own_give = backward(True, where, delta_back, cot, blocks_0, blocks_1)
-    own_keep, own_give, got, up, down, back_got = tie(own_keep, own_give, got, up, down, back_got)
+    got, up, down, own_keep, own_give = tie(got, up, down, own_keep, own_give)
 
     up, down = merge(up, down, got)
     got = shift(up, "y", 1), shift(down, "y", -1)
     back_own = own_keep + swap(own_give, "core")
 
     grads = slab(0) + got_g[0] + got_g[1]
+    grads, back_got = tie(grads, back_got)
     grads_zl = grads.reshape(2, -1, size, size)
     grads = lax.dynamic_index_in_dim(grads_zl, zl, 0, keepdims=False) + swap(
         lax.dynamic_index_in_dim(grads_zl, 1 - zl, 0, keepdims=False), "zl"
     )
+    grad_input = (back_own + back_got).astype(jnp.bfloat16)
+    grads, grad_input = tie(grads, grad_input)
     grads = grads[:per_owner] + swap(grads[per_owner:], "zh")
     delta_grad = (grads * scaling * live[:, None, None].astype(jnp.float32))[None]
 
     mine_out = (mine_out + got[0] + got[1]).astype(jnp.bfloat16)
     kept, got = mine_out[:tokens], swap(mine_out[tokens:], "core")
     output = jnp.concatenate([jnp.where(core == 0, kept, got), jnp.where(core == 0, got, kept)], axis=1)
-    grad_input = (back_own + back_got).astype(jnp.bfloat16)
     return output, grad_input, delta_grad
 
 

time: 250 us -> 240 us (0.960)
  waiting for transfers between devices: 59.6 us -> 54.6 us
  other arithmetic: 36.6 us -> 32.7 us
  Pallas kernels: 62.4 us -> 59 us
  starting transfers between devices: 62.9 us -> 65.8 us
    ppermute x3 -> x4, waiting for transfers between devices: 11.9 us -> 1.78 us  [along_z(): part_0 = lax.ppermute(block, ('zl', 'zh'), [(0, 2), (1, 0), (2, 3), (3, 1)])]
    ppermute x20, waiting for transfers between devices: 24.5 us -> 30.2 us  [shift(): lax.ppermute(value, axis, [(i, (i + step) % RING) for i in range(RING)])]
    ppermute x12, starting transfers between devices: 23 us -> 27.7 us  [swap(): return lax.ppermute(value, axis, [(0, 1), (1, 0)])]
    pallas_call x5, Pallas kernels: 62.4 us -> 59 us  [call(): pl.pallas_call(kernel, out_shape=outs, in_specs=in_specs, out_specs=[pl.B...]
    ppermute x3 -> x4, starting transfers between devices: 7.35 us -> 6.01 us  [along_z(): part_0 = lax.ppermute(block, ('zl', 'zh'), [(0, 2), (1, 0), (2, 3), (3, 1)])]
  transfers between devices with their start and end apart: 39 -> 41, of which waited for: 9 -> 12; matrix products, arithmetic and copies ran while one was open for 16% -> 17% of each run, Pallas kernels for 21% -> 21%
where the time goes in v5:
time: 240 us
  starting transfers between devices  65.8 us (27%)
  Pallas kernels  59 us (25%)
  waiting for transfers between devices  54.6 us (23%)
  other arithmetic  32.7 us (14%)
  between operations  15.3 us (6%)
  local copies, waits for them, and re-layouts  12.3 us (5%)
    pallas_call x5, Pallas kernels, call(): pl.pallas_call(kernel, out_shape=outs, in_specs=in_specs, out_specs=[pl.B...  59 us
    ppermute x20, waiting for transfers between devices, shift(): lax.ppermute(value, axis, [(i, (i + step) % RING) for i in range(RING)])  30.2 us
    ppermute x12, starting transfers between devices, swap(): return lax.ppermute(value, axis, [(0, 1), (1, 0)])  27.7 us
    ppermute x20, starting transfers between devices, shift(): lax.ppermute(value, axis, [(i, (i + step) % RING) for i in range(RING)])  27.3 us
    ppermute x12, waiting for transfers between devices, swap(): return lax.ppermute(value, axis, [(0, 1), (1, 0)])  22.6 us
    ppermute x4, starting transfers between devices, along_z(): part_0 = lax.ppermute(block, ('zl', 'zh'), [(0, 2), (1, 0), (2, 3), (3, 1)])  6.01 us
  transfers between devices with their start and end apart: 41, of which 12 were waited for; matrix products, arithmetic and copies ran while one was open for 17% of the time, Pallas kernels for 21%

profile of v5, /device:TPU:1, one launch (start us, length us, event | category | flops | bytes accessed | tf_op | source)
XLA Modules:
  0.0 239.6 jit_solution(18118389936199252505)
XLA Ops:
  8.6 3.4 %collective-permute-start.5 = (bf16[1024,256]{1,0:T(8,128)(2,1)S(1)}, bf16[1024,256]{1,0:T(8,128)(2,1)}, u32[]{:S(2)}, u32[]{:S(2)}) collective-permute-start(bf16[1024,256]{1,0:T(8,128)(2,1)S(1)} %get-tuple-element.133.refs_5_.refs_8_), channel_id=1, source_target_pairs={{0,96},{32,0},{64,32},{96,64},{1,97},{33,1},{65,33},{97,65},{2,98}... | collective-permute-start | bytes 1572872 | tf_op jit(solution)/shard_map/ppermute | solution.py:20
  12.9 3.7 %collective-permute-start.2 = (bf16[4,144,128]{2,1,0:T(8,128)(2,1)S(1)}, bf16[4,144,128]{2,1,0:T(8,128)(2,1)S(1)}, u32[]{:S(2)}, u32[]{:S(2)}) collective-permute-start(bf16[4,144,128]{2,1,0:T(8,128)(2,1)S(1)} %pad_maximum_fusion.9), channel_id=1, source_target_pairs={{0,1},{1,0},{2,3},{3,2},{4,5},{5,4},{6,7},{7,6},{8,9},{9,8},{10,11... | collective-permute-start | bytes 442376 | tf_op jit(solution)/shard_map/ppermute | solution.py:24
  21.4 4.4 %collective-permute-done.6.refs_7_.refs_10_ = bf16[1024,256]{1,0:T(8,128)(2,1)S(1)} collective-permute-done((bf16[1024,256]{1,0:T(8,128)(2,1)S(1)}, bf16[1024,256]{1,0:T(8,128)(2,1)S(1)}, u32[]{:S(2)}, u32[]{:S(2)}) %collective-permute-start.6) | collective-permute-done | bytes 524320 | tf_op jit(solution)/shard_map/ppermute | solution.py:20
  33.3 4.6 %collective-permute-done.3 = bf16[8,144,128]{2,1,0:T(8,128)(2,1)S(1)} collective-permute-done((bf16[8,144,128]{2,1,0:T(8,128)(2,1)S(1)}, bf16[8,144,128]{2,1,0:T(8,128)(2,1)S(1)}, u32[]{:S(2)}, u32[]{:S(2)}) %collective-permute-start.3) | collective-permute-done | bytes 294944 | tf_op jit(solution)/shard_map/ppermute | solution.py:24
  44.5 12.7 %collective-permute-done.9 = bf16[768,512]{1,0:T(8,128)(2,1)S(1)} collective-permute-done((bf16[768,512]{1,0:T(8,128)(2,1)}, bf16[768,512]{1,0:T(8,128)(2,1)S(1)}, u32[]{:S(2)}, u32[]{:S(2)}) %collective-permute-start.9) | collective-permute-done | bytes 786464 | tf_op jit(solution)/shard_map/ppermute | solution.py:20
  57.2 3.5 %collective-permute-start.12 = (bf16[384,512]{1,0:T(8,128)(2,1)S(1)}, bf16[384,512]{1,0:T(8,128)(2,1)S(1)}, u32[]{:S(2)}, u32[]{:S(2)}) collective-permute-start(bf16[384,512]{1,0:T(8,128)(2,1)S(1)} %slice.173), channel_id=1, source_target_pairs={{0,6},{2,0},{4,2},{6,4},{1,7},{3,1},{5,3},{7,5},{8,14},{10,8},{12,... | collective-permute-start | bytes 1179656 | tf_op jit(solution)/shard_map/ppermute | solution.py:20
  73.3 2.9 %collective-permute-start.15 = (bf16[2048,256]{1,0:T(8,128)(2,1)S(1)}, bf16[2048,256]{1,0:T(8,128)(2,1)S(1)}, u32[]{:S(2)}, u32[]{:S(2)}) collective-permute-start(bf16[2048,256]{1,0:T(8,128)(2,1)S(1)} %pad_maximum_fusion.3.refs_0_.refs_3_), channel_id=1, source_target_pairs={{0,96},{32,0},{64,32},{96,64},{1,97},{33,1},{65,33},{97,65},{2,98}... | collective-permute-start | bytes 3145736 | tf_op jit(solution)/shard_map/ppermute | solution.py:20
  76.2 4.4 %collective-permute-start.17 = (bf16[2,1024,256]{2,1,0:T(8,128)(2,1)S(1)}, bf16[2,1024,256]{2,1,0:T(8,128)(2,1)}, u32[]{:S(2)}, u32[]{:S(2)}) collective-permute-start(bf16[2,1024,256]{2,1,0:T(8,128)(2,1)S(1)} %pad_maximum_fusion.2.refs_6_.refs_9_), channel_id=1, source_target_pairs={{0,16},{1,0},{16,17},{17,1},{2,18},{3,2},{18,19},{19,3},{4,20},{5,... | collective-permute-start | bytes 3145736 | tf_op jit(solution)/shard_map/ppermute | solution.py:405
  82.9 3.2 %pad_maximum_fusion.cot_ref = bf16[4,768,512]{2,1,0:T(8,128)(2,1)} fusion(bf16[1,768,512]{2,1,0:T(8,128)(2,1)} %bitcast.21, bf16[1,768,512]{2,1,0:T(8,128)(2,1)} %bitcast.55, bf16[1,768,512]{2,1,0:T(8,128)(2,1)} %bitcast.56, bf16[1,768,512]{2,1,0:T(8,128)(2,1)} %bitcast.18), kind=kLoop, calls=%fused_computation | loop fusion | flops 4718592 | bytes 6291456 | tf_op jit(solution)/shard_map/stack | solution.py:443
  87.7 15.7 %shard_map.85 = (f32[2,768,1024]{2,1,0:T(8,128)}, f32[64,128,128]{2,1,0:T(8,128)}, f32[64,128,128]{2,1,0:T(8,128)}) custom-call(s32[5]{0:T(128)} %stack.56.where_ref, s32[128]{0:T(128)} %bitcast_select_fusion.codes_ref, bf16[128,144,128]{2,1,0:T(8,128)(2,1)} %all-gather.2.cloned.1.call-done.tiles_ref, bf16[4,768,512]{2,1,0:T(8,128)(2,1)} %pad_maximum_fusion.cot_ref, ...), custom_call_target="tpu_custom_call" | custom-call | flops 3221225 | bytes 25165 | tf_op jit(solution)/shard_map/pallas_call | solution.py:292
  103.5 4.8 %collective-permute-start.21 = (f32[64,128,128]{2,1,0:T(8,128)}, f32[64,128,128]{2,1,0:T(8,128)}, u32[]{:S(2)}, u32[]{:S(2)}) collective-permute-start(f32[64,128,128]{2,1,0:T(8,128)} %get-tuple-element.159), channel_id=1, source_target_pairs={{0,8},{8,0},{1,9},{9,1},{2,10},{10,2},{3,11},{11,3},{4,12},{12,4},... | collective-permute-start | bytes 12582920 | tf_op jit(solution)/shard_map/ppermute | solution.py:24
  111.0 3.0 %collective-permute-start.23 = (bf16[1024,256]{1,0:T(8,128)(2,1)}, bf16[1024,256]{1,0:T(8,128)(2,1)S(1)}, u32[]{:S(2)}, u32[]{:S(2)}) collective-permute-start(bf16[1024,256]{1,0:T(8,128)(2,1)} %slice.159), channel_id=1, source_target_pairs={{0,96},{32,0},{64,32},{96,64},{1,97},{33,1},{65,33},{97,65},{2,98}... | collective-permute-start | bytes 1572872 | tf_op jit(solution)/shard_map/ppermute | solution.py:20
  115.2 11.3 %shard_map.86.delta_ref = f32[4,768,512]{2,1,0:T(8,128)} custom-call(s32[5]{0:T(128)} %stack.56.where_ref, s32[128]{0:T(128)} %bitcast_select_fusion.codes_ref, bf16[128,144,128]{2,1,0:T(8,128)(2,1)} %all-gather.2.cloned.1.call-done.tiles_ref, bf16[384,1024]{1,0:T(8,128)(2,1)} %refs_0_.2, bf16[384,1024]{1,0:T(8,128)(2,1)} %copy-done.4, ...), custom_call_target="tpu_custom_call" | custom-call | flops 1610612 | bytes 16777 | tf_op jit(solution)/shard_map/pallas_call | solution.py:292
  129.3 9.5 %shard_map.87 = (f32[384,1024]{1,0:T(8,128)}, f32[384,1024]{1,0:T(8,128)}) custom-call(s32[5]{0:T(128)} %stack.56.where_ref, f32[2,768,1024]{2,1,0:T(8,128)} %get-tuple-element.152.delta_ref, bf16[4,768,512]{2,1,0:T(8,128)(2,1)} %pad_maximum_fusion.cot_ref, bf16[2048,256]{1,0:T(8,128)(2,1)} %copy-done.1, bf16[2048,256]{1,0:T(8,128)(2,1)} %copy-done.2, ...), custom_call_target="tpu_custom_call" | custom-call | flops 3221225 | bytes 16777 | tf_op jit(solution)/shard_map/pallas_call | solution.py:292
  140.4 3.4 %dynamic-slice_add_fusion.1 = (f32[16,128,128]{2,1,0:T(8,128)S(1)}, f32[16,128,128]{2,1,0:T(8,128)S(1)}, f32[16,128,128]{2,1,0:T(8,128)S(1)}) fusion(f32[64,128,128]{2,1,0:T(8,128)} %collective-permute-done.21, s32[]{:T(128)S(6)} %select_n.102, f32[64,128,128]{2,1,0:T(8,128)} %get-tuple-element.182, s32[]{:T(128)S(6)} %select_n.104, s32[]{:T(128)S(6)} %select_n.96), kind=kLoop, calls=%fused_computation.8 | loop fusion | flops 786432 | bytes 9437196 | tf_op jit(solution)/shard_map/add | solution.py:462
  147.3 13.1 %shard_map.88 = (f32[768,512]{1,0:T(8,128)}, f32[768,512]{1,0:T(8,128)}, f32[384,512]{1,0:T(8,128)}, f32[384,512]{1,0:T(8,128)}, f32[768,512]{1,0:T(8,128)}) custom-call(s32[5]{0:T(128)} %stack.56.where_ref, f32[4,768,512]{2,1,0:T(8,128)} %shard_map.86.delta_ref, bf16[384,1024]{1,0:T(8,128)(2,1)} %refs_0_.2, bf16[384,1024]{1,0:T(8,128)(2,1)} %copy-done.4, ...), custom_call_target="tpu_custom_call" | custom-call | flops 6442450 | bytes 25165 | tf_op jit(solution)/shard_map/pallas_call | solution.py:292
  167.4 3.1 %collective-permute-start.36 = (f32[384,1024]{1,0:T(8,128)}, f32[384,1024]{1,0:T(8,128)}, u32[]{:S(2)}, u32[]{:S(2)}) collective-permute-start(f32[384,1024]{1,0:T(8,128)} %add.143), channel_id=1, source_target_pairs={{0,1},{1,0},{2,3},{3,2},{4,5},{5,4},{6,7},{7,6},{8,9},{9,8},{10,11... | collective-permute-start | bytes 4718600 | tf_op jit(solution)/shard_map/ppermute | solution.py:24
  171.3 9.5 %shard_map.89 = (f32[384,1024]{1,0:T(8,128)}, f32[384,1024]{1,0:T(8,128)}) custom-call(s32[5]{0:T(128)} %stack.56.where_ref, f32[2,768,1024]{2,1,0:T(8,128)} %get-tuple-element.152.delta_ref, bf16[4,768,512]{2,1,0:T(8,128)(2,1)} %pad_maximum_fusion.cot_ref, bf16[2048,256]{1,0:T(8,128)(2,1)} %copy-done.1, bf16[2048,256]{1,0:T(8,128)(2,1)} %copy-done.2, ...), custom_call_target="tpu_custom_call" | custom-call | flops 3221225 | bytes 16777 | tf_op jit(solution)/shard_map/pallas_call | solution.py:292
  189.6 5.1 %collective-permute-done.34 = f32[16,128,128]{2,1,0:T(8,128)} collective-permute-done((f32[16,128,128]{2,1,0:T(8,128)S(1)}, f32[16,128,128]{2,1,0:T(8,128)}, u32[]{:S(2)}, u32[]{:S(2)}) %collective-permute-start.34) | collective-permute-done | bytes 1048608 | tf_op jit(solution)/shard_map/ppermute | solution.py:20
  196.8 6.7 %collective-permute-done.36 = f32[384,1024]{1,0:T(8,128)} collective-permute-done((f32[384,1024]{1,0:T(8,128)}, f32[384,1024]{1,0:T(8,128)}, u32[]{:S(2)}, u32[]{:S(2)}) %collective-permute-start.36) | collective-permute-done | bytes 1572896 | tf_op jit(solution)/shard_map/ppermute | solution.py:24
  204.3 2.9 %collective-permute-start.37 = (f32[8,128,128]{2,1,0:T(8,128)}, f32[8,128,128]{2,1,0:T(8,128)S(1)}, u32[]{:S(2)}, u32[]{:S(2)}) collective-permute-start(f32[8,128,128]{2,1,0:T(8,128)} %dynamic-slice_bitcast_fusion), channel_id=1, source_target_pairs={{0,16},{16,0},{1,17},{17,1},{2,18},{18,2},{3,19},{19,3},{4,20},{20... | collective-permute-start | bytes 1572872 | tf_op jit(solution)/shard_map/ppermute | solution.py:24
  207.2 9.6 %collective-permute-done.37 = f32[8,128,128]{2,1,0:T(8,128)S(1)} collective-permute-done((f32[8,128,128]{2,1,0:T(8,128)}, f32[8,128,128]{2,1,0:T(8,128)S(1)}, u32[]{:S(2)}, u32[]{:S(2)}) %collective-permute-start.37) | collective-permute-done | bytes 524320 | tf_op jit(solution)/shard_map/ppermute | solution.py:24
  216.9 3.3 %add_convert_fusion = bf16[384,1024]{1,0:T(8,128)(2,1)} fusion(f32[384,1024]{1,0:T(8,128)} %collective-permute-done.36, f32[384,1024]{1,0:T(8,128)S(1)} %copy-done.19, f32[384,1024]{1,0:T(8,128)} %collective-permute-done.38), kind=kLoop, calls=%fused_computation.2 | loop fusion | flops 1179648 | bytes 5505024 | tf_op jit(solution)/shard_map/convert_element_type | solution.py:496
  221.6 5.2 %collective-permute-done.31 = f32[768,512]{1,0:T(8,128)} collective-permute-done((f32[768,512]{1,0:T(8,128)}, f32[768,512]{1,0:T(8,128)}, u32[]{:S(2)}, u32[]{:S(2)}) %collective-permute-start.31) | collective-permute-done | bytes 1572896 | tf_op jit(solution)/shard_map/ppermute | solution.py:20
  (161 shorter events, 75.7 us)
Async XLA Ops:
  7.2 78.9 %all-gather.2.cloned.1.call-start = ((), (), s32[]{:S(2)}) async-start(), calls=%async_computation | async-start | bytes 5308416 | tf_op jit(solution)/shard_map/all_gather | solution.py:429
  8.6 19.4 %collective-permute-start.5 = (bf16[1024,256]{1,0:T(8,128)(2,1)S(1)}, bf16[1024,256]{1,0:T(8,128)(2,1)}, u32[]{:S(2)}, u32[]{:S(2)}) collective-permute-start(bf16[1024,256]{1,0:T(8,128)(2,1)S(1)} %get-tuple-element.133.refs_5_.refs_8_), channel_id=1, source_target_pairs={{0,96},{32,0},{64,32},{96,64},{1,97},{33,1},{65,33},{97,65},{2,98}... | collective-permute-start | bytes 1572872 | tf_op jit(solution)/shard_map/ppermute | solution.py:20
  18.0 20.0 %collective-permute-start = (bf16[1024,256]{1,0:T(8,128)(2,1)S(1)}, bf16[1024,256]{1,0:T(8,128)(2,1)}, u32[]{:S(2)}, u32[]{:S(2)}) collective-permute-start(bf16[1024,256]{1,0:T(8,128)(2,1)S(1)} %get-tuple-element.138), channel_id=1, source_target_pairs={{0,16},{1,0},{16,17},{17,1},{2,18},{3,2},{18,19},{19,3},{4,20},{5,... | collective-permute-start | bytes 1572872 | tf_op jit(solution)/shard_map/ppermute | solution.py:405
  19.9 18.1 %collective-permute-start.1 = (bf16[1024,256]{1,0:T(8,128)(2,1)S(1)}, bf16[1024,256]{1,0:T(8,128)(2,1)}, u32[]{:S(2)}, u32[]{:S(2)}) collective-permute-start(bf16[1024,256]{1,0:T(8,128)(2,1)S(1)} %get-tuple-element.138), channel_id=1, source_target_pairs={{1,16},{16,1},{3,18},{18,3},{5,20},{20,5},{7,22},{22,7},{9,24},{24... | collective-permute-start | bytes 1572872 | tf_op jit(solution)/shard_map/ppermute | solution.py:406
  39.0 18.2 %collective-permute-start.9 = (bf16[768,512]{1,0:T(8,128)(2,1)}, bf16[768,512]{1,0:T(8,128)(2,1)S(1)}, u32[]{:S(2)}, u32[]{:S(2)}) collective-permute-start(bf16[768,512]{1,0:T(8,128)(2,1)} %pad_maximum_fusion.4), channel_id=1, source_target_pairs={{0,6},{2,0},{4,2},{6,4},{1,7},{3,1},{5,3},{7,5},{8,14},{10,8},{12,... | collective-permute-start | bytes 2359304 | tf_op jit(solution)/shard_map/ppermute | solution.py:20
  41.8 18.9 %collective-permute-start.10 = (bf16[768,512]{1,0:T(8,128)(2,1)}, bf16[768,512]{1,0:T(8,128)(2,1)}, u32[]{:S(2)}, u32[]{:S(2)}) collective-permute-start(bf16[768,512]{1,0:T(8,128)(2,1)} %pad_maximum_fusion.4), channel_id=1, source_target_pairs={{0,2},{2,4},{4,6},{6,0},{1,3},{3,5},{5,7},{7,1},{8,10},{10,12},{12... | collective-permute-start | bytes 2359304 | tf_op jit(solution)/shard_map/ppermute | solution.py:20
  41.8 22.3 %collective-permute-start.19 = (bf16[384,1024]{1,0:T(8,128)(2,1)S(1)}, bf16[384,1024]{1,0:T(8,128)(2,1)S(1)}, u32[]{:S(2)}, u32[]{:S(2)}) collective-permute-start(bf16[384,1024]{1,0:T(8,128)(2,1)S(1)} %copy-done.3), channel_id=1, source_target_pairs={{0,1},{1,0},{2,3},{3,2},{4,5},{5,4},{6,7},{7,6},{8,9},{9,8},{10,11... | collective-permute-start | bytes 2359304 | tf_op jit(solution)/shard_map/ppermute | solution.py:24
  43.2 28.5 %collective-permute-start.13 = (bf16[1024,256]{1,0:T(8,128)(2,1)S(1)}, bf16[1024,256]{1,0:T(8,128)(2,1)S(1)}, u32[]{:S(2)}, u32[]{:S(2)}) collective-permute-start(bf16[1024,256]{1,0:T(8,128)(2,1)S(1)} %get-tuple-element.133.refs_5_.refs_8_), channel_id=1, source_target_pairs={{0,16},{1,0},{16,17},{17,1},{2,18},{3,2},{18,19},{19,3},{4,20},{5,... | collective-permute-start | bytes 1572872 | tf_op jit(solution)/shard_map/ppermute | solution.py:405
  43.8 28.0 %collective-permute-start.14 = (bf16[1024,256]{1,0:T(8,128)(2,1)S(1)}, bf16[1024,256]{1,0:T(8,128)(2,1)S(1)}, u32[]{:S(2)}, u32[]{:S(2)}) collective-permute-start(bf16[1024,256]{1,0:T(8,128)(2,1)S(1)} %get-tuple-element.133.refs_5_.refs_8_), channel_id=1, source_target_pairs={{1,16},{16,1},{3,18},{18,3},{5,20},{20,5},{7,22},{22,7},{9,24},{24... | collective-permute-start | bytes 1572872 | tf_op jit(solution)/shard_map/ppermute | solution.py:406
  65.5 22.3 %collective-permute-start.20 = (bf16[2,384,1024]{2,1,0:T(8,128)(2,1)}, bf16[2,384,1024]{2,1,0:T(8,128)(2,1)}, u32[]{:S(2)}, u32[]{:S(2)}) collective-permute-start(bf16[2,384,1024]{2,1,0:T(8,128)(2,1)} %pad_maximum_fusion.1), channel_id=1, source_target_pairs={{0,8},{8,0},{1,9},{9,1},{2,10},{10,2},{3,11},{11,3},{4,12},{12,4},... | collective-permute-start | bytes 4718600 | tf_op jit(solution)/shard_map/ppermute | solution.py:24
  73.3 30.1 %collective-permute-start.15 = (bf16[2048,256]{1,0:T(8,128)(2,1)S(1)}, bf16[2048,256]{1,0:T(8,128)(2,1)S(1)}, u32[]{:S(2)}, u32[]{:S(2)}) collective-permute-start(bf16[2048,256]{1,0:T(8,128)(2,1)S(1)} %pad_maximum_fusion.3.refs_0_.refs_3_), channel_id=1, source_target_pairs={{0,96},{32,0},{64,32},{96,64},{1,97},{33,1},{65,33},{97,65},{2,98}... | collective-permute-start | bytes 3145736 | tf_op jit(solution)/shard_map/ppermute | solution.py:20
  76.2 27.3 %collective-permute-start.16 = (bf16[2048,256]{1,0:T(8,128)(2,1)S(1)}, bf16[2048,256]{1,0:T(8,128)(2,1)}, u32[]{:S(2)}, u32[]{:S(2)}) collective-permute-start(bf16[2048,256]{1,0:T(8,128)(2,1)S(1)} %pad_maximum_fusion.3.refs_0_.refs_3_), channel_id=1, source_target_pairs={{0,32},{32,64},{64,96},{96,0},{1,33},{33,65},{65,97},{97,1},{2,34}... | collective-permute-start | bytes 3145736 | tf_op jit(solution)/shard_map/ppermute | solution.py:20
  76.2 27.3 %collective-permute-start.17 = (bf16[2,1024,256]{2,1,0:T(8,128)(2,1)S(1)}, bf16[2,1024,256]{2,1,0:T(8,128)(2,1)}, u32[]{:S(2)}, u32[]{:S(2)}) collective-permute-start(bf16[2,1024,256]{2,1,0:T(8,128)(2,1)S(1)} %pad_maximum_fusion.2.refs_6_.refs_9_), channel_id=1, source_target_pairs={{0,16},{1,0},{16,17},{17,1},{2,18},{3,2},{18,19},{19,3},{4,20},{5,... | collective-permute-start | bytes 3145736 | tf_op jit(solution)/shard_map/ppermute | solution.py:405
  80.6 22.9 %collective-permute-start.18 = (bf16[2,1024,256]{2,1,0:T(8,128)(2,1)S(1)}, bf16[2,1024,256]{2,1,0:T(8,128)(2,1)}, u32[]{:S(2)}, u32[]{:S(2)}) collective-permute-start(bf16[2,1024,256]{2,1,0:T(8,128)(2,1)S(1)} %pad_maximum_fusion.2.refs_6_.refs_9_), channel_id=1, source_target_pairs={{1,16},{16,1},{3,18},{18,3},{5,20},{20,5},{7,22},{22,7},{9,24},{24... | collective-permute-start | bytes 3145736 | tf_op jit(solution)/shard_map/ppermute | solution.py:406
  103.5 24.8 %collective-permute-start.21 = (f32[64,128,128]{2,1,0:T(8,128)}, f32[64,128,128]{2,1,0:T(8,128)}, u32[]{:S(2)}, u32[]{:S(2)}) collective-permute-start(f32[64,128,128]{2,1,0:T(8,128)} %get-tuple-element.159), channel_id=1, source_target_pairs={{0,8},{8,0},{1,9},{9,1},{2,10},{10,2},{3,11},{11,3},{4,12},{12,4},... | collective-permute-start | bytes 12582920 | tf_op jit(solution)/shard_map/ppermute | solution.py:24
  138.8 21.8 %collective-permute-start.28 = (f32[384,1024]{1,0:T(8,128)}, f32[384,1024]{1,0:T(8,128)}, u32[]{:S(2)}, u32[]{:S(2)}) collective-permute-start(f32[384,1024]{1,0:T(8,128)} %get-tuple-element.185), channel_id=1, source_target_pairs={{0,8},{8,0},{1,9},{9,1},{2,10},{10,2},{3,11},{11,3},{4,12},{12,4},... | collective-permute-start | bytes 4718600 | tf_op jit(solution)/shard_map/ppermute | solution.py:24
  160.5 20.3 %collective-permute-start.29 = (f32[384,512]{1,0:T(8,128)}, f32[384,512]{1,0:T(8,128)}, u32[]{:S(2)}, u32[]{:S(2)}) collective-permute-start(f32[384,512]{1,0:T(8,128)} %get-tuple-element.187), channel_id=1, source_target_pairs={{0,2},{2,4},{4,6},{6,0},{1,3},{3,5},{5,7},{7,1},{8,10},{10,12},{12... | collective-permute-start | bytes 2359304 | tf_op jit(solution)/shard_map/ppermute | solution.py:20
  160.6 20.2 %collective-permute-start.30 = (f32[384,512]{1,0:T(8,128)}, f32[384,512]{1,0:T(8,128)}, u32[]{:S(2)}, u32[]{:S(2)}) collective-permute-start(f32[384,512]{1,0:T(8,128)} %get-tuple-element.188), channel_id=1, source_target_pairs={{0,6},{2,0},{4,2},{6,4},{1,7},{3,1},{5,3},{7,5},{8,14},{10,8},{12,... | collective-permute-start | bytes 2359304 | tf_op jit(solution)/shard_map/ppermute | solution.py:20
  163.4 26.2 %collective-permute-start.35 = (f32[16,128,128]{2,1,0:T(8,128)S(1)}, f32[16,128,128]{2,1,0:T(8,128)S(1)}, u32[]{:S(2)}, u32[]{:S(2)}) collective-permute-start(f32[16,128,128]{2,1,0:T(8,128)S(1)} %fusion), channel_id=1, source_target_pairs={{0,96},{32,0},{64,32},{96,64},{1,97},{33,1},{65,33},{97,65},{2,98}... | collective-permute-start | bytes 3145736 | tf_op jit(solution)/shard_map/ppermute | solution.py:20
  167.4 36.0 %collective-permute-start.36 = (f32[384,1024]{1,0:T(8,128)}, f32[384,1024]{1,0:T(8,128)}, u32[]{:S(2)}, u32[]{:S(2)}) collective-permute-start(f32[384,1024]{1,0:T(8,128)} %add.143), channel_id=1, source_target_pairs={{0,1},{1,0},{2,3},{3,2},{4,5},{5,4},{6,7},{7,6},{8,9},{9,8},{10,11... | collective-permute-start | bytes 4718600 | tf_op jit(solution)/shard_map/ppermute | solution.py:24
  170.7 24.0 %collective-permute-start.34 = (f32[16,128,128]{2,1,0:T(8,128)S(1)}, f32[16,128,128]{2,1,0:T(8,128)}, u32[]{:S(2)}, u32[]{:S(2)}) collective-permute-start(f32[16,128,128]{2,1,0:T(8,128)S(1)} %fusion.1), channel_id=1, source_target_pairs={{0,32},{32,64},{64,96},{96,0},{1,33},{33,65},{65,97},{97,1},{2,34}... | collective-permute-start | bytes 3145736 | tf_op jit(solution)/shard_map/ppermute | solution.py:20
  180.8 36.1 %collective-permute-start.38 = (f32[384,1024]{1,0:T(8,128)}, f32[384,1024]{1,0:T(8,128)}, u32[]{:S(2)}, u32[]{:S(2)}) collective-permute-start(f32[384,1024]{1,0:T(8,128)} %get-tuple-element.203), channel_id=1, source_target_pairs={{0,8},{8,0},{1,9},{9,1},{2,10},{10,2},{3,11},{11,3},{4,12},{12,4},... | collective-permute-start | bytes 4718600 | tf_op jit(solution)/shard_map/ppermute | solution.py:24
  185.3 36.3 %collective-permute-start.32 = (f32[768,512]{1,0:T(8,128)}, f32[768,512]{1,0:T(8,128)}, u32[]{:S(2)}, u32[]{:S(2)}) collective-permute-start(f32[768,512]{1,0:T(8,128)} %add_dynamic-update-slice_fusion), channel_id=1, source_target_pairs={{0,6},{2,0},{4,2},{6,4},{1,7},{3,1},{5,3},{7,5},{8,14},{10,8},{12,... | collective-permute-start | bytes 4718600 | tf_op jit(solution)/shard_map/ppermute | solution.py:20
  189.6 37.2 %collective-permute-start.31 = (f32[768,512]{1,0:T(8,128)}, f32[768,512]{1,0:T(8,128)}, u32[]{:S(2)}, u32[]{:S(2)}) collective-permute-start(f32[768,512]{1,0:T(8,128)} %add_dynamic-update-slice_fusion.1), channel_id=1, source_target_pairs={{0,2},{2,4},{4,6},{6,0},{1,3},{3,5},{5,7},{7,1},{8,10},{10,12},{12... | collective-permute-start | bytes 4718600 | tf_op jit(solution)/shard_map/ppermute | solution.py:20
  (40 other events, 417.5 us)
Sparse Core Ops, SparseCore 0:
  39.1 37.9 all-gather.1

commit v6 on v5

--- a/solution.py
+++ b/solution.py
@@ -498,8 +498,8 @@
     grads = grads[:per_owner] + swap(grads[per_owner:], "zh")
     delta_grad = (grads * scaling * live[:, None, None].astype(jnp.float32))[None]
 
-    mine_out = (mine_out + got[0] + got[1]).astype(jnp.bfloat16)
-    kept, got = mine_out[:tokens], swap(mine_out[tokens:], "core")
+    leaving = (mine_out[tokens:] + got[0][tokens:] + got[1][tokens:]).astype(jnp.bfloat16)
+    kept, got = (mine_out[:tokens] + got[0][:tokens] + got[1][:tokens]).astype(jnp.bfloat16), swap(leaving, "core")
     output = jnp.concatenate([jnp.where(core == 0, kept, got), jnp.where(core == 0, got, kept)], axis=1)
     return output, grad_input, delta_grad
 

time: 240 us -> 241 us (level)
  no operation moved by 1% of the time
where the time goes in v6:
time: 241 us; the launch traced here: 240 us
  starting transfers between devices  64.3 us (27%)
  Pallas kernels  60.6 us (25%)
  waiting for transfers between devices  53.9 us (22%)
  other arithmetic  33.6 us (14%)
  between operations  15.3 us (6%)
  local copies, waits for them, and re-layouts  12.2 us (5%)
    pallas_call x5, Pallas kernels, call(): pl.pallas_call(kernel, out_shape=outs, in_specs=in_specs, out_specs=[pl.B...  60.6 us
    ppermute x20, waiting for transfers between devices, shift(): lax.ppermute(value, axis, [(i, (i + step) % RING) for i in range(RING)])  30.2 us
    ppermute x20, starting transfers between devices, shift(): lax.ppermute(value, axis, [(i, (i + step) % RING) for i in range(RING)])  27.3 us
    ppermute x12, starting transfers between devices, swap(): return lax.ppermute(value, axis, [(0, 1), (1, 0)])  26.3 us
    ppermute x12, waiting for transfers between devices, swap(): return lax.ppermute(value, axis, [(0, 1), (1, 0)])  22.6 us
    ppermute x4, starting transfers between devices, along_z(): part_0 = lax.ppermute(block, ('zl', 'zh'), [(0, 2), (1, 0), (2, 3), (3, 1)])  6 us
  transfers between devices with their start and end apart: 41, of which 12 were waited for; matrix products, arithmetic and copies ran while one was open for 17% of the time, Pallas kernels for 21%

profile of v6, /device:TPU:1, one launch (start us, length us, event | category | flops | bytes accessed | tf_op | source)
XLA Modules:
  0.0 240.0 jit_solution(15472532781526183888)
XLA Ops:
  8.6 3.4 %collective-permute-start.5 = (bf16[1024,256]{1,0:T(8,128)(2,1)S(1)}, bf16[1024,256]{1,0:T(8,128)(2,1)}, u32[]{:S(2)}, u32[]{:S(2)}) collective-permute-start(bf16[1024,256]{1,0:T(8,128)(2,1)S(1)} %get-tuple-element.133.refs_5_.refs_8_), channel_id=1, source_target_pairs={{0,96},{32,0},{64,32},{96,64},{1,97},{33,1},{65,33},{97,65},{2,98}... | collective-permute-start | bytes 1572872 | tf_op jit(solution)/shard_map/ppermute | solution.py:20
  12.9 3.7 %collective-permute-start.2 = (bf16[4,144,128]{2,1,0:T(8,128)(2,1)S(1)}, bf16[4,144,128]{2,1,0:T(8,128)(2,1)S(1)}, u32[]{:S(2)}, u32[]{:S(2)}) collective-permute-start(bf16[4,144,128]{2,1,0:T(8,128)(2,1)S(1)} %pad_maximum_fusion.9), channel_id=1, source_target_pairs={{0,1},{1,0},{2,3},{3,2},{4,5},{5,4},{6,7},{7,6},{8,9},{9,8},{10,11... | collective-permute-start | bytes 442376 | tf_op jit(solution)/shard_map/ppermute | solution.py:24
  21.4 4.4 %collective-permute-done.6.refs_7_.refs_10_ = bf16[1024,256]{1,0:T(8,128)(2,1)S(1)} collective-permute-done((bf16[1024,256]{1,0:T(8,128)(2,1)S(1)}, bf16[1024,256]{1,0:T(8,128)(2,1)S(1)}, u32[]{:S(2)}, u32[]{:S(2)}) %collective-permute-start.6) | collective-permute-done | bytes 524320 | tf_op jit(solution)/shard_map/ppermute | solution.py:20
  33.3 4.6 %collective-permute-done.3 = bf16[8,144,128]{2,1,0:T(8,128)(2,1)S(1)} collective-permute-done((bf16[8,144,128]{2,1,0:T(8,128)(2,1)S(1)}, bf16[8,144,128]{2,1,0:T(8,128)(2,1)S(1)}, u32[]{:S(2)}, u32[]{:S(2)}) %collective-permute-start.3) | collective-permute-done | bytes 294944 | tf_op jit(solution)/shard_map/ppermute | solution.py:24
  44.5 12.7 %collective-permute-done.9 = bf16[768,512]{1,0:T(8,128)(2,1)S(1)} collective-permute-done((bf16[768,512]{1,0:T(8,128)(2,1)}, bf16[768,512]{1,0:T(8,128)(2,1)S(1)}, u32[]{:S(2)}, u32[]{:S(2)}) %collective-permute-start.9) | collective-permute-done | bytes 786464 | tf_op jit(solution)/shard_map/ppermute | solution.py:20
  57.2 3.5 %collective-permute-start.12 = (bf16[384,512]{1,0:T(8,128)(2,1)S(1)}, bf16[384,512]{1,0:T(8,128)(2,1)S(1)}, u32[]{:S(2)}, u32[]{:S(2)}) collective-permute-start(bf16[384,512]{1,0:T(8,128)(2,1)S(1)} %slice.189), channel_id=1, source_target_pairs={{0,6},{2,0},{4,2},{6,4},{1,7},{3,1},{5,3},{7,5},{8,14},{10,8},{12,... | collective-permute-start | bytes 1179656 | tf_op jit(solution)/shard_map/ppermute | solution.py:20
  73.3 2.9 %collective-permute-start.15 = (bf16[2048,256]{1,0:T(8,128)(2,1)S(1)}, bf16[2048,256]{1,0:T(8,128)(2,1)S(1)}, u32[]{:S(2)}, u32[]{:S(2)}) collective-permute-start(bf16[2048,256]{1,0:T(8,128)(2,1)S(1)} %pad_maximum_fusion.3.refs_0_.refs_3_), channel_id=1, source_target_pairs={{0,96},{32,0},{64,32},{96,64},{1,97},{33,1},{65,33},{97,65},{2,98}... | collective-permute-start | bytes 3145736 | tf_op jit(solution)/shard_map/ppermute | solution.py:20
  76.2 4.4 %collective-permute-start.17 = (bf16[2,1024,256]{2,1,0:T(8,128)(2,1)S(1)}, bf16[2,1024,256]{2,1,0:T(8,128)(2,1)}, u32[]{:S(2)}, u32[]{:S(2)}) collective-permute-start(bf16[2,1024,256]{2,1,0:T(8,128)(2,1)S(1)} %pad_maximum_fusion.2.refs_6_.refs_9_), channel_id=1, source_target_pairs={{0,16},{1,0},{16,17},{17,1},{2,18},{3,2},{18,19},{19,3},{4,20},{5,... | collective-permute-start | bytes 3145736 | tf_op jit(solution)/shard_map/ppermute | solution.py:405
  82.9 3.2 %pad_maximum_fusion.cot_ref = bf16[4,768,512]{2,1,0:T(8,128)(2,1)} fusion(bf16[1,768,512]{2,1,0:T(8,128)(2,1)} %bitcast.21, bf16[1,768,512]{2,1,0:T(8,128)(2,1)} %bitcast.55, bf16[1,768,512]{2,1,0:T(8,128)(2,1)} %bitcast.56, bf16[1,768,512]{2,1,0:T(8,128)(2,1)} %bitcast.18), kind=kLoop, calls=%fused_computation | loop fusion | flops 4718592 | bytes 6291456 | tf_op jit(solution)/shard_map/stack | solution.py:443
  87.7 16.5 %shard_map.85 = (f32[2,768,1024]{2,1,0:T(8,128)}, f32[64,128,128]{2,1,0:T(8,128)}, f32[64,128,128]{2,1,0:T(8,128)}) custom-call(s32[5]{0:T(128)} %stack.56.where_ref, s32[128]{0:T(128)} %bitcast_select_fusion.codes_ref, bf16[128,144,128]{2,1,0:T(8,128)(2,1)} %all-gather.2.cloned.1.call-done.tiles_ref, bf16[4,768,512]{2,1,0:T(8,128)(2,1)} %pad_maximum_fusion.cot_ref, ...), custom_call_target="tpu_custom_call" | custom-call | flops 3221225 | bytes 25165 | tf_op jit(solution)/shard_map/pallas_call | solution.py:292
  104.3 3.4 %collective-permute-start.21 = (f32[64,128,128]{2,1,0:T(8,128)}, f32[64,128,128]{2,1,0:T(8,128)}, u32[]{:S(2)}, u32[]{:S(2)}) collective-permute-start(f32[64,128,128]{2,1,0:T(8,128)} %get-tuple-element.159), channel_id=1, source_target_pairs={{0,8},{8,0},{1,9},{9,1},{2,10},{10,2},{3,11},{11,3},{4,12},{12,4},... | collective-permute-start | bytes 12582920 | tf_op jit(solution)/shard_map/ppermute | solution.py:24
  110.5 3.0 %collective-permute-start.23 = (bf16[1024,256]{1,0:T(8,128)(2,1)}, bf16[1024,256]{1,0:T(8,128)(2,1)S(1)}, u32[]{:S(2)}, u32[]{:S(2)}) collective-permute-start(bf16[1024,256]{1,0:T(8,128)(2,1)} %slice.171), channel_id=1, source_target_pairs={{0,96},{32,0},{64,32},{96,64},{1,97},{33,1},{65,33},{97,65},{2,98}... | collective-permute-start | bytes 1572872 | tf_op jit(solution)/shard_map/ppermute | solution.py:20
  114.6 12.0 %shard_map.86.delta_ref = f32[4,768,512]{2,1,0:T(8,128)} custom-call(s32[5]{0:T(128)} %stack.56.where_ref, s32[128]{0:T(128)} %bitcast_select_fusion.codes_ref, bf16[128,144,128]{2,1,0:T(8,128)(2,1)} %all-gather.2.cloned.1.call-done.tiles_ref, bf16[384,1024]{1,0:T(8,128)(2,1)} %refs_0_.2, bf16[384,1024]{1,0:T(8,128)(2,1)} %copy-done.4, ...), custom_call_target="tpu_custom_call" | custom-call | flops 1610612 | bytes 16777 | tf_op jit(solution)/shard_map/pallas_call | solution.py:292
  128.7 9.5 %shard_map.87 = (f32[384,1024]{1,0:T(8,128)}, f32[384,1024]{1,0:T(8,128)}) custom-call(s32[5]{0:T(128)} %stack.56.where_ref, f32[2,768,1024]{2,1,0:T(8,128)} %get-tuple-element.152.delta_ref, bf16[4,768,512]{2,1,0:T(8,128)(2,1)} %pad_maximum_fusion.cot_ref, bf16[2048,256]{1,0:T(8,128)(2,1)} %copy-done.1, bf16[2048,256]{1,0:T(8,128)(2,1)} %copy-done.2, ...), custom_call_target="tpu_custom_call" | custom-call | flops 3221225 | bytes 16777 | tf_op jit(solution)/shard_map/pallas_call | solution.py:292
  139.8 3.4 %dynamic-slice_add_fusion.1 = (f32[16,128,128]{2,1,0:T(8,128)S(1)}, f32[16,128,128]{2,1,0:T(8,128)S(1)}, f32[16,128,128]{2,1,0:T(8,128)S(1)}) fusion(f32[64,128,128]{2,1,0:T(8,128)} %collective-permute-done.21, s32[]{:T(128)S(6)} %select_n.102, f32[64,128,128]{2,1,0:T(8,128)} %get-tuple-element.182, s32[]{:T(128)S(6)} %select_n.104, s32[]{:T(128)S(6)} %select_n.96), kind=kLoop, calls=%fused_computation.7 | loop fusion | flops 786432 | bytes 9437196 | tf_op jit(solution)/shard_map/add | solution.py:462
  146.8 13.1 %shard_map.88 = (f32[768,512]{1,0:T(8,128)}, f32[768,512]{1,0:T(8,128)}, f32[384,512]{1,0:T(8,128)}, f32[384,512]{1,0:T(8,128)}, f32[768,512]{1,0:T(8,128)}) custom-call(s32[5]{0:T(128)} %stack.56.where_ref, f32[4,768,512]{2,1,0:T(8,128)} %shard_map.86.delta_ref, bf16[384,1024]{1,0:T(8,128)(2,1)} %refs_0_.2, bf16[384,1024]{1,0:T(8,128)(2,1)} %copy-done.4, ...), custom_call_target="tpu_custom_call" | custom-call | flops 6442450 | bytes 25165 | tf_op jit(solution)/shard_map/pallas_call | solution.py:292
  164.0 2.8 %add.151 = f32[384,1024]{1,0:T(8,128)} add(f32[384,1024]{1,0:T(8,128)S(1)} %copy-done.17, f32[384,1024]{1,0:T(8,128)} %collective-permute-done.28) | non-fusion elementwise | flops 393216 | bytes 4718592 | tf_op jit(solution)/shard_map/add | solution.py:482
  166.9 3.1 %collective-permute-start.36 = (f32[384,1024]{1,0:T(8,128)}, f32[384,1024]{1,0:T(8,128)}, u32[]{:S(2)}, u32[]{:S(2)}) collective-permute-start(f32[384,1024]{1,0:T(8,128)} %add.151), channel_id=1, source_target_pairs={{0,1},{1,0},{2,3},{3,2},{4,5},{5,4},{6,7},{7,6},{8,9},{9,8},{10,11... | collective-permute-start | bytes 4718600 | tf_op jit(solution)/shard_map/ppermute | solution.py:24
  170.8 9.5 %shard_map.89 = (f32[384,1024]{1,0:T(8,128)}, f32[384,1024]{1,0:T(8,128)}) custom-call(s32[5]{0:T(128)} %stack.56.where_ref, f32[2,768,1024]{2,1,0:T(8,128)} %get-tuple-element.152.delta_ref, bf16[4,768,512]{2,1,0:T(8,128)(2,1)} %pad_maximum_fusion.cot_ref, bf16[2048,256]{1,0:T(8,128)(2,1)} %copy-done.1, bf16[2048,256]{1,0:T(8,128)(2,1)} %copy-done.2, ...), custom_call_target="tpu_custom_call" | custom-call | flops 3221225 | bytes 16777 | tf_op jit(solution)/shard_map/pallas_call | solution.py:292
  189.0 5.1 %collective-permute-done.34 = f32[16,128,128]{2,1,0:T(8,128)} collective-permute-done((f32[16,128,128]{2,1,0:T(8,128)S(1)}, f32[16,128,128]{2,1,0:T(8,128)}, u32[]{:S(2)}, u32[]{:S(2)}) %collective-permute-start.34) | collective-permute-done | bytes 1048608 | tf_op jit(solution)/shard_map/ppermute | solution.py:20
  196.2 6.7 %collective-permute-done.36 = f32[384,1024]{1,0:T(8,128)} collective-permute-done((f32[384,1024]{1,0:T(8,128)}, f32[384,1024]{1,0:T(8,128)}, u32[]{:S(2)}, u32[]{:S(2)}) %collective-permute-start.36) | collective-permute-done | bytes 1572896 | tf_op jit(solution)/shard_map/ppermute | solution.py:24
  206.3 9.6 %collective-permute-done.37 = f32[8,128,128]{2,1,0:T(8,128)S(1)} collective-permute-done((f32[8,128,128]{2,1,0:T(8,128)}, f32[8,128,128]{2,1,0:T(8,128)S(1)}, u32[]{:S(2)}, u32[]{:S(2)}) %collective-permute-start.37) | collective-permute-done | bytes 524320 | tf_op jit(solution)/shard_map/ppermute | solution.py:24
  216.0 3.2 %add_convert_fusion = bf16[384,1024]{1,0:T(8,128)(2,1)} fusion(f32[384,1024]{1,0:T(8,128)} %collective-permute-done.36, f32[384,1024]{1,0:T(8,128)S(1)} %copy-done.18, f32[384,1024]{1,0:T(8,128)} %collective-permute-done.38), kind=kLoop, calls=%fused_computation.2 | loop fusion | flops 1179648 | bytes 5505024 | tf_op jit(solution)/shard_map/convert_element_type | solution.py:496
  221.1 5.2 %collective-permute-done.31 = f32[768,512]{1,0:T(8,128)} collective-permute-done((f32[768,512]{1,0:T(8,128)}, f32[768,512]{1,0:T(8,128)}, u32[]{:S(2)}, u32[]{:S(2)}) %collective-permute-start.31) | collective-permute-done | bytes 1572896 | tf_op jit(solution)/shard_map/ppermute | solution.py:20
  (161 shorter events, 76.0 us)
Async XLA Ops:
  7.2 78.9 %all-gather.2.cloned.1.call-start = ((), (), s32[]{:S(2)}) async-start(), calls=%async_computation | async-start | bytes 5308416 | tf_op jit(solution)/shard_map/all_gather | solution.py:429
  8.6 19.4 %collective-permute-start.5 = (bf16[1024,256]{1,0:T(8,128)(2,1)S(1)}, bf16[1024,256]{1,0:T(8,128)(2,1)}, u32[]{:S(2)}, u32[]{:S(2)}) collective-permute-start(bf16[1024,256]{1,0:T(8,128)(2,1)S(1)} %get-tuple-element.133.refs_5_.refs_8_), channel_id=1, source_target_pairs={{0,96},{32,0},{64,32},{96,64},{1,97},{33,1},{65,33},{97,65},{2,98}... | collective-permute-start | bytes 1572872 | tf_op jit(solution)/shard_map/ppermute | solution.py:20
  18.0 20.0 %collective-permute-start = (bf16[1024,256]{1,0:T(8,128)(2,1)S(1)}, bf16[1024,256]{1,0:T(8,128)(2,1)}, u32[]{:S(2)}, u32[]{:S(2)}) collective-permute-start(bf16[1024,256]{1,0:T(8,128)(2,1)S(1)} %get-tuple-element.138), channel_id=1, source_target_pairs={{0,16},{1,0},{16,17},{17,1},{2,18},{3,2},{18,19},{19,3},{4,20},{5,... | collective-permute-start | bytes 1572872 | tf_op jit(solution)/shard_map/ppermute | solution.py:405
  19.9 18.1 %collective-permute-start.1 = (bf16[1024,256]{1,0:T(8,128)(2,1)S(1)}, bf16[1024,256]{1,0:T(8,128)(2,1)}, u32[]{:S(2)}, u32[]{:S(2)}) collective-permute-start(bf16[1024,256]{1,0:T(8,128)(2,1)S(1)} %get-tuple-element.138), channel_id=1, source_target_pairs={{1,16},{16,1},{3,18},{18,3},{5,20},{20,5},{7,22},{22,7},{9,24},{24... | collective-permute-start | bytes 1572872 | tf_op jit(solution)/shard_map/ppermute | solution.py:406
  39.0 18.2 %collective-permute-start.9 = (bf16[768,512]{1,0:T(8,128)(2,1)}, bf16[768,512]{1,0:T(8,128)(2,1)S(1)}, u32[]{:S(2)}, u32[]{:S(2)}) collective-permute-start(bf16[768,512]{1,0:T(8,128)(2,1)} %pad_maximum_fusion.4), channel_id=1, source_target_pairs={{0,6},{2,0},{4,2},{6,4},{1,7},{3,1},{5,3},{7,5},{8,14},{10,8},{12,... | collective-permute-start | bytes 2359304 | tf_op jit(solution)/shard_map/ppermute | solution.py:20
  41.8 18.9 %collective-permute-start.10 = (bf16[768,512]{1,0:T(8,128)(2,1)}, bf16[768,512]{1,0:T(8,128)(2,1)}, u32[]{:S(2)}, u32[]{:S(2)}) collective-permute-start(bf16[768,512]{1,0:T(8,128)(2,1)} %pad_maximum_fusion.4), channel_id=1, source_target_pairs={{0,2},{2,4},{4,6},{6,0},{1,3},{3,5},{5,7},{7,1},{8,10},{10,12},{12... | collective-permute-start | bytes 2359304 | tf_op jit(solution)/shard_map/ppermute | solution.py:20
  41.8 22.3 %collective-permute-start.19 = (bf16[384,1024]{1,0:T(8,128)(2,1)S(1)}, bf16[384,1024]{1,0:T(8,128)(2,1)S(1)}, u32[]{:S(2)}, u32[]{:S(2)}) collective-permute-start(bf16[384,1024]{1,0:T(8,128)(2,1)S(1)} %copy-done.3), channel_id=1, source_target_pairs={{0,1},{1,0},{2,3},{3,2},{4,5},{5,4},{6,7},{7,6},{8,9},{9,8},{10,11... | collective-permute-start | bytes 2359304 | tf_op jit(solution)/shard_map/ppermute | solution.py:24
  43.2 28.5 %collective-permute-start.13 = (bf16[1024,256]{1,0:T(8,128)(2,1)S(1)}, bf16[1024,256]{1,0:T(8,128)(2,1)S(1)}, u32[]{:S(2)}, u32[]{:S(2)}) collective-permute-start(bf16[1024,256]{1,0:T(8,128)(2,1)S(1)} %get-tuple-element.133.refs_5_.refs_8_), channel_id=1, source_target_pairs={{0,16},{1,0},{16,17},{17,1},{2,18},{3,2},{18,19},{19,3},{4,20},{5,... | collective-permute-start | bytes 1572872 | tf_op jit(solution)/shard_map/ppermute | solution.py:405
  43.8 28.0 %collective-permute-start.14 = (bf16[1024,256]{1,0:T(8,128)(2,1)S(1)}, bf16[1024,256]{1,0:T(8,128)(2,1)S(1)}, u32[]{:S(2)}, u32[]{:S(2)}) collective-permute-start(bf16[1024,256]{1,0:T(8,128)(2,1)S(1)} %get-tuple-element.133.refs_5_.refs_8_), channel_id=1, source_target_pairs={{1,16},{16,1},{3,18},{18,3},{5,20},{20,5},{7,22},{22,7},{9,24},{24... | collective-permute-start | bytes 1572872 | tf_op jit(solution)/shard_map/ppermute | solution.py:406
  65.5 22.3 %collective-permute-start.20 = (bf16[2,384,1024]{2,1,0:T(8,128)(2,1)}, bf16[2,384,1024]{2,1,0:T(8,128)(2,1)}, u32[]{:S(2)}, u32[]{:S(2)}) collective-permute-start(bf16[2,384,1024]{2,1,0:T(8,128)(2,1)} %pad_maximum_fusion.1), channel_id=1, source_target_pairs={{0,8},{8,0},{1,9},{9,1},{2,10},{10,2},{3,11},{11,3},{4,12},{12,4},... | collective-permute-start | bytes 4718600 | tf_op jit(solution)/shard_map/ppermute | solution.py:24
  73.3 31.0 %collective-permute-start.15 = (bf16[2048,256]{1,0:T(8,128)(2,1)S(1)}, bf16[2048,256]{1,0:T(8,128)(2,1)S(1)}, u32[]{:S(2)}, u32[]{:S(2)}) collective-permute-start(bf16[2048,256]{1,0:T(8,128)(2,1)S(1)} %pad_maximum_fusion.3.refs_0_.refs_3_), channel_id=1, source_target_pairs={{0,96},{32,0},{64,32},{96,64},{1,97},{33,1},{65,33},{97,65},{2,98}... | collective-permute-start | bytes 3145736 | tf_op jit(solution)/shard_map/ppermute | solution.py:20
  76.2 28.1 %collective-permute-start.16 = (bf16[2048,256]{1,0:T(8,128)(2,1)S(1)}, bf16[2048,256]{1,0:T(8,128)(2,1)}, u32[]{:S(2)}, u32[]{:S(2)}) collective-permute-start(bf16[2048,256]{1,0:T(8,128)(2,1)S(1)} %pad_maximum_fusion.3.refs_0_.refs_3_), channel_id=1, source_target_pairs={{0,32},{32,64},{64,96},{96,0},{1,33},{33,65},{65,97},{97,1},{2,34}... | collective-permute-start | bytes 3145736 | tf_op jit(solution)/shard_map/ppermute | solution.py:20
  76.2 28.1 %collective-permute-start.17 = (bf16[2,1024,256]{2,1,0:T(8,128)(2,1)S(1)}, bf16[2,1024,256]{2,1,0:T(8,128)(2,1)}, u32[]{:S(2)}, u32[]{:S(2)}) collective-permute-start(bf16[2,1024,256]{2,1,0:T(8,128)(2,1)S(1)} %pad_maximum_fusion.2.refs_6_.refs_9_), channel_id=1, source_target_pairs={{0,16},{1,0},{16,17},{17,1},{2,18},{3,2},{18,19},{19,3},{4,20},{5,... | collective-permute-start | bytes 3145736 | tf_op jit(solution)/shard_map/ppermute | solution.py:405
  80.6 23.7 %collective-permute-start.18 = (bf16[2,1024,256]{2,1,0:T(8,128)(2,1)S(1)}, bf16[2,1024,256]{2,1,0:T(8,128)(2,1)}, u32[]{:S(2)}, u32[]{:S(2)}) collective-permute-start(bf16[2,1024,256]{2,1,0:T(8,128)(2,1)S(1)} %pad_maximum_fusion.2.refs_6_.refs_9_), channel_id=1, source_target_pairs={{1,16},{16,1},{3,18},{18,3},{5,20},{20,5},{7,22},{22,7},{9,24},{24... | collective-permute-start | bytes 3145736 | tf_op jit(solution)/shard_map/ppermute | solution.py:406
  104.3 23.4 %collective-permute-start.21 = (f32[64,128,128]{2,1,0:T(8,128)}, f32[64,128,128]{2,1,0:T(8,128)}, u32[]{:S(2)}, u32[]{:S(2)}) collective-permute-start(f32[64,128,128]{2,1,0:T(8,128)} %get-tuple-element.159), channel_id=1, source_target_pairs={{0,8},{8,0},{1,9},{9,1},{2,10},{10,2},{3,11},{11,3},{4,12},{12,4},... | collective-permute-start | bytes 12582920 | tf_op jit(solution)/shard_map/ppermute | solution.py:24
  138.2 21.8 %collective-permute-start.28 = (f32[384,1024]{1,0:T(8,128)}, f32[384,1024]{1,0:T(8,128)}, u32[]{:S(2)}, u32[]{:S(2)}) collective-permute-start(f32[384,1024]{1,0:T(8,128)} %get-tuple-element.185), channel_id=1, source_target_pairs={{0,8},{8,0},{1,9},{9,1},{2,10},{10,2},{3,11},{11,3},{4,12},{12,4},... | collective-permute-start | bytes 4718600 | tf_op jit(solution)/shard_map/ppermute | solution.py:24
  160.0 20.3 %collective-permute-start.29 = (f32[384,512]{1,0:T(8,128)}, f32[384,512]{1,0:T(8,128)}, u32[]{:S(2)}, u32[]{:S(2)}) collective-permute-start(f32[384,512]{1,0:T(8,128)} %get-tuple-element.187), channel_id=1, source_target_pairs={{0,2},{2,4},{4,6},{6,0},{1,3},{3,5},{5,7},{7,1},{8,10},{10,12},{12... | collective-permute-start | bytes 2359304 | tf_op jit(solution)/shard_map/ppermute | solution.py:20
  160.0 20.2 %collective-permute-start.30 = (f32[384,512]{1,0:T(8,128)}, f32[384,512]{1,0:T(8,128)}, u32[]{:S(2)}, u32[]{:S(2)}) collective-permute-start(f32[384,512]{1,0:T(8,128)} %get-tuple-element.188), channel_id=1, source_target_pairs={{0,6},{2,0},{4,2},{6,4},{1,7},{3,1},{5,3},{7,5},{8,14},{10,8},{12,... | collective-permute-start | bytes 2359304 | tf_op jit(solution)/shard_map/ppermute | solution.py:20
  162.8 26.2 %collective-permute-start.35 = (f32[16,128,128]{2,1,0:T(8,128)S(1)}, f32[16,128,128]{2,1,0:T(8,128)S(1)}, u32[]{:S(2)}, u32[]{:S(2)}) collective-permute-start(f32[16,128,128]{2,1,0:T(8,128)S(1)} %fusion.2), channel_id=1, source_target_pairs={{0,96},{32,0},{64,32},{96,64},{1,97},{33,1},{65,33},{97,65},{2,98}... | collective-permute-start | bytes 3145736 | tf_op jit(solution)/shard_map/ppermute | solution.py:20
  166.9 36.0 %collective-permute-start.36 = (f32[384,1024]{1,0:T(8,128)}, f32[384,1024]{1,0:T(8,128)}, u32[]{:S(2)}, u32[]{:S(2)}) collective-permute-start(f32[384,1024]{1,0:T(8,128)} %add.151), channel_id=1, source_target_pairs={{0,1},{1,0},{2,3},{3,2},{4,5},{5,4},{6,7},{7,6},{8,9},{9,8},{10,11... | collective-permute-start | bytes 4718600 | tf_op jit(solution)/shard_map/ppermute | solution.py:24
  170.1 24.0 %collective-permute-start.34 = (f32[16,128,128]{2,1,0:T(8,128)S(1)}, f32[16,128,128]{2,1,0:T(8,128)}, u32[]{:S(2)}, u32[]{:S(2)}) collective-permute-start(f32[16,128,128]{2,1,0:T(8,128)S(1)} %fusion.3), channel_id=1, source_target_pairs={{0,32},{32,64},{64,96},{96,0},{1,33},{33,65},{65,97},{97,1},{2,34}... | collective-permute-start | bytes 3145736 | tf_op jit(solution)/shard_map/ppermute | solution.py:20
  180.3 35.7 %collective-permute-start.38 = (f32[384,1024]{1,0:T(8,128)}, f32[384,1024]{1,0:T(8,128)}, u32[]{:S(2)}, u32[]{:S(2)}) collective-permute-start(f32[384,1024]{1,0:T(8,128)} %get-tuple-element.203), channel_id=1, source_target_pairs={{0,8},{8,0},{1,9},{9,1},{2,10},{10,2},{3,11},{11,3},{4,12},{12,4},... | collective-permute-start | bytes 4718600 | tf_op jit(solution)/shard_map/ppermute | solution.py:24
  184.8 36.3 %collective-permute-start.32 = (f32[768,512]{1,0:T(8,128)}, f32[768,512]{1,0:T(8,128)}, u32[]{:S(2)}, u32[]{:S(2)}) collective-permute-start(f32[768,512]{1,0:T(8,128)} %add_dynamic-update-slice_fusion), channel_id=1, source_target_pairs={{0,6},{2,0},{4,2},{6,4},{1,7},{3,1},{5,3},{7,5},{8,14},{10,8},{12,... | collective-permute-start | bytes 4718600 | tf_op jit(solution)/shard_map/ppermute | solution.py:20
  189.0 37.2 %collective-permute-start.31 = (f32[768,512]{1,0:T(8,128)}, f32[768,512]{1,0:T(8,128)}, u32[]{:S(2)}, u32[]{:S(2)}) collective-permute-start(f32[768,512]{1,0:T(8,128)} %add_dynamic-update-slice_fusion.1), channel_id=1, source_target_pairs={{0,2},{2,4},{4,6},{6,0},{1,3},{3,5},{5,7},{7,1},{8,10},{10,12},{12... | collective-permute-start | bytes 4718600 | tf_op jit(solution)/shard_map/ppermute | solution.py:20
  (40 other events, 414.7 us)
Sparse Core Ops, SparseCore 0:
  39.1 37.9 all-gather.1
